TPU v7x, 32 devices: a whole 2x2x4 slice. The times are simulated.
32 devices in a mesh: tm: 4 (over x, core), batch: 8 (over z, y).
Axes of the slice: x: 2, y: 2, z: 4, core: 2. Of those that a mesh axis runs over, the one named last changes fastest.
Arguments:
- video: bfloat16 [64, 16, 7, 7, 192], P('batch', 'tm'), may hold values from -12 to 12
- video_ids: int32 [64], P('batch'), may hold values from 0 to 63, as said below
- crop_scales: int32 [64], P('batch'), may hold values from 0 to 3
- labels: int32 [64], P('batch'), may hold values from 0 to 399
- valid_clips: int32 [64], P('batch'), may hold values from 0 to 1, as said below
- stem_weight: float32 [2304, 192], P('batch'), may hold values from -0.4375 to 0.4375
- lateral_weight: float32 [512, 1280], P('batch'), may hold values from -0.15625 to 0.15625
- condense: float32 [512, 6144], P('batch'), may hold values from -0.078125 to 0.078125
- mixing: float32 [512, 4608], P('batch'), may hold values from -0.09375 to 0.09375
- restore: float32 [2048, 512], P('batch'), may hold values from -0.25 to 0.25
- squeeze: float32 [64, 768], P('batch'), may hold values from -0.21875 to 0.21875
- blending: float32 [64, 576], P('batch'), may hold values from -0.25 to 0.25
- recover: float32 [256, 64], P('batch'), may hold values from -0.75 to 0.75
- head_weight: float32 [2304, 400], P('batch'), may hold values from -0.125 to 0.125
- stem_velocity: float32 [2304, 192], P('batch'), may hold values from -1.9073486e-05 to 1.9073486e-05
- lateral_velocity: float32 [512, 1280], P('batch'), may hold values from -1.9073486e-05 to 1.9073486e-05
- condense_velocity: float32 [512, 6144], P('batch'), may hold values from -1.9073486e-05 to 1.9073486e-05
- mixing_velocity: float32 [512, 4608], P('batch'), may hold values from -1.9073486e-05 to 1.9073486e-05
- restore_velocity: float32 [2048, 512], P('batch'), may hold values from -1.9073486e-05 to 1.9073486e-05
- squeeze_velocity: float32 [64, 768], P('batch'), may hold values from -1.9073486e-05 to 1.9073486e-05
- blending_velocity: float32 [64, 576], P('batch'), may hold values from -1.9073486e-05 to 1.9073486e-05
- recover_velocity: float32 [256, 64], P('batch'), may hold values from -1.9073486e-05 to 1.9073486e-05
- head_moment: float32 [2304, 400], P('batch'), may hold values from -2.3841858e-06 to 2.3841858e-06
- head_square: float32 [2304, 400], P('batch'), may hold values from 1.1517234e-14 to 4.6068936e-14
- affine: float32 [7312], replicated, may hold values from -1 to 7, as said below
- affine_moment: float32 [7312], replicated, may hold values from -1.1444092e-05 to 1.1444092e-05
- affine_square: float32 [7312], replicated, may hold values from 2.8793087e-13 to 1.1517235e-12
Outputs:
- stem_carried: float32 [2304, 192], P('batch')
- lateral_carried: float32 [512, 1280], P('batch')
- condense_carried: float32 [512, 6144], P('batch')
- mixing_carried: float32 [512, 4608], P('batch')
- restore_carried: float32 [2048, 512], P('batch')
- squeeze_carried: float32 [64, 768], P('batch')
- blending_carried: float32 [64, 576], P('batch')
- recover_carried: float32 [256, 64], P('batch')
- stem_updated: float32 [2304, 192], P('batch')
- lateral_updated: float32 [512, 1280], P('batch')
- condense_updated: float32 [512, 6144], P('batch')
- mixing_updated: float32 [512, 4608], P('batch')
- restore_updated: float32 [2048, 512], P('batch')
- squeeze_updated: float32 [64, 768], P('batch')
- blending_updated: float32 [64, 576], P('batch')
- recover_updated: float32 [256, 64], P('batch')
- head_updated: float32 [2304, 400], P('batch')
- moment_head: float32 [2304, 400], P('batch')
- square_head: float32 [2304, 400], P('batch')
- affine_updated: float32 [7312], replicated
- moment_affine: float32 [7312], replicated
- square_affine: float32 [7312], replicated
- loss_total: float32 [], replicated
- clip_count: float32 [], replicated
- grad_norm: float32 [], replicated
Inputs may be any that keep to these rules, and one draw needn't show every extreme that they name: `video_ids`: never falling; clips that share an id lie in one aligned block of 8 clips; the last clip of every block has id (block index + 1) * 8 - 1. `valid_clips`: zero or one. `affine`: gains are positive.
All inputs are finite; a program needn't handle non-finite values.
Results may differ from a plain program's by a relative error of at most 0.005.
Values may be sent and summed in bfloat16 or wider, within the bound.
No kernel may reach another device: no remote copies, remote signals or barrier semaphores. Data moves between devices by JAX's collectives and lax.ppermute only.
A program may use at most 256 MiB of HBM per device.

v0:
```python
import math

import jax
import jax.numpy as jnp
from jax import lax
from jax.sharding import PartitionSpec as P

CS = 2048
CSM = 512
CF = 256
CFM = 64
CLS = 400
ALPHA = 4
NS_STEPS = 3
STEP = 10


HIGHEST = lax.Precision.HIGHEST
NORM_EPS = 1e-05
CLIP_AT = 0.01
MUON_RATE = 0.5
MUON_KEEP = 0.95
WEIGHT_DECAY = 0.01
ADAM_ONE = 0.9
ADAM_TWO = 0.999
ADAM_EPS = 1e-08
HEAD_RATE = 0.02
AFFINE_RATE = 0.1
NS_FIRST = 3.4445
NS_SECOND = -4.775
NS_THIRD = 2.0315


def padded_2(cells, sides, width):
    for axis, dim in sides:
        count = lax.axis_size(axis)
        ends = count - 1
        head = lax.slice_in_dim(cells, 0, width, axis=dim)
        tail = lax.slice_in_dim(cells, cells.shape[dim] - width, cells.shape[dim], axis=dim)
        cells = jnp.concatenate(
            [
                lax.ppermute(tail, axis, [(i, (i + 1) % count) for i in range(ends)]),
                cells,
                lax.ppermute(head, axis, [((i + 1) % count, i) for i in range(ends)]),
            ],
            axis=dim,
        )
    return cells


def from_behind(block, axis, distance):
    devices = range(lax.axis_size(axis))
    route = [(i - distance, i) for i in devices if i - distance in devices]
    return lax.ppermute(block, axis, route)


def split_affine(vector):
    widths = (CSM, CSM, CS, CFM, CFM, CF)
    gains = []
    shifts = []
    start = 0
    for width in widths:
        gains.append(vector[start : start + width])
        start = start + width
    for width in widths:
        shifts.append(vector[start : start + width])
        start = start + width
    return (gains, shifts, vector[start : start + CLS])


def silu_grad(values):
    sigma = jax.nn.sigmoid(values)
    return sigma * (1.0 + values * (1.0 - sigma))


def apply_weight(inputs, weight):
    return lax.dot_general(
        inputs, weight, (((inputs.ndim - 1,), (1,)), ((), ())), preferred_element_type=jnp.float32
    )


def apply_back(upstream, weight):
    return lax.dot_general(
        upstream,
        weight,
        (((upstream.ndim - 1,), (0,)), ((), ())),
        preferred_element_type=jnp.float32,
    )


def outer_total(upstream, inputs):
    leading = tuple(range(upstream.ndim - 1))
    return lax.dot_general(
        upstream, inputs, ((leading, leading), ((), ())), preferred_element_type=jnp.float32
    )


def frame_rims(values):
    return padded_2(values, (("tm", 1),), 1)


def grad_rims(values):
    return padded_2(values, (("tm", 1),), 1)


def pad_space(values):
    return jnp.pad(values, ((0, 0), (0, 0), (1, 1), (1, 1), (0, 0)))


def temporal_forward(padded, weight):
    width = padded.shape[-1]
    frames = padded.shape[1] - 2
    total = apply_weight(padded[:, 0:frames], weight[:, 0:width])
    for offset in range(1, 3):
        total = total + apply_weight(
            padded[:, offset : offset + frames], weight[:, offset * width : (offset + 1) * width]
        )
    return total


def temporal_backward(padded, upstream, weight):
    width = padded.shape[-1]
    frames = padded.shape[1] - 2
    weight_grad = jnp.concatenate(
        [outer_total(upstream, padded[:, offset : offset + frames]) for offset in range(3)], axis=1
    )
    rimmed = grad_rims(upstream)
    input_grad = apply_back(rimmed[:, 2 : 2 + frames], weight[:, 0:width])
    for offset in range(1, 3):
        input_grad = input_grad + apply_back(
            rimmed[:, 2 - offset : 2 - offset + frames],
            weight[:, offset * width : (offset + 1) * width],
        )
    return (weight_grad, input_grad)


def spatial_forward(values, weight):
    width = values.shape[-1]
    height = values.shape[2]
    padded = pad_space(values)
    total = None
    for tap in range(9):
        down, across = (tap // 3, tap % 3)
        term = apply_weight(
            padded[:, :, down : down + height, across : across + height],
            weight[:, tap * width : (tap + 1) * width],
        )
        total = term if total is None else total + term
    return total


def spatial_backward(values, upstream, weight):
    width = values.shape[-1]
    height = values.shape[2]
    padded = pad_space(values)
    upper = pad_space(upstream)
    pieces = []
    input_grad = None
    for tap in range(9):
        down, across = (tap // 3, tap % 3)
        pieces.append(
            outer_total(upstream, padded[:, :, down : down + height, across : across + height])
        )
        term = apply_back(
            upper[:, :, 2 - down : 2 - down + height, 2 - across : 2 - across + height],
            weight[:, tap * width : (tap + 1) * width],
        )
        input_grad = term if input_grad is None else input_grad + term
    return (jnp.concatenate(pieces, axis=1), input_grad)


def lateral_forward(extended, weight, slow_frames):
    width = extended.shape[-1]
    total = None
    for offset in range(5):
        picked = extended[:, offset : offset + ALPHA * slow_frames : ALPHA]
        term = apply_weight(picked, weight[:, offset * width : (offset + 1) * width])
        total = term if total is None else total + term
    return total


def lateral_backward(extended, upstream, weight):
    width = extended.shape[-1]
    slow_frames = upstream.shape[1]
    frames = extended.shape[1] - 2
    pieces = []
    input_grad = jnp.zeros(extended.shape, jnp.float32)
    for offset in range(5):
        picked = extended[:, offset : offset + ALPHA * slow_frames : ALPHA]
        pieces.append(outer_total(upstream, picked))
        input_grad = input_grad.at[:, offset : offset + ALPHA * slow_frames : ALPHA].add(
            apply_back(upstream, weight[:, offset * width : (offset + 1) * width])
        )
    returned = from_behind(input_grad[:, 0:2], "tm", -1)
    own_grad = input_grad[:, 2:].at[:, frames - 2 :].add(returned)
    return (jnp.concatenate(pieces, axis=1), own_grad)


def norm_stats(values, mask, count_term):
    total, squares, count = lax.psum(
        (
            jnp.sum(mask * values, axis=(0, 1, 2, 3)),
            jnp.sum(mask * values * values, axis=(0, 1, 2, 3)),
            count_term,
        ),
        ("tm", "batch"),
    )
    mean = total / count
    spread = squares / count - mean * mean
    inverse = lax.rsqrt(spread + NORM_EPS)
    return ((values - mean) * inverse, inverse, count)


def norm_back(upstream, scaled, inverse, count, gain, mask, extra):
    shift_sum, scale_sum, carried = lax.psum(
        (
            jnp.sum(mask * upstream, axis=(0, 1, 2, 3)),
            jnp.sum(mask * upstream * scaled, axis=(0, 1, 2, 3)),
            extra,
        ),
        ("tm", "batch"),
    )
    below = mask * gain * inverse * (upstream - (shift_sum + scaled * scale_sum) / count)
    return (below, scale_sum, shift_sum, carried)


def block_forward(
    source,
    padded,
    added,
    reduce_weight,
    middle_weight,
    expand_weight,
    gains,
    shifts,
    mask,
    count_term,
):
    first = temporal_forward(padded, reduce_weight) + added
    scaled_one, inverse_one, count = norm_stats(first, mask, count_term)
    level_one = gains[0] * scaled_one + shifts[0]
    act_one = (jax.nn.silu(level_one) * mask).astype(jnp.bfloat16)
    second = spatial_forward(act_one, middle_weight)
    scaled_two, inverse_two, count = norm_stats(second, mask, count_term)
    level_two = gains[1] * scaled_two + shifts[1]
    act_two = (jax.nn.silu(level_two) * mask).astype(jnp.bfloat16)
    third = apply_weight(act_two, expand_weight)
    scaled_three, inverse_three, count = norm_stats(third, mask, count_term)
    residual = source + gains[2] * scaled_three + shifts[2]
    output = jax.nn.silu(residual) * mask
    saved = (
        scaled_one,
        inverse_one,
        level_one,
        act_one,
        scaled_two,
        inverse_two,
        level_two,
        act_two,
        scaled_three,
        inverse_three,
        residual,
        count,
    )
    return (output, saved)


def block_backward(
    out_grad, saved, padded, reduce_weight, middle_weight, expand_weight, gains, mask, extra
):
    (
        scaled_one,
        inverse_one,
        level_one,
        act_one,
        scaled_two,
        inverse_two,
        level_two,
        act_two,
        scaled_three,
        inverse_three,
        residual,
        count,
    ) = saved
    nothing = jnp.zeros((), jnp.float32)
    residual_grad = out_grad * mask * silu_grad(residual)
    upper_three, gain_three, shift_three, carried = norm_back(
        residual_grad, scaled_three, inverse_three, count, gains[2], mask, extra
    )
    upper_three = upper_three.astype(jnp.bfloat16)
    expand_grad = outer_total(upper_three, act_two)
    level_two_grad = apply_back(upper_three, expand_weight) * mask * silu_grad(level_two)
    upper_two, gain_two, shift_two, unused = norm_back(
        level_two_grad, scaled_two, inverse_two, count, gains[1], mask, nothing
    )
    upper_two = upper_two.astype(jnp.bfloat16)
    middle_grad, act_one_grad = spatial_backward(act_one, upper_two, middle_weight)
    level_one_grad = act_one_grad * mask * silu_grad(level_one)
    upper_one, gain_one, shift_one, unused = norm_back(
        level_one_grad, scaled_one, inverse_one, count, gains[0], mask, nothing
    )
    upper_one = upper_one.astype(jnp.bfloat16)
    reduce_grad, source_grad = temporal_backward(padded, upper_one, reduce_weight)
    source_grad = source_grad + residual_grad
    return (
        source_grad,
        upper_one,
        (reduce_grad, middle_grad, expand_grad),
        (gain_one, gain_two, gain_three),
        (shift_one, shift_two, shift_three),
        carried,
    )


def orthogonalize(matrix):
    rows, columns = matrix.shape
    wide = matrix.T if rows > columns else matrix
    wide = wide / (jnp.sqrt(jnp.sum(wide * wide)) + 1e-07)
    for step in range(NS_STEPS):
        gram = jnp.dot(wide, wide.T, precision=HIGHEST)
        poly = NS_SECOND * gram + NS_THIRD * jnp.dot(gram, gram, precision=HIGHEST)
        wide = NS_FIRST * wide + jnp.dot(poly, wide, precision=HIGHEST)
    result = wide.T if rows > columns else wide
    return lax.optimization_barrier(result.astype(jnp.bfloat16))


def owner_result(whole, owner, batch_place):
    return lax.cond(
        batch_place == owner,
        lambda: orthogonalize(whole.astype(jnp.float32)),
        lambda: jnp.zeros(whole.shape, jnp.bfloat16),
    )


def adam(weight, moment, square, grad, rate, decay):
    moment = ADAM_ONE * moment + (1.0 - ADAM_ONE) * grad
    square = ADAM_TWO * square + (1.0 - ADAM_TWO) * grad * grad
    fixed_one = 1.0 - ADAM_ONE**STEP
    fixed_two = 1.0 - ADAM_TWO**STEP
    weight = weight - rate * (
        moment / fixed_one / (jnp.sqrt(square / fixed_two) + ADAM_EPS) + decay * weight
    )
    return (weight, moment, square)


def per_device(
    video,
    video_ids,
    crop_scales,
    labels,
    valid_clips,
    stem_weight,
    lateral_weight,
    condense,
    mixing,
    restore,
    squeeze,
    blending,
    recover,
    head_weight,
    stem_velocity,
    lateral_velocity,
    condense_velocity,
    mixing_velocity,
    restore_velocity,
    squeeze_velocity,
    blending_velocity,
    recover_velocity,
    head_moment,
    head_square,
    affine,
    affine_moment,
    affine_square,
):
    shards = (
        stem_weight,
        lateral_weight,
        condense,
        mixing,
        restore,
        squeeze,
        blending,
        recover,
        head_weight,
    )
    velocities = (
        stem_velocity,
        lateral_velocity,
        condense_velocity,
        mixing_velocity,
        restore_velocity,
        squeeze_velocity,
        blending_velocity,
        recover_velocity,
    )
    (
        stem_full,
        lateral_full,
        condense_full,
        mixing_full,
        restore_full,
        squeeze_full,
        blending_full,
        recover_full,
        head_full,
    ) = (
        lax.all_gather(stem_weight.astype(jnp.bfloat16), "batch", axis=0, tiled=True),
        lax.all_gather(lateral_weight.astype(jnp.bfloat16), "batch", axis=0, tiled=True),
        lax.all_gather(condense.astype(jnp.bfloat16), "batch", axis=0, tiled=True),
        lax.all_gather(mixing.astype(jnp.bfloat16), "batch", axis=0, tiled=True),
        lax.all_gather(restore.astype(jnp.bfloat16), "batch", axis=0, tiled=True),
        lax.all_gather(squeeze.astype(jnp.bfloat16), "batch", axis=0, tiled=True),
        lax.all_gather(blending.astype(jnp.bfloat16), "batch", axis=0, tiled=True),
        lax.all_gather(recover.astype(jnp.bfloat16), "batch", axis=0, tiled=True),
        lax.all_gather(head_weight.astype(jnp.bfloat16), "batch", axis=0, tiled=True),
    )
    tm_count = lax.axis_size("tm")
    batch_count = lax.axis_size("batch")
    tm_place = lax.axis_index("tm")
    batch_place = lax.axis_index("batch")
    fast_frames = video.shape[1]
    slow_frames = fast_frames // ALPHA
    height = video.shape[2]
    side = (height - crop_scales).astype(jnp.float32)
    places = jnp.arange(height).astype(jnp.float32)
    inside = (places[None, :] < side[:, None]).astype(jnp.float32)
    mask = (inside[:, :, None] * inside[:, None, :])[:, None, :, :, None]
    area = side * side
    local_area = jnp.sum(area)
    gains, shifts, class_bias = split_affine(affine)
    slow_video = video[:, ::ALPHA]
    slow_pre = apply_weight(slow_video, stem_full[0:CS])
    fast_pre = apply_weight(video, stem_full[CS:])
    slow_x = jax.nn.silu(slow_pre) * mask
    fast_x = jax.nn.silu(fast_pre) * mask
    slow_low = slow_x.astype(jnp.bfloat16)
    fast_low = fast_x.astype(jnp.bfloat16)
    slow_padded = frame_rims(slow_low)
    fast_padded = frame_rims(fast_low)
    tail = from_behind(fast_low[:, fast_frames - 2 :], "tm", 1)
    extended = jnp.concatenate([tail, fast_low], axis=1)
    added = lateral_forward(extended, lateral_full, slow_frames)
    slow_out, slow_saved = block_forward(
        slow_x,
        slow_padded,
        added,
        condense_full,
        mixing_full,
        restore_full,
        gains[0:3],
        shifts[0:3],
        mask,
        local_area * slow_frames,
    )
    fast_out, fast_saved = block_forward(
        fast_x,
        fast_padded,
        jnp.zeros((), jnp.float32),
        squeeze_full,
        blending_full,
        recover_full,
        gains[3:6],
        shifts[3:6],
        mask,
        local_area * fast_frames,
    )
    slow_pool, fast_pool = lax.psum(
        (jnp.sum(slow_out, axis=(1, 2, 3)), jnp.sum(fast_out, axis=(1, 2, 3))), "tm"
    )
    slow_divide = slow_frames * tm_count * area
    fast_divide = fast_frames * tm_count * area
    features = jnp.concatenate(
        [slow_pool / slow_divide[:, None], fast_pool / fast_divide[:, None]], axis=1
    )
    feature_low = features.astype(jnp.bfloat16)
    logits = jnp.dot(feature_low, head_full, preferred_element_type=jnp.float32) + class_bias
    same = (video_ids[:, None] == video_ids[None, :]).astype(jnp.float32)
    average = same / jnp.sum(same, axis=1, keepdims=True)
    mean_logits = jnp.dot(average, logits, precision=HIGHEST)
    onehot = (labels[:, None] == jnp.arange(CLS)[None, :]).astype(jnp.float32)
    valid = valid_clips.astype(jnp.float32)
    log_norm = jax.nn.logsumexp(mean_logits, axis=1)
    picked = jnp.sum(onehot * mean_logits, axis=1)
    loss_local = jnp.sum(valid * (log_norm - picked))
    count_local = jnp.sum(valid)
    mean_grad = valid[:, None] * (jax.nn.softmax(mean_logits, axis=1) - onehot)
    logit_low = jnp.dot(average.T, mean_grad, precision=HIGHEST).astype(jnp.bfloat16)
    leader = (tm_place == 0).astype(jnp.float32)
    head_grad = outer_total(feature_low, logit_low) * leader
    bias_grad = jnp.sum(logit_low.astype(jnp.float32), axis=0) * leader
    feature_grad = apply_weight(logit_low, head_full)
    slow_grad_pool = feature_grad[:, 0:CS] / slow_divide[:, None]
    fast_grad_pool = feature_grad[:, CS:] / fast_divide[:, None]
    slow_out_grad = jnp.broadcast_to(slow_grad_pool[:, None, None, None, :], slow_out.shape)
    fast_out_grad = jnp.broadcast_to(fast_grad_pool[:, None, None, None, :], fast_out.shape)
    slow_source, slow_upper, slow_grads, slow_gains, slow_shifts, class_grad = block_backward(
        slow_out_grad,
        slow_saved,
        slow_padded,
        condense_full,
        mixing_full,
        restore_full,
        gains[0:3],
        mask,
        bias_grad,
    )
    lateral_grad, fast_side = lateral_backward(extended, slow_upper, lateral_full)
    fast_source, fast_upper, fast_grads, fast_gains, fast_shifts, unused = block_backward(
        fast_out_grad,
        fast_saved,
        fast_padded,
        squeeze_full,
        blending_full,
        recover_full,
        gains[3:6],
        mask,
        jnp.zeros((), jnp.float32),
    )
    fast_source = fast_source + fast_side
    slow_stem_up = (slow_source * mask * silu_grad(slow_pre)).astype(jnp.bfloat16)
    fast_stem_up = (fast_source * mask * silu_grad(fast_pre)).astype(jnp.bfloat16)
    stem_grad = jnp.concatenate(
        [outer_total(slow_stem_up, slow_video), outer_total(fast_stem_up, video)], axis=0
    )
    summed = (
        lax.psum_scatter(stem_grad, "batch", scatter_dimension=0, tiled=True),
        lax.psum_scatter(lateral_grad, "batch", scatter_dimension=0, tiled=True),
        lax.psum_scatter(slow_grads[0], "batch", scatter_dimension=0, tiled=True),
        lax.psum_scatter(slow_grads[1], "batch", scatter_dimension=0, tiled=True),
        lax.psum_scatter(slow_grads[2], "batch", scatter_dimension=0, tiled=True),
        lax.psum_scatter(fast_grads[0], "batch", scatter_dimension=0, tiled=True),
        lax.psum_scatter(fast_grads[1], "batch", scatter_dimension=0, tiled=True),
        lax.psum_scatter(fast_grads[2], "batch", scatter_dimension=0, tiled=True),
        lax.psum_scatter(head_grad, "batch", scatter_dimension=0, tiled=True),
    )
    reduced = lax.psum(
        (
            summed[0],
            summed[1],
            summed[2],
            summed[3],
            summed[4],
            summed[5],
            summed[6],
            summed[7],
            summed[8],
        ),
        "tm",
    )
    affine_grad = jnp.concatenate(
        list(slow_gains) + list(fast_gains) + list(slow_shifts) + list(fast_shifts) + [class_grad]
    )
    squares = jnp.where(batch_place == 0, jnp.sum(affine_grad * affine_grad), 0.0)
    for item in reduced:
        squares = squares + jnp.sum(item * item)
    total_squares, loss_total, clip_count = lax.psum((squares, loss_local, count_local), "batch")
    grad_norm = jnp.sqrt(total_squares) / clip_count
    factor = jnp.minimum(1.0, CLIP_AT / grad_norm)
    scaled = [item / clip_count * factor for item in reduced]
    affine_scaled = affine_grad / clip_count * factor
    carried = [MUON_KEEP * velocity + grad for velocity, grad in zip(velocities, scaled[0:8])]
    carried_low = [item.astype(jnp.bfloat16) for item in carried]
    gathered = (
        lax.all_gather(carried_low[0], "batch", axis=0, tiled=True),
        lax.all_gather(carried_low[1], "batch", axis=0, tiled=True),
        lax.all_gather(carried_low[2], "batch", axis=0, tiled=True),
        lax.all_gather(carried_low[3], "batch", axis=0, tiled=True),
        lax.all_gather(carried_low[4], "batch", axis=0, tiled=True),
        lax.all_gather(carried_low[5], "batch", axis=0, tiled=True),
        lax.all_gather(carried_low[6], "batch", axis=0, tiled=True),
        lax.all_gather(carried_low[7], "batch", axis=0, tiled=True),
    )
    orthos = [owner_result(gathered[place], place % batch_count, batch_place) for place in range(8)]
    returned = (
        lax.psum_scatter(orthos[0], "batch", scatter_dimension=0, tiled=True).astype(jnp.float32),
        lax.psum_scatter(orthos[1], "batch", scatter_dimension=0, tiled=True).astype(jnp.float32),
        lax.psum_scatter(orthos[2], "batch", scatter_dimension=0, tiled=True).astype(jnp.float32),
        lax.psum_scatter(orthos[3], "batch", scatter_dimension=0, tiled=True).astype(jnp.float32),
        lax.psum_scatter(orthos[4], "batch", scatter_dimension=0, tiled=True).astype(jnp.float32),
        lax.psum_scatter(orthos[5], "batch", scatter_dimension=0, tiled=True).astype(jnp.float32),
        lax.psum_scatter(orthos[6], "batch", scatter_dimension=0, tiled=True).astype(jnp.float32),
        lax.psum_scatter(orthos[7], "batch", scatter_dimension=0, tiled=True).astype(jnp.float32),
    )
    returned = [item for item in returned]
    updated = []
    for place in range(8):
        weight = shards[place]
        rows = weight.shape[0] * batch_count
        columns = weight.shape[1]
        updated.append(
            weight
            - MUON_RATE
            * (returned[place] * math.sqrt(max(1.0, rows / columns)) + WEIGHT_DECAY * weight)
        )
    head_new, head_first, head_second = adam(
        head_weight, head_moment, head_square, scaled[8], HEAD_RATE, WEIGHT_DECAY
    )
    affine_new, affine_first, affine_second = adam(
        affine, affine_moment, affine_square, affine_scaled, AFFINE_RATE, 0.0
    )
    return (
        carried[0],
        carried[1],
        carried[2],
        carried[3],
        carried[4],
        carried[5],
        carried[6],
        carried[7],
        updated[0],
        updated[1],
        updated[2],
        updated[3],
        updated[4],
        updated[5],
        updated[6],
        updated[7],
        head_new,
        head_first,
        head_second,
        affine_new,
        affine_first,
        affine_second,
        loss_total,
        clip_count,
        grad_norm,
    )


def solution(mesh):
    in_specs = (
        P("batch", "tm", None, None, None),
        P("batch"),
        P("batch"),
        P("batch"),
        P("batch"),
        P("batch", None),
        P("batch", None),
        P("batch", None),
        P("batch", None),
        P("batch", None),
        P("batch", None),
        P("batch", None),
        P("batch", None),
        P("batch", None),
        P("batch", None),
        P("batch", None),
        P("batch", None),
        P("batch", None),
        P("batch", None),
        P("batch", None),
        P("batch", None),
        P("batch", None),
        P("batch", None),
        P("batch", None),
        P(),
        P(),
        P(),
    )
    out_specs = (
        P("batch", None),
        P("batch", None),
        P("batch", None),
        P("batch", None),
        P("batch", None),
        P("batch", None),
        P("batch", None),
        P("batch", None),
        P("batch", None),
        P("batch", None),
        P("batch", None),
        P("batch", None),
        P("batch", None),
        P("batch", None),
        P("batch", None),
        P("batch", None),
        P("batch", None),
        P("batch", None),
        P("batch", None),
        P(),
        P(),
        P(),
        P(),
        P(),
        P(),
    )
    return jax.shard_map(
        per_device, mesh=mesh, in_specs=in_specs, out_specs=out_specs, check_vma=False
    )
```

profile of v0, /device:TPU:0, one launch (start us, length us, event | category | flops | bytes accessed | tf_op | source)
XLA Modules:
  0.0 2634.6 jit_solution(8629356641841012413)
XLA Ops:
  13.9 37.6 %all_gather.75 = bf16[2304,192]{1,0:T(8,128)(2,1)S(1)} all-gather(bf16[288,192]{1,0:T(8,128)(2,1)S(1)} %convert_element_type.255), channel_id=1, replica_groups=mesh['tm'=4,'batch'=8] {'batch'}, dimensions={0}, use_global_device_ids=true | all-gather | bytes 995328 | tf_op jit(solution)/shard_map/all_gather | solution.py:407
  55.8 4.2 collective-permute-start
  63.2 3.7 collective-permute-start.3
  72.1 31.0 %all_gather.82 = bf16[256,64]{1,0:T(8,128)(2,1)S(1)} all-gather(bf16[32,64]{1,0:T(8,128)(2,1)S(1)} %convert_element_type.272), channel_id=1, replica_groups=mesh['tm'=4,'batch'=8] {'batch'}, dimensions={0}, use_global_device_ids=true | all-gather | bytes 36864 | tf_op jit(solution)/shard_map/all_gather | solution.py:414
  103.1 31.6 %all_gather.80 = bf16[64,768]{1,0:T(8,128)(2,1)S(1)} all-gather(bf16[8,768]{1,0:T(8,128)(2,1)S(1)} %convert_element_type.268), channel_id=1, replica_groups=mesh['tm'=4,'batch'=8] {'batch'}, dimensions={0}, use_global_device_ids=true | all-gather | bytes 110592 | tf_op jit(solution)/shard_map/all_gather | solution.py:412
  135.9 30.9 %all_gather.81 = bf16[64,576]{1,0:T(8,128)(2,1)S(1)} all-gather(bf16[8,576]{1,0:T(8,128)(2,1)S(1)} %convert_element_type.270), channel_id=1, replica_groups=mesh['tm'=4,'batch'=8] {'batch'}, dimensions={0}, use_global_device_ids=true | all-gather | bytes 82944 | tf_op jit(solution)/shard_map/all_gather | solution.py:413
  179.9 4.1 fusion.161
  184.0 40.4 %all-reduce.12 = (f32[64]{0:T(128)S(1)}, f32[]{:T(128)}, f32[64]{0:T(128)S(1)}, f32[512]{0:T(512)S(1)}, f32[]{:T(128)}, /*index=5*/f32[512]{0:T(512)S(1)}) all-reduce(f32[64]{0:T(128)S(1)} %get-tuple-element.227, f32[]{:T(128)S(6)} %mul.1446, f32[64]{0:T(128)S(1)} %get-tuple-element.226, ...), channel_id=1, replica_groups=mesh['tm'=4,'batch'=8] {'tm','batch'}, use_global_device_ids=true, to_apply=%region_18.19 | all-reduce | flops 1154 | bytes 9232 | tf_op jit(solution)/shard_map/psum | solution.py:200
  229.5 16.7 all-gather.14.cloned.1.call-done
  255.1 39.1 %all-reduce.11 = (f32[64]{0:T(128)S(1)}, f32[64]{0:T(128)S(1)}, f32[512]{0:T(512)S(1)}, f32[512]{0:T(512)S(1)}) all-reduce(f32[64]{0:T(128)S(1)} %get-tuple-element.225, f32[64]{0:T(128)S(1)} %get-tuple-element.224, f32[512]{0:T(512)S(1)} %get-tuple-element.221, ...), channel_id=1, replica_groups=mesh['tm'=4,'batch'=8] {'tm','batch'}, use_global_device_ids=true, to_apply=%region_23.24 | all-reduce | flops 1152 | bytes 9216 | tf_op jit(solution)/shard_map/psum | solution.py:200
  297.5 4.7 multiply_reduce_fusion
  302.3 40.9 %all-reduce.10 = (f32[256]{0:T(256)}, f32[256]{0:T(256)}, f32[2048]{0:T(1024)S(1)}, f32[2048]{0:T(1024)S(1)}) all-reduce(f32[256]{0:T(256)S(1)} %get-tuple-element.211, f32[256]{0:T(256)S(1)} %get-tuple-element.210, f32[2048]{0:T(1024)S(1)} %get-tuple-element.207, ...), channel_id=1, replica_groups=mesh['tm'=4,'batch'=8] {'tm','batch'}, use_global_device_ids=true, to_apply=%region_27.28 | all-reduce | flops 4608 | bytes 36864 | tf_op jit(solution)/shard_map/psum | solution.py:200
  343.9 4.6 multiply_reduce_fusion.2
  355.4 6.8 psum.314
  364.6 15.0 all-reduce.21.cloned.1.call-done
  380.6 54.0 %all-gather.18.cloned.1.call-done = bf16[2304,400]{1,0:T(8,128)(2,1)} async-done(((bf16[288,400]{1,0:T(8,128)(2,1)}), bf16[2304,400]{1,0:T(8,128)(2,1)}) %all-gather.18.cloned.1.call-update) | async-done | bytes 1843216 | tf_op jit(solution)/shard_map/all_gather | solution.py:415
  441.4 5.4 multiply_reduce_fusion.3
  449.3 39.5 %all-reduce.9 = (f32[2048]{0:T(1024)S(1)}, f32[2048]{0:T(1024)S(1)}, f32[256]{0:T(256)S(1)}, f32[256]{0:T(256)S(1)}) all-reduce(f32[2048]{0:T(1024)S(1)} %get-tuple-element.205, f32[2048]{0:T(1024)S(1)} %get-tuple-element.204, f32[256]{0:T(256)S(1)} %get-tuple-element.209, ...), channel_id=1, replica_groups=mesh['tm'=4,'batch'=8] {'tm','batch'}, use_global_device_ids=true, to_apply=%region_37.38 | all-reduce | flops 4608 | bytes 36864 | tf_op jit(solution)/shard_map/psum | solution.py:215
  499.3 40.2 %all-reduce.8 = (f32[512]{0:T(512)S(1)}, f32[512]{0:T(512)S(1)}, f32[64]{0:T(128)S(1)}, f32[64]{0:T(128)S(1)}) all-reduce(f32[512]{0:T(512)S(1)} %get-tuple-element.219, f32[512]{0:T(512)S(1)} %get-tuple-element.218, f32[64]{0:T(128)S(1)} %get-tuple-element.215, ...), channel_id=1, replica_groups=mesh['tm'=4,'batch'=8] {'tm','batch'}, use_global_device_ids=true, to_apply=%region_41.42 | all-reduce | flops 1152 | bytes 9216 | tf_op jit(solution)/shard_map/psum | solution.py:215
  551.8 40.2 %all-reduce.7 = (f32[512]{0:T(512)S(1)}, f32[512]{0:T(512)S(1)}, f32[64]{0:T(128)S(1)}, f32[64]{0:T(128)S(1)}, f32[400]{0:T(512)}) all-reduce(f32[512]{0:T(512)S(1)} %get-tuple-element.217, f32[512]{0:T(512)S(1)} %get-tuple-element.216, f32[64]{0:T(128)S(1)} %get-tuple-element.213, ...), channel_id=1, replica_groups=mesh['tm'=4,'batch'=8] {'tm','batch'}, use_global_device_ids=true, to_apply=%region_45.46 | all-reduce | flops 1552 | bytes 12416 | tf_op jit(solution)/shard_map/psum | solution.py:215
  603.4 3.8 collective-permute-start.6
  609.8 4.5 collective-permute-start.8
  614.4 4.4 fusion.106
  620.2 4.3 fusion.105
  624.5 9.0 convolution_bitcast_fusion.4
  635.9 4.7 convolution_bitcast_fusion.24
  669.1 9.7 copy.183
  683.6 4.9 convolution_bitcast_fusion
  695.8 5.0 pad_maximum_fusion
  711.2 7.0 reduce-scatter.46.cloned.1.call-done
  720.1 71.7 %reduce-scatter.48.cloned.1.call-done = f32[64,1280]{1,0:T(8,128)} async-done(((f32[512,1280]{1,0:T(8,128)}), f32[64,1280]{1,0:T(8,128)}) %reduce-scatter.48.cloned.1.call-update) | async-done | bytes 327696
  793.8 164.3 %reduce-scatter.50.cloned.1.call-done = f32[64,4608]{1,0:T(8,128)} async-done(((f32[512,4608]{1,0:T(8,128)}), f32[64,4608]{1,0:T(8,128)}) %reduce-scatter.50.cloned.1.call-update) | async-done | bytes 1179664
  961.0 95.6 %reduce-scatter.30.cloned.1.call-done = f32[288,400]{1,0:T(8,128)} async-done(((f32[2304,400]{1,0:T(8,128)}), f32[288,400]{1,0:T(8,128)}) %reduce-scatter.30.cloned.1.call-update) | async-done | bytes 460816 | tf_op jit(solution)/shard_map/reduce_scatter | solution.py:534
  1056.6 91.9 %reduce-scatter.24.cloned.1.call-done = f32[256,512]{1,0:T(8,128)} async-done(((f32[2048,512]{1,0:T(8,128)}), f32[256,512]{1,0:T(8,128)}) %reduce-scatter.24.cloned.1.call-update) | async-done | bytes 524304 | tf_op jit(solution)/shard_map/reduce_scatter | solution.py:530
  1148.5 210.6 %reduce-scatter.22.cloned.1.call-done = f32[64,6144]{1,0:T(8,128)} async-done(((f32[512,6144]{1,0:T(8,128)}), f32[64,6144]{1,0:T(8,128)}) %reduce-scatter.22.cloned.1.call-update) | async-done | bytes 1572880 | tf_op jit(solution)/shard_map/reduce_scatter | solution.py:528
  1364.5 67.1 %all-reduce.23.cloned.1.call-done = f32[64,576]{1,0:T(8,128)} async-done(((f32[64,576]{1,0:T(8,128)}), f32[64,576]{1,0:T(8,128)}) %all-reduce.23.cloned.1.call-update) | async-done | bytes 147472
  1432.3 64.0 %reduce-scatter.28.cloned.1.call-done = f32[32,64]{1,0:T(8,128)} async-done(((f32[256,64]{1,0:T(8,128)}), f32[32,64]{1,0:T(8,128)}) %reduce-scatter.28.cloned.1.call-update) | async-done | bytes 8208 | tf_op jit(solution)/shard_map/reduce_scatter | solution.py:533
  1496.4 64.2 %reduce-scatter.26.cloned.1.call-done = f32[8,768]{1,0:T(8,128)} async-done(((f32[64,768]{1,0:T(8,128)}), f32[8,768]{1,0:T(8,128)}) %reduce-scatter.26.cloned.1.call-update) | async-done | bytes 24592 | tf_op jit(solution)/shard_map/reduce_scatter | solution.py:531
  1560.5 12.1 all-reduce.14
  1574.5 104.4 %all-reduce.27.cloned.1.call-done = (f32[288,192]{0,1:T(8,128)}, f32[64,1280]{0,1:T(8,128)}, f32[64,6144]{1,0:T(8,128)}, f32[64,4608]{0,1:T(8,128)}, f32[256,512]{1,0:T(8,128)}, /*index=5*/f32[288,400]{1,0:T(8,128)}) async-done(((f32[288,192]{0,1:T(8,128)}, f32[64,1280]{0,1:T(8,128)}, f32[64,6144]{1,0:T(8,128)}, f32[64,4608]{0,1:T(8,128)}, f32[256,512]{1,0:T(8,128)}, /*index=5*/f32[288,400]{1,0:T(8,128)}), ...) | async-done | bytes 4286480 | tf_op jit(solution)/shard_map/psum | solution.py:536
  1693.6 22.0 all-reduce.13
  1727.3 4.1 fusion.317
  1733.0 3.7 fusion.318
  1738.2 30.6 %all_gather.91 = bf16[256,64]{1,0:T(8,128)(2,1)S(1)} all-gather(bf16[32,64]{1,0:T(8,128)(2,1)S(1)} %get-tuple-element.278), channel_id=1, replica_groups=mesh['tm'=4,'batch'=8] {'batch'}, dimensions={0}, use_global_device_ids=true | all-gather | bytes 36864 | tf_op jit(solution)/shard_map/all_gather | solution.py:571
  1772.3 30.8 %all_gather.90 = bf16[64,576]{1,0:T(8,128)(2,1)S(1)} all-gather(bf16[8,576]{1,0:T(8,128)(2,1)S(1)} %get-tuple-element.280), channel_id=1, replica_groups=mesh['tm'=4,'batch'=8] {'batch'}, dimensions={0}, use_global_device_ids=true | all-gather | bytes 82944 | tf_op jit(solution)/shard_map/all_gather | solution.py:570
  1805.2 31.6 %all_gather.89 = bf16[64,768]{1,0:T(8,128)(2,1)S(1)} all-gather(bf16[8,768]{1,0:T(8,128)(2,1)S(1)} %get-tuple-element.282), channel_id=1, replica_groups=mesh['tm'=4,'batch'=8] {'batch'}, dimensions={0}, use_global_device_ids=true | all-gather | bytes 110592 | tf_op jit(solution)/shard_map/all_gather | solution.py:569
  1837.6 35.8 %all_gather.84 = bf16[2304,192]{1,0:T(8,128)(2,1)S(1)} all-gather(bf16[288,192]{1,0:T(8,128)(2,1)S(1)} %copy.100), channel_id=1, replica_groups=mesh['tm'=4,'batch'=8] {'batch'}, dimensions={0}, use_global_device_ids=true | all-gather | bytes 995328 | tf_op jit(solution)/shard_map/all_gather | solution.py:564
  1873.4 15.7 conditional.8
  1890.6 16.0 conditional.9
  1907.8 11.2 conditional.12
  1919.0 3.9 copy.106
  1923.0 11.0 conditional.11
  1934.1 70.3 %all-gather.22.cloned.1.call-done = bf16[512,6144]{1,0:T(8,128)(2,1)} async-done(((bf16[64,6144]{1,0:T(8,128)(2,1)}), bf16[512,6144]{1,0:T(8,128)(2,1)}) %all-gather.22.cloned.1.call-update) | async-done | bytes 6291472 | tf_op jit(solution)/shard_map/all_gather | solution.py:566
  2004.4 6.2 conditional.10
  2004.4 3.5 broadcast.455
  2016.5 3.7 multiply_subtract_fusion.2
  2020.2 47.1 %reduce-scatter.44.cloned.1.call-done = bf16[32,64]{1,0:T(8,128)(2,1)} async-done(((bf16[256,64]{1,0:T(8,128)(2,1)}), bf16[32,64]{1,0:T(8,128)(2,1)}) %reduce-scatter.44.cloned.1.call-update) | async-done | bytes 4112 | tf_op jit(solution)/shard_map/reduce_scatter | solution.py:582
  2068.6 70.5 %all-reduce.25.cloned.1.call-done = bf16[64,576]{1,0:T(8,128)(2,1)} async-done(((bf16[64,576]{1,0:T(8,128)(2,1)}), bf16[64,576]{1,0:T(8,128)(2,1)}) %all-reduce.25.cloned.1.call-update) | async-done | bytes 73744
  2140.4 59.9 %reduce-scatter.42.cloned.1.call-done = bf16[8,768]{1,0:T(8,128)(2,1)} async-done(((bf16[64,768]{1,0:T(8,128)(2,1)}), bf16[8,768]{1,0:T(8,128)(2,1)}) %reduce-scatter.42.cloned.1.call-update) | async-done | bytes 12304 | tf_op jit(solution)/shard_map/reduce_scatter | solution.py:580
  2201.6 65.7 %reduce-scatter.32.cloned.1.call-done = bf16[288,192]{1,0:T(8,128)(2,1)} async-done(((bf16[2304,192]{1,0:T(8,128)(2,1)}), bf16[288,192]{1,0:T(8,128)(2,1)}) %reduce-scatter.32.cloned.1.call-update) | async-done | bytes 110608 | tf_op jit(solution)/shard_map/reduce_scatter | solution.py:575
  2269.0 65.6 %reduce-scatter.34.cloned.1.call-done = bf16[64,1280]{1,0:T(8,128)(2,1)} async-done(((bf16[512,1280]{1,0:T(8,128)(2,1)}), bf16[64,1280]{1,0:T(8,128)(2,1)}) %reduce-scatter.34.cloned.1.call-update) | async-done | bytes 163856 | tf_op jit(solution)/shard_map/reduce_scatter | solution.py:576
  2336.4 68.5 %reduce-scatter.40.cloned.1.call-done = bf16[256,512]{1,0:T(8,128)(2,1)} async-done(((bf16[2048,512]{1,0:T(8,128)(2,1)}), bf16[256,512]{1,0:T(8,128)(2,1)}) %reduce-scatter.40.cloned.1.call-update) | async-done | bytes 262160 | tf_op jit(solution)/shard_map/reduce_scatter | solution.py:579
  2406.9 95.8 %reduce-scatter.38.cloned.1.call-done = bf16[64,4608]{1,0:T(8,128)(2,1)} async-done(((bf16[512,4608]{1,0:T(8,128)(2,1)}), bf16[64,4608]{1,0:T(8,128)(2,1)}) %reduce-scatter.38.cloned.1.call-update) | async-done | bytes 589840 | tf_op jit(solution)/shard_map/reduce_scatter | solution.py:578
  2504.9 119.0 %reduce-scatter.36.cloned.1.call-done = bf16[64,6144]{1,0:T(8,128)(2,1)} async-done(((bf16[512,6144]{1,0:T(8,128)(2,1)}), bf16[64,6144]{1,0:T(8,128)(2,1)}) %reduce-scatter.36.cloned.1.call-update) | async-done | bytes 786448 | tf_op jit(solution)/shard_map/reduce_scatter | solution.py:577
  (639 shorter events, 242.2 us)
Async XLA Ops:
  7.2 162.5 %all-gather.12.cloned.1.call-start = ((), (), s32[]{:S(2)}) async-start(), calls=%async_computation.16 | async-start | bytes 1474560 | tf_op jit(solution)/shard_map/all_gather | solution.py:408
  9.0 164.7 %all-gather.10.cloned.1.call-start = ((), (), s32[]{:S(2)}) async-start(), calls=%async_computation.15 | async-start | bytes 7077888 | tf_op jit(solution)/shard_map/all_gather | solution.py:409
  11.5 234.7 %all-gather.14.cloned.1.call-start = ((), (), s32[]{:S(2)}) async-start(), calls=%async_computation.17 | async-start | bytes 5308416 | tf_op jit(solution)/shard_map/all_gather | solution.py:410
  12.5 285.0 %all-gather.16.cloned.1.call-start = ((), (), s32[]{:S(2)}) async-start(), calls=%async_computation.18 | async-start | bytes 2359296 | tf_op jit(solution)/shard_map/all_gather | solution.py:411
  54.4 119.3 %collective-permute-start.1 = (bf16[8,1,7,7,2048]{4,0,3,2,1:T(8,128)(2,1)}, bf16[8,1,7,7,2048]{4,0,3,2,1:T(8,128)(2,1)}, u32[]{:S(2)}, u32[]{:S(2)}) collective-permute-start(bf16[8,1,7,7,2048]{4,0,3,2,1:T(8,128)(2,1)} %convert_bitcast_fusion), channel_id=1, source_target_pairs={{8,0},{16,8},{24,16},{9,1},{17,9},{25,17},{10,2},{18,10},{26,18},{... | collective-permute-start | bytes 4816904 | tf_op jit(solution)/shard_map/ppermute | solution.py:44
  55.8 124.1 %collective-permute-start = (bf16[8,1,7,7,2048]{4,0,3,2,1:T(8,128)(2,1)}, bf16[8,1,7,7,2048]{4,0,3,2,1:T(8,128)(2,1)}, u32[]{:S(2)}, u32[]{:S(2)}) collective-permute-start(bf16[8,1,7,7,2048]{4,0,3,2,1:T(8,128)(2,1)} %convert_bitcast_fusion), channel_id=1, source_target_pairs={{0,8},{8,16},{16,24},{1,9},{9,17},{17,25},{2,10},{10,18},{18,26},{... | collective-permute-start | bytes 4816904 | tf_op jit(solution)/shard_map/ppermute | solution.py:42
  61.7 589.4 %copy-start = (bf16[8,4,7,7,256]{4,0,3,2,1:T(8,128)(2,1)}, bf16[8,4,7,7,256]{4,0,3,2,1:T(8,128)(2,1)S(1)}, u32[]{:S(2)}) copy-start(bf16[8,4,7,7,256]{4,0,3,2,1:T(8,128)(2,1)S(1)} %get-tuple-element.329) | copy-start | bytes 2408452
  61.8 74.1 %copy-start.77 = (f32[8,576]{1,0:T(8,128)S(1)}, f32[8,576]{1,0:T(8,128)}, u32[]{:S(2)}) copy-start(f32[8,576]{1,0:T(8,128)} %param.66) | copy-start | bytes 55300
  61.8 105.7 %collective-permute-start.4 = (bf16[8,1,7,7,256]{4,0,3,2,1:T(8,128)(2,1)S(1)}, bf16[8,1,7,7,256]{4,0,3,2,1:T(8,128)(2,1)S(1)}, u32[]{:S(2)}, u32[]{:S(2)}) collective-permute-start(bf16[8,1,7,7,256]{4,0,3,2,1:T(8,128)(2,1)S(1)} %get-tuple-element.303), channel_id=1, source_target_pairs={{8,0},{16,8},{24,16},{9,1},{17,9},{25,17},{10,2},{18,10},{26,18},{... | collective-permute-start | bytes 602120 | tf_op jit(solution)/shard_map/ppermute | solution.py:44
  63.2 104.7 %collective-permute-start.3 = (bf16[8,1,7,7,256]{4,0,3,2,1:T(8,128)(2,1)S(1)}, bf16[8,1,7,7,256]{4,0,3,2,1:T(8,128)(2,1)}, u32[]{:S(2)}, u32[]{:S(2)}) collective-permute-start(bf16[8,1,7,7,256]{4,0,3,2,1:T(8,128)(2,1)S(1)} %get-tuple-element.302), channel_id=1, source_target_pairs={{0,8},{8,16},{16,24},{1,9},{9,17},{17,25},{2,10},{10,18},{18,26},{... | collective-permute-start | bytes 602120 | tf_op jit(solution)/shard_map/ppermute | solution.py:42
  67.8 103.6 %collective-permute-start.2 = (bf16[8,2,7,7,256]{4,0,3,2,1:T(8,128)(2,1)}, bf16[8,2,7,7,256]{4,0,3,2,1:T(8,128)(2,1)S(1)}, u32[]{:S(2)}, u32[]{:S(2)}) collective-permute-start(bf16[8,2,7,7,256]{4,0,3,2,1:T(8,128)(2,1)} %slice.647), channel_id=1, source_target_pairs={{0,8},{8,16},{16,24},{1,9},{9,17},{17,25},{2,10},{10,18},{18,26},{... | collective-permute-start | bytes 1204232 | tf_op jit(solution)/shard_map/ppermute | solution.py:54
  70.8 308.8 %all-reduce.21.cloned.1.call-start = ((), (), s32[]{:S(2)}) async-start(), calls=%async_computation.19 | async-start | bytes 131072 | tf_op jit(solution)/shard_map/psum | solution.py:467
  72.0 179.7 %copy-start.95 = (f32[512]{0:T(512)}, f32[512]{0:T(512)S(1)}, u32[]{:S(2)}) copy-start(f32[512]{0:T(512)S(1)} %get-tuple-element.313) | copy-start | bytes 6148
  72.0 179.7 %copy-start.105 = (f32[512]{0:T(512)}, f32[512]{0:T(512)S(1)}, u32[]{:S(2)}) copy-start(f32[512]{0:T(512)S(1)} %get-tuple-element.312) | copy-start | bytes 6148
  72.0 225.5 %copy-start.121 = (f32[512]{0:T(512)}, f32[512]{0:T(512)S(1)}, u32[]{:S(2)}) copy-start(f32[512]{0:T(512)S(1)} %get-tuple-element.310) | copy-start | bytes 6148
  72.0 225.5 %copy-start.147 = (f32[512]{0:T(512)}, f32[512]{0:T(512)S(1)}, u32[]{:S(2)}) copy-start(f32[512]{0:T(512)S(1)} %get-tuple-element.311) | copy-start | bytes 6148
  103.0 192.6 %copy-start.81 = (bf16[256,64]{1,0:T(8,128)(2,1)}, bf16[256,64]{1,0:T(8,128)(2,1)S(1)}, u32[]{:S(2)}) copy-start(bf16[256,64]{1,0:T(8,128)(2,1)S(1)} %all_gather.82) | copy-start | bytes 98308
  167.5 57.6 %copy-start.123 = (f32[64]{0:T(128)}, f32[64]{0:T(128)S(1)}, u32[]{:S(2)}) copy-start(f32[64]{0:T(128)S(1)} %get-tuple-element.317) | copy-start | bytes 772
  167.5 57.6 %copy-start.136 = (f32[64]{0:T(128)}, f32[64]{0:T(128)S(1)}, u32[]{:S(2)}) copy-start(f32[64]{0:T(128)S(1)} %get-tuple-element.316) | copy-start | bytes 772
  167.5 128.1 %copy-start.138 = (f32[64]{0:T(128)}, f32[64]{0:T(128)S(1)}, u32[]{:S(2)}) copy-start(f32[64]{0:T(128)S(1)} %get-tuple-element.314) | copy-start | bytes 772
  167.5 128.1 %copy-start.164 = (f32[64]{0:T(128)}, f32[64]{0:T(128)S(1)}, u32[]{:S(2)}) copy-start(f32[64]{0:T(128)S(1)} %get-tuple-element.315) | copy-start | bytes 772
  169.7 55.5 %copy-start.18 = (f32[8,4,7,7,64]{4,0,3,2,1:T(8,128)}, f32[8,4,7,7,64]{4,0,3,2,1:T(8,128)S(1)}, u32[]{:S(2)}) copy-start(f32[8,4,7,7,64]{4,0,3,2,1:T(8,128)S(1)} %get-tuple-element.331) | copy-start | bytes 1204228
  348.5 86.1 %all-gather.18.cloned.1.call-start = ((), (), s32[]{:S(2)}) async-start(), calls=%async_computation.20 | async-start | bytes 2654208 | tf_op jit(solution)/shard_map/all_gather | solution.py:415
  349.3 368.9 %reduce-scatter.46.cloned.1.call-start = ((), (), s32[]{:S(2)}) async-start(), calls=%async_computation.37 | async-start | bytes 2654208
  351.5 85.3 %copy-start.97 = (f32[256]{0:T(256)}, f32[256]{0:T(256)S(1)}, u32[]{:S(2)}) copy-start(f32[256]{0:T(256)S(1)} %get-tuple-element.308) | copy-start | bytes 3076
  352.9 83.9 %copy-start.100 = (f32[256]{0:T(256)}, f32[256]{0:T(256)S(1)}, u32[]{:S(2)}) copy-start(f32[256]{0:T(256)S(1)} %get-tuple-element.297) | copy-start | bytes 3076
  352.9 83.9 %copy-start.169 = (s32[8]{0:T(128)S(1)}, s32[8]{0:T(128)}, u32[]{:S(2)}) copy-start(s32[8]{0:T(128)} %param.56) | copy-start | bytes 100
  352.9 84.3 %copy-start.160 = (s32[8]{0:T(128)S(1)}, s32[8]{0:T(128)}, u32[]{:S(2)}) copy-start(s32[8]{0:T(128)} %param.58) | copy-start | bytes 100
  449.3 42.3 %copy-start.158 = (f32[64]{0:T(128)S(1)}, f32[64]{0:T(128)}, u32[]{:S(2)}) copy-start(f32[64]{0:T(128)} %copy-done.157) | copy-start | bytes 772
  497.1 42.4 %copy-start.30 = (f32[8,4,7,7,64]{4,0,3,2,1:T(8,128)S(1)}, f32[8,4,7,7,64]{4,0,3,2,1:T(8,128)}, u32[]{:S(2)}) copy-start(f32[8,4,7,7,64]{4,0,3,2,1:T(8,128)} %get-tuple-element.333) | copy-start | bytes 1204228
  497.1 42.4 %copy-start.56 = (f32[8,7,7,64]{3,0,2,1:T(8,128)S(1)}, f32[8,7,7,64]{3,0,2,1:T(8,128)}, u32[]{:S(2)}) copy-start(f32[8,7,7,64]{3,0,2,1:T(8,128)} %get-tuple-element.319) | copy-start | bytes 301060
  602.1 18.1 collective-permute-start.5
  603.4 21.1 collective-permute-start.6
  607.2 26.3 collective-permute-start.9
  608.5 10.2 collective-permute-start.7
  609.8 26.1 collective-permute-start.8
  646.5 145.3 %reduce-scatter.48.cloned.1.call-start = ((), (), s32[]{:S(2)}) async-start(), calls=%async_computation.38 | async-start | bytes 2949120
  655.5 302.6 %reduce-scatter.50.cloned.1.call-start = ((), (), s32[]{:S(2)}) async-start(), calls=%async_computation.39 | async-start | bytes 10616832
  678.8 377.8 %reduce-scatter.30.cloned.1.call-start = ((), (), s32[]{:S(2)}) async-start(), calls=%async_computation.25 | async-start | bytes 5308416 | tf_op jit(solution)/shard_map/reduce_scatter | solution.py:534
  682.4 466.1 %reduce-scatter.24.cloned.1.call-start = ((), (), s32[]{:S(2)}) async-start(), calls=%async_computation.22 | async-start | bytes 4718592 | tf_op jit(solution)/shard_map/reduce_scatter | solution.py:530
  688.5 670.6 %reduce-scatter.22.cloned.1.call-start = ((), (), s32[]{:S(2)}) async-start(), calls=%async_computation.21 | async-start | bytes 14155776 | tf_op jit(solution)/shard_map/reduce_scatter | solution.py:528
  700.9 730.8 %all-reduce.23.cloned.1.call-start = ((), (), s32[]{:S(2)}) async-start(), calls=%async_computation.40 | async-start | bytes 327680
  708.3 788.1 %reduce-scatter.28.cloned.1.call-start = ((), (), s32[]{:S(2)}) async-start(), calls=%async_computation.24 | async-start | bytes 147456 | tf_op jit(solution)/shard_map/reduce_scatter | solution.py:533
  708.8 851.7 %reduce-scatter.26.cloned.1.call-start = ((), (), s32[]{:S(2)}) async-start(), calls=%async_computation.23 | async-start | bytes 221184 | tf_op jit(solution)/shard_map/reduce_scatter | solution.py:531
  711.2 967.7 %all-reduce.27.cloned.1.call-start = ((), (), s32[]{:S(2)}) async-start(), calls=%async_computation.42 | async-start | bytes 11993088 | tf_op jit(solution)/shard_map/psum | solution.py:536
  1359.3 531.3 %all-gather.20.cloned.1.call-start = ((), (), s32[]{:S(2)}) async-start(), calls=%async_computation.27 | async-start | bytes 1474560 | tf_op jit(solution)/shard_map/all_gather | solution.py:565
  1362.6 211.9 %copy-start.68 = (f32[7312]{0:T(1024)}, f32[7312]{0:T(1024)S(1)}, u32[]{:S(2)}) copy-start(f32[7312]{0:T(1024)S(1)} %concatenate.58) | copy-start | bytes 87748
  1721.6 186.1 %all-gather.26.cloned.1.call-start = ((), (), s32[]{:S(2)}) async-start(), calls=%async_computation.33 | async-start | bytes 2359296 | tf_op jit(solution)/shard_map/all_gather | solution.py:568
  1724.4 198.6 %all-gather.24.cloned.1.call-start = ((), (), s32[]{:S(2)}) async-start(), calls=%async_computation.31 | async-start | bytes 5308416 | tf_op jit(solution)/shard_map/all_gather | solution.py:567
  1732.7 271.7 %all-gather.22.cloned.1.call-start = ((), (), s32[]{:S(2)}) async-start(), calls=%async_computation.29 | async-start | bytes 7077888 | tf_op jit(solution)/shard_map/all_gather | solution.py:566
  1736.7 330.6 %reduce-scatter.44.cloned.1.call-start = ((), (), s32[]{:S(2)}) async-start(), calls=%async_computation.36 | async-start | bytes 73728 | tf_op jit(solution)/shard_map/reduce_scatter | solution.py:582
  1771.0 368.1 %all-reduce.25.cloned.1.call-start = ((), (), s32[]{:S(2)}) async-start(), calls=%async_computation.41 | async-start | bytes 163840
  1803.8 396.6 %reduce-scatter.42.cloned.1.call-start = ((), (), s32[]{:S(2)}) async-start(), calls=%async_computation.35 | async-start | bytes 110592 | tf_op jit(solution)/shard_map/reduce_scatter | solution.py:580
  1837.5 429.8 %reduce-scatter.32.cloned.1.call-start = ((), (), s32[]{:S(2)}) async-start(), calls=%async_computation.26 | async-start | bytes 1327104 | tf_op jit(solution)/shard_map/reduce_scatter | solution.py:575
  1890.5 444.1 %reduce-scatter.34.cloned.1.call-start = ((), (), s32[]{:S(2)}) async-start(), calls=%async_computation.28 | async-start | bytes 1474560 | tf_op jit(solution)/shard_map/reduce_scatter | solution.py:576
  1907.7 497.2 %reduce-scatter.40.cloned.1.call-start = ((), (), s32[]{:S(2)}) async-start(), calls=%async_computation.34 | async-start | bytes 2359296 | tf_op jit(solution)/shard_map/reduce_scatter | solution.py:579
  1922.9 579.7 %reduce-scatter.38.cloned.1.call-start = ((), (), s32[]{:S(2)}) async-start(), calls=%async_computation.32 | async-start | bytes 5308416 | tf_op jit(solution)/shard_map/reduce_scatter | solution.py:578
  1934.0 689.9 %reduce-scatter.36.cloned.1.call-start = ((), (), s32[]{:S(2)}) async-start(), calls=%async_computation.30 | async-start | bytes 7077888 | tf_op jit(solution)/shard_map/reduce_scatter | solution.py:577
  2015.1 52.2 %copy-start.84 = (f32[32,64]{1,0:T(8,128)S(1)}, f32[32,64]{1,0:T(8,128)}, u32[]{:S(2)}) copy-start(f32[32,64]{1,0:T(8,128)} %param.67) | copy-start | bytes 24580
  2015.1 124.0 %copy-start.78 = (f32[8,576]{1,0:T(8,128)S(1)}, f32[8,576]{1,0:T(8,128)}, u32[]{:S(2)}) copy-start(f32[8,576]{1,0:T(8,128)} %param.66) | copy-start | bytes 55300
  2015.1 185.2 %copy-start.74 = (f32[8,768]{1,0:T(8,128)S(1)}, f32[8,768]{1,0:T(8,128)}, u32[]{:S(2)}) copy-start(f32[8,768]{1,0:T(8,128)} %param.65) | copy-start | bytes 73732
  2015.1 252.2 %copy-start.54 = (f32[288,192]{1,0:T(8,128)S(1)}, f32[288,192]{1,0:T(8,128)}, u32[]{:S(2)}) copy-start(f32[288,192]{1,0:T(8,128)} %param.60) | copy-start | bytes 663556
  2016.5 486.2 %copy-start.28 = (f32[64,4608]{1,0:T(8,128)S(1)}, f32[64,4608]{1,0:T(8,128)}, u32[]{:S(2)}) copy-start(f32[64,4608]{1,0:T(8,128)} %param.63) | copy-start | bytes 3538948
  2269.0 355.0 %copy-start.22 = (f32[64,6144]{1,0:T(8,128)S(1)}, f32[64,6144]{1,0:T(8,128)}, u32[]{:S(2)}) copy-start(f32[64,6144]{1,0:T(8,128)} %param.62) | copy-start | bytes 4718596
  (146 other events, 1097.1 us)
Sparse Core Ops, SparseCore 0:
  10.8 50.1 all-gather.11
  63.7 100.8 all-gather.9
  167.4 78.7 all-gather.13
  248.7 47.7 all-gather.15
  348.6 30.9 all-reduce.20
  382.5 52.0 all-gather.17
  646.6 71.5 reduce-scatter.45
  722.1 69.5 reduce-scatter.47
  795.8 162.3 reduce-scatter.49
  962.1 94.5 reduce-scatter.29
  1060.7 87.7 reduce-scatter.23
  1152.0 207.0 reduce-scatter.21
  1363.0 68.5 all-reduce.22
  1435.7 60.5 reduce-scatter.27
  1500.4 60.0 reduce-scatter.25
  1564.0 114.8 all-reduce.26
  1721.8 38.6 all-gather.19
  1763.0 49.2 all-gather.25
  1815.1 88.9 all-gather.23
  1906.7 97.6 all-gather.21
  2007.8 59.4 reduce-scatter.43
  2071.2 67.7 all-reduce.24
  2142.9 57.3 reduce-scatter.41
  2204.1 63.1 reduce-scatter.31
  2271.3 63.3 reduce-scatter.33
  2338.0 66.8 reduce-scatter.39
  2408.4 94.2 reduce-scatter.37
  2506.2 117.6 reduce-scatter.35
where the time goes:
time: 2650 us; the launch traced here: 2630 us
  waiting for transfers between devices  1690 us (64%)
  blocking collectives  541 us (20%)
  matrix products  138 us (5%)
  other arithmetic  107 us (4%)
  local copies, waits for them, and re-layouts  65.1 us (2%)
  loops' own time  37.9 us (1%)
  between operations  28.5 us (1%)
  starting transfers between devices  27.4 us (1%)
    unnamed x33, waiting for transfers between devices  381 us
    reduce_scatter x1, waiting for transfers between devices, per_device(): lax.psum_scatter(slow_grads[0], 'batch', scatter_dimension=0, tiled=True)  211 us
    psum x3, blocking collectives, norm_stats(): lax.psum((jnp.sum(mask * values, axis=(0, 1, 2, 3)), jnp.sum(mask * value...  120 us
    psum x3, blocking collectives, norm_back(): lax.psum((jnp.sum(mask * upstream, axis=(0, 1, 2, 3)), jnp.sum(mask * ups...  120 us
    reduce_scatter x1, waiting for transfers between devices, per_device(): lax.psum_scatter(orthos[2], 'batch', scatter_dimension=0, tiled=True)  119 us
    psum x1, waiting for transfers between devices, per_device(): lax.psum((summed[0], summed[1], summed[2], summed[3], summed[4], summed[5...  104 us
    reduce_scatter x1, waiting for transfers between devices, per_device(): lax.psum_scatter(orthos[3], 'batch', scatter_dimension=0, tiled=True)  95.8 us
    reduce_scatter x1, waiting for transfers between devices, per_device(): lax.psum_scatter(head_grad, 'batch', scatter_dimension=0, tiled=True)  95.6 us
  transfers between devices with their start and end apart: 38, of which 22 were waited for; matrix products, arithmetic and copies ran while one was open for 8% of the time, Pallas kernels for 0%

commit v1 on v0

v1 whole, which is shorter than its diff:
```python
import functools
import math

import jax
import jax.numpy as jnp
from jax import lax
from jax.experimental import pallas as pl
from jax.experimental.pallas import tpu as pltpu
from jax.sharding import PartitionSpec as P

CS = 2048
CSM = 512
CF = 256
CFM = 64
CLS = 400
ALPHA = 4
NS_STEPS = 3
STEP = 10


HIGHEST = lax.Precision.HIGHEST
NORM_EPS = 1e-05
CLIP_AT = 0.01
MUON_RATE = 0.5
MUON_KEEP = 0.95
WEIGHT_DECAY = 0.01
ADAM_ONE = 0.9
ADAM_TWO = 0.999
ADAM_EPS = 1e-08
HEAD_RATE = 0.02
AFFINE_RATE = 0.1
NS_FIRST = 3.4445
NS_SECOND = -4.775
NS_THIRD = 2.0315


F32 = jnp.float32
BF16 = jnp.bfloat16
VMEM = 61 * 1024 * 1024
SIDE_AT = 9 * CSM
CONDENSE_AT = SIDE_AT + 5 * CF
RESTORE_AT = CONDENSE_AT + 3 * CS
GRAM = BF16
SIX = (CSM, CSM, CS, CFM, CFM, CF)


def swap(values, axis, mask):
    count = lax.axis_size(axis)
    return lax.ppermute(values, axis, [(i, i ^ mask) for i in range(count)])


def shift(values, axis, step):
    count = lax.axis_size(axis)
    route = [(i, i + step) for i in range(count) if 0 <= i + step < count]
    return lax.ppermute(values, axis, route)


def spread_all(rows, axes):
    count = math.prod(lax.axis_size(axis) for axis in axes)
    copies = jnp.broadcast_to(rows[None], (count,) + rows.shape)
    return lax.all_to_all(copies, axes, 0, 0, tiled=True)


def all_sum(pieces, axes):
    flat = jnp.concatenate([piece.reshape(-1) for piece in pieces])
    length = flat.shape[0]
    wide = -(-length // 1024) * 128
    flat = jnp.pad(flat, (0, 8 * wide - length)).reshape(8, wide)
    total = jnp.sum(spread_all(flat, axes), axis=0).reshape(-1)
    parts = []
    start = 0
    for piece in pieces:
        parts.append(total[start : start + piece.size].reshape(piece.shape))
        start = start + piece.size
    return parts


def pick(values, dim, place):
    return lax.dynamic_index_in_dim(values, place, dim, keepdims=False)


def bits(axis, low):
    count = lax.axis_size(axis).bit_length() - 1
    return [(axis, bit) for bit in range(count - 1, low - 1, -1)]


def halve(view, live, order):
    live = list(live)
    for axis, bit in order:
        dim = live.index((axis, bit))
        flag = (lax.axis_index(axis) >> bit) & 1
        got = swap(pick(view, dim, 1 - flag).astype(BF16), axis, 1 << bit)
        view = pick(view, dim, flag) + got.astype(F32)
        live.remove((axis, bit))
    return view


def dot(left, right, dims):
    return lax.dot_general(left, right, ((dims[0], dims[1]), ((), ())), preferred_element_type=F32)


def rows_by_rows(left, right):
    return dot(left, right, ((1,), (1,)))


def rows_by_columns(left, right):
    return dot(left, right, ((1,), (0,)))


def over_rows(left, right):
    return dot(left, right, ((0,), (0,)))


def split_affine(vector):
    gains = []
    shifts = []
    start = 0
    for width in SIX:
        gains.append(vector[start : start + width])
        start = start + width
    for width in SIX:
        shifts.append(vector[start : start + width])
        start = start + width
    return (gains, shifts, vector[start : start + CLS])


def silu_grad(values):
    sigma = jax.nn.sigmoid(values)
    return sigma * (1.0 + values * (1.0 - sigma))


def call(kernel, outs, args, scratch=(), far=(), copies=0, micros=6, scalars=()):
    specs = [
        pl.BlockSpec(
            memory_space=pl.ANY
            if place in far
            else pltpu.SMEM
            if place in scalars
            else pltpu.VMEM
        )
        for place in range(len(args))
    ]
    shapes = [pltpu.VMEM(shape, kind) for shape, kind in scratch]
    if copies:
        shapes.append(pltpu.SemaphoreType.DMA((copies,)))
    return pl.pallas_call(
        kernel,
        in_specs=specs,
        out_shape=[jax.ShapeDtypeStruct(shape, kind) for shape, kind in outs],
        scratch_shapes=shapes,
        compiler_params=pltpu.CompilerParams(vmem_limit_bytes=VMEM),
        cost_estimate=pl.CostEstimate(
            flops=micros * 1150000000, bytes_accessed=micros * 3000000, transcendentals=0
        ),
    )(*args)


def fetch(source, target, flags, spans):
    started = []
    for place, (there, here, width) in enumerate(spans):
        copy = pltpu.make_async_copy(
            source.at[:, pl.ds(there, width)], target.at[:, pl.ds(here, width)], flags.at[place]
        )
        copy.start()
        started.append(copy)
    return started


def fetch_tall(source, target, flags, start):
    started = []
    count = flags.shape[0] // 4
    block = source.shape[0] // count
    for place in range(4 * count):
        b, k = (place // 4, place % 4)
        copy = pltpu.make_async_copy(
            source.at[pl.ds(b * block, block), pl.ds(start + k * CSM, CSM)],
            target.at[pl.ds(place * block, block), :],
            flags.at[place],
        )
        copy.start()
        started.append(copy)
    return started


def nt(left, right):
    return dot(left, right, ((1,), (1,)))


def nn(left, right):
    return dot(left, right, ((1,), (0,)))


def silu(values):
    return values * jax.nn.sigmoid(values)


def low(values):
    return values.astype(BF16)


def sums(held, other):
    return (
        jnp.sum(held, axis=0, keepdims=True),
        jnp.sum(held * other, axis=0, keepdims=True),
    )


def flat(values):
    return values.reshape(values.shape[0] * values.shape[1], values.shape[2])


def put_narrow(out, block, slow, fast, extra=()):
    block[...] = jnp.zeros_like(block)
    for place, vector in enumerate(slow):
        block[2 * place : 2 * place + 1, :] = vector[:, 0:256]
        block[2 * place + 1 : 2 * place + 2, :] = vector[:, 256:512]
    for place, vector in enumerate(fast):
        block[4 + place : 5 + place, 0:CFM] = vector
    for place, value in enumerate(extra):
        block[6 + place : 7 + place, 0:128] = jnp.broadcast_to(value, (1, 128))
    out[...] = jnp.broadcast_to(block[...][None], out.shape).astype(out.dtype)


def get_narrow(total):
    slow = [
        jnp.concatenate([total[2 * k : 2 * k + 1], total[2 * k + 1 : 2 * k + 2]], axis=1)
        for k in range(2)
    ]
    fast = [total[4 + k : 5 + k, 0:CFM] for k in range(2)]
    return slow, fast


def put_wide(out, slow, fast, extra=None):
    out[...] = jnp.zeros_like(out)
    for place, vector in enumerate(slow):
        for row in range(4):
            out[4 * place + row : 4 * place + row + 1, 0:512] = vector[:, 512 * row : 512 * row + 512]
    for place, vector in enumerate(fast):
        for row in range(2):
            spot = 2 * place + row
            out[spot : spot + 1, 512:640] = vector[:, 128 * row : 128 * row + 128]
    if extra is not None:
        for row in range(4, 7):
            part = low(jnp.broadcast_to(extra, (1, 128))).astype(F32)
            out[row : row + 1, 512:640] = part
            extra = extra - part


def get_wide(total):
    slow = [
        jnp.concatenate([total[4 * k + row : 4 * k + row + 1, 0:512] for row in range(4)], axis=1)
        for k in range(2)
    ]
    fast = [
        jnp.concatenate(
            [total[2 * k + row : 2 * k + row + 1, 512:640] for row in range(2)], axis=1
        )
        for k in range(2)
    ]
    return slow, fast


def moments(pair, count):
    mean = pair[0] / count
    spread = pair[1] / count - mean * mean
    return mean, lax.rsqrt(spread + NORM_EPS)


def counts(total, frames):
    count = total[6:7, 0:1]
    return count, count * frames


def in_relation(place, outs, values):
    for k, out in enumerate(outs):
        for p, value in enumerate(values):

            @pl.when(jnp.bitwise_xor(place, k) == p)
            def store(out=out, value=value):
                out[...] = value


def stem_kernel(
    near, place, slow_video, fast_video, weight, mask, slow_pre, fast_pre, slow_low, fast_low, *shares
):
    held = mask[...]
    for k in range(3):
        pre = nt(slow_video[k], weight[0:CS, :])
        if k == 1:
            slow_pre[...] = pre
        act = low(silu(pre) * held)
        slow_low[k] = act
        if k == 1 and near:
            width = CS // 4
            parts = [act[:, p * width : (p + 1) * width] for p in range(4)]
            in_relation(place[0], shares[0:4], parts)
        elif k == 1:
            count, _, width = shares[0].shape
            for p in range(count):
                shares[0][p] = act[:, p * width : (p + 1) * width]
    count = fast_video.shape[0]
    for k in range(count):
        pre = nt(fast_video[k], weight[CS:, :])
        if 2 <= k < count - 1:
            fast_pre[k - 2] = pre
        act = low(silu(pre) * held)
        fast_low[k] = act
        if near and k < 5:
            parts = [act[:, 0:128], act[:, 128:256]]
            in_relation(place[0] // 2, [side.at[k] for side in shares[4:6]], parts)


def first_kernel(
    slow_low, fast_low, weights, squeeze, mask, valid, h1, h4, out, block, first, flags
):
    spans = [(SIDE_AT, 0, 5 * CF)]
    spans += [(CONDENSE_AT + k * CS, 5 * CF + k * CS, CS) for k in range(3)]
    copies = fetch(weights, first, flags, spans)
    held = mask[...]
    copies[0].wait()
    total = None
    for k in range(5):
        term = nt(fast_low[k], first[:, k * CF : (k + 1) * CF])
        total = term if total is None else total + term
    for k in range(3):
        start = 5 * CF + k * CS
        copies[1 + k].wait()
        total = total + nt(slow_low[k], first[:, start : start + CS])
    h1[...] = total
    slow = sums(total * held, total)
    frames = h4.shape[0]
    fast = None
    for frame in range(frames):
        piece = None
        for k in range(3):
            term = nt(fast_low[1 + k + frame], squeeze[:, k * CF : (k + 1) * CF])
            piece = term if piece is None else piece + term
        h4[frame] = piece
        pair = sums(piece * held, piece)
        fast = pair if fast is None else tuple(a + b for a, b in zip(fast, pair))
    put_narrow(out, block, slow, fast, (jnp.sum(held), jnp.sum(valid[...])))


def fill(pad, values):
    side = pad.shape[0] - 2
    pad[1 : side + 1, 1 : side + 1] = values.reshape(side, side, pad.shape[2], pad.shape[3])


def tap_of(pad, down, right):
    side = pad.shape[0] - 2
    values = pad[down : down + side, right : right + side]
    return values.reshape(side * side * pad.shape[2], pad.shape[3])


def second_kernel(near, *refs):
    place, h1, h4, got, slow_par, fast_par, mask, weights, blending = refs[0:9]
    h2, h5, total_out, out = refs[9:13]
    shares = refs[13:17] if near else refs[13:14]
    pad, fast_pad, block, mixing, flags = refs[-5:]
    copies = fetch(weights, mixing, flags, [(tap * CSM, tap * CSM, CSM) for tap in range(9)])
    held = mask[...]
    frames = h4.shape[0]
    total = jnp.sum(got[...].astype(F32), axis=0)
    total_out[...] = total
    slow, fast = get_narrow(total)
    slow_count, fast_count = counts(total, frames)
    mean, inverse = moments(slow, slow_count)
    level = slow_par[0:1] * ((h1[...] - mean) * inverse) + slow_par[1:2]
    pad[...] = jnp.zeros_like(pad)
    act = low(silu(level) * held)
    if near:
        in_relation(place[0], shares, [act[:, p * 128 : (p + 1) * 128] for p in range(4)])
    else:
        shares[0][...] = act
    fill(pad, act.astype(F32))
    acc = None
    for tap in range(9):
        piece = low(tap_of(pad, tap // 3, tap % 3))
        copies[tap].wait()
        term = nt(piece, mixing[:, tap * CSM : (tap + 1) * CSM])
        acc = term if acc is None else acc + term
    h2[...] = acc
    slow_pair = sums(acc * held, acc)
    mean, inverse = moments(fast, fast_count)
    fast_pad[...] = jnp.zeros_like(fast_pad)
    fast_pair = None
    for frame in range(frames):
        level = fast_par[0:1] * ((h4[frame] - mean) * inverse) + fast_par[1:2]
        fill(fast_pad, low(silu(level) * held).astype(F32))
        acc = None
        for tap in range(9):
            piece = low(tap_of(fast_pad, tap // 3, tap % 3))
            term = nn(piece, blending[tap])
            acc = term if acc is None else acc + term
        h5[frame] = acc
        pair = sums(acc * held, acc)
        fast_pair = pair if fast_pair is None else tuple(a + b for a, b in zip(fast_pair, pair))
    put_narrow(out, block, slow_pair, fast_pair)


def third_kernel(
    h2, h5, before, got, slow_par, fast_par, mask, weights, recover, a2, a5, h3, h6, total_out, out,
    restore, flags,
):
    copies = fetch_tall(weights, restore, flags, RESTORE_AT)
    held = mask[...]
    frames = h5.shape[0]
    total = jnp.sum(got[...].astype(F32), axis=0)
    total_out[...] = total
    slow, fast = get_narrow(total)
    slow_count, fast_count = counts(before[...], frames)
    mean, inverse = moments(slow, slow_count)
    level = slow_par[0:1] * ((h2[...] - mean) * inverse) + slow_par[1:2]
    act = low(silu(level) * held)
    a2[...] = act
    for copy in copies:
        copy.wait()
    acc = nt(act, restore[...])
    h3[...] = acc
    slow_pair = sums(acc * held, acc)
    mean, inverse = moments(fast, fast_count)
    fast_pair = None
    for frame in range(frames):
        level = fast_par[0:1] * ((h5[frame] - mean) * inverse) + fast_par[1:2]
        act = low(silu(level) * held)
        a5[frame] = act
        acc = nt(act, recover[...])
        h6[frame] = acc
        pair = sums(acc * held, acc)
        fast_pair = pair if fast_pair is None else tuple(a + b for a, b in zip(fast_pair, pair))
    put_wide(out, slow_pair, fast_pair)


def by_clip(values, clips):
    return jnp.sum(values.reshape(-1, clips, values.shape[1]), axis=0)


def pool_kernel(
    h3, h6, slow_pre, fast_pre, before, got, slow_par, fast_par, mask, out, total_out
):
    held = mask[...]
    frames = h6.shape[0]
    clips = out.shape[0]
    total = jnp.sum(got[...].astype(F32), axis=0)
    total_out[...] = total
    slow, fast = get_wide(total)
    slow_count, fast_count = counts(before[...], frames)
    mean, inverse = moments(slow, slow_count)
    scaled = (h3[...] - mean) * inverse
    residual = silu(slow_pre[...]) * held + slow_par[0:1] * scaled + slow_par[1:2]
    out[:, 0:CS] = by_clip(silu(residual) * held, clips)
    mean, inverse = moments(fast, fast_count)
    pooled = None
    for frame in range(frames):
        scaled = (h6[frame] - mean) * inverse
        residual = silu(fast_pre[frame]) * held + fast_par[0:1] * scaled + fast_par[1:2]
        part = by_clip(silu(residual) * held, clips)
        pooled = part if pooled is None else pooled + part
    out[:, CS:] = pooled


def mixed(average, values):
    total = None
    for k in range(values.shape[0]):
        term = average[:, k : k + 1] * values[k : k + 1, :]
        total = term if total is None else total + term
    return total


def head_kernel(
    pools, head, bias, ids_down, ids_across, labels, valid, area, h3, h6, slow_pre, fast_pre,
    before, total_in, slow_par, fast_par, mask, features, logit_low, d3, d6, out,
):
    held = mask[...]
    frames = h6.shape[0]
    clips = features.shape[0]
    tm_count = pools.shape[0]
    parts = [pools[k] for k in range(tm_count)]
    while len(parts) > 1:
        parts = [parts[k] + parts[k + 1] for k in range(0, len(parts), 2)]
    (pool,) = parts
    slow_divide = area[...] * tm_count
    fast_divide = slow_divide * frames
    slow_feature = low(pool[:, 0:CS] / slow_divide)
    fast_feature = low(pool[:, CS:] / fast_divide)
    features[:, 0:CS] = slow_feature
    features[:, CS:] = fast_feature
    logits = nn(slow_feature, head[0:CS, :]) + nn(fast_feature, head[CS:, :]) + bias[...]
    same = (ids_down[...] == ids_across[...]).astype(F32)
    average = same / jnp.sum(same, axis=1, keepdims=True)
    mean_logits = mixed(average, logits)
    top = jnp.max(mean_logits, axis=1, keepdims=True)
    powers = jnp.exp(mean_logits - top)
    whole = jnp.sum(powers, axis=1, keepdims=True)
    classes = lax.broadcasted_iota(jnp.int32, mean_logits.shape, 1)
    onehot = (labels[...] == classes).astype(F32)
    picked = jnp.sum(onehot * mean_logits, axis=1, keepdims=True)
    loss = jnp.sum(valid[...] * (jnp.log(whole) + top - picked))
    mean_grad = valid[...] * (powers / whole - onehot)
    logit = low(mixed(average, mean_grad))
    logit_low[...] = logit
    slow_count, fast_count = counts(before[...], frames)
    slow, fast = get_wide(total_in[...])

    grad = nt(logit, head[0:CS, :]) / slow_divide
    mean, inverse = moments(slow, slow_count)
    scaled = (h3[...] - mean) * inverse
    residual = silu(slow_pre[...]) * held + slow_par[0:1] * scaled + slow_par[1:2]
    down = held * silu_grad(residual)
    down = (down.reshape(-1, clips, CS) * grad[None]).reshape(down.shape)
    d3[...] = down
    slow_pair = sums(down, scaled)

    grad = nt(logit, head[CS:, :]) / fast_divide
    mean, inverse = moments(fast, fast_count)
    fast_pair = None
    for frame in range(frames):
        scaled = (h6[frame] - mean) * inverse
        residual = silu(fast_pre[frame]) * held + fast_par[0:1] * scaled + fast_par[1:2]
        down = held * silu_grad(residual)
        down = (down.reshape(-1, clips, CF) * grad[None]).reshape(down.shape)
        d6[frame] = down
        pair = sums(down, scaled)
        fast_pair = pair if fast_pair is None else tuple(a + b for a, b in zip(fast_pair, pair))
    put_wide(out, slow_pair, fast_pair, loss)


def under(upstream, values, mean, inverse, gain, pair, count, held):
    scaled = (values - mean) * inverse
    return low(held * gain * inverse * (upstream - (pair[0] + scaled * pair[1]) / count))


def third_back_kernel(
    near, place, d3, d6, h3, h6, h2, h5, before, total3, total2, got, slow3, fast3, slow2, fast2, mask,
    weights, recover, u6, e2, e5, total_out, out, *rest
):
    u3 = rest[0:4] if near else rest[0:1]
    block, restore, flags = rest[-3:]
    copies = fetch_tall(weights, restore, flags, RESTORE_AT)
    held = mask[...]
    frames = h6.shape[0]
    total = jnp.sum(got[...].astype(F32), axis=0)
    total_out[...] = total
    slow_count, fast_count = counts(before[...], frames)
    slow_pair, fast_pair = get_wide(total)
    slow, fast = get_wide(total3[...])
    slow_two, fast_two = get_narrow(total2[...])
    mean, inverse = moments(slow, slow_count)
    upper = under(d3[...], h3[...], mean, inverse, slow3[0:1], slow_pair, slow_count, held)
    if near:
        wide = upper.astype(F32)
        tiles = [wide[:, k * 128 : (k + 1) * 128] for k in range(CS // 128)]
        turned = [pltpu.roll(tile, 64, 1) for tile in tiles]
        first_half = lax.broadcasted_iota(jnp.int32, tiles[0].shape, 1) < 64
        parts = []
        for p in range(4):
            held_tiles = []
            for k in range(4):
                one = 4 * k + p // 2
                two = one + 2
                if p % 2 == 0:
                    tile = jnp.where(first_half, tiles[one], turned[two])
                else:
                    tile = jnp.where(first_half, turned[one], tiles[two])
                held_tiles.append(low(tile))
            parts.append(jnp.concatenate(held_tiles, axis=1))
        in_relation(place[0], u3, parts)
    else:
        u3[0][...] = upper
    mean, inverse = moments(slow_two, slow_count)
    scaled = (h2[...] - mean) * inverse
    for copy in copies:
        copy.wait()
    down = nn(upper, restore[...]) * held * silu_grad(slow2[0:1] * scaled + slow2[1:2])
    e2[...] = down
    slow_out = sums(down, scaled)
    mean, inverse = moments(fast, fast_count)
    mean_two, inverse_two = moments(fast_two, fast_count)
    fast_out = None
    for frame in range(frames):
        upper = under(d6[frame], h6[frame], mean, inverse, fast3[0:1], fast_pair, fast_count, held)
        u6[frame] = upper
        scaled = (h5[frame] - mean_two) * inverse_two
        down = nn(upper, recover[...]) * held * silu_grad(fast2[0:1] * scaled + fast2[1:2])
        e5[frame] = down
        pair = sums(down, scaled)
        fast_out = pair if fast_out is None else tuple(a + b for a, b in zip(fast_out, pair))
    put_narrow(out, block, slow_out, fast_out)


def second_back_kernel(
    e2, e5, h2, h5, h1, h4, total2, total1, got, slow2, fast2, slow1, fast1, mask,
    weights, blending, u2, u5, e1, e4, blend_grad, total_out, out, pad, fast_pad, act_pad, block,
    mixing, flags,
):
    copies = fetch(weights, mixing, flags, [(tap * CSM, tap * CSM, CSM) for tap in range(9)])
    held = mask[...]
    frames = h5.shape[0]
    total = jnp.sum(got[...].astype(F32), axis=0)
    total_out[...] = total
    slow_count, fast_count = counts(total1[...], frames)
    slow_pair, fast_pair = get_narrow(total)
    slow_two, fast_two = get_narrow(total2[...])
    slow_one, fast_one = get_narrow(total1[...])
    mean, inverse = moments(slow_two, slow_count)
    upper = under(e2[...], h2[...], mean, inverse, slow2[0:1], slow_pair, slow_count, held)
    u2[...] = upper
    pad[...] = jnp.zeros_like(pad)
    fill(pad, upper.astype(F32))
    acc = None
    for tap in range(9):
        piece = low(tap_of(pad, 2 - tap // 3, 2 - tap % 3))
        copies[tap].wait()
        term = nn(piece, mixing[:, tap * CSM : (tap + 1) * CSM])
        acc = term if acc is None else acc + term
    mean, inverse = moments(slow_one, slow_count)
    scaled = (h1[...] - mean) * inverse
    down = acc * held * silu_grad(slow1[0:1] * scaled + slow1[1:2])
    e1[...] = down
    slow_out = sums(down, scaled)
    mean, inverse = moments(fast_two, fast_count)
    mean_one, inverse_one = moments(fast_one, fast_count)
    fast_pad[...] = jnp.zeros_like(fast_pad)
    act_pad[...] = jnp.zeros_like(act_pad)
    fast_out = None
    for frame in range(frames):
        upper = under(e5[frame], h5[frame], mean, inverse, fast2[0:1], fast_pair, fast_count, held)
        u5[frame] = upper
        scaled = (h4[frame] - mean_one) * inverse_one
        level = fast1[0:1] * scaled + fast1[1:2]
        fill(fast_pad, upper.astype(F32))
        fill(act_pad, low(silu(level) * held).astype(F32))
        turned = low(upper.astype(F32).T)
        acc = None
        for tap in range(9):
            down_by, right_by = (tap // 3, tap % 3)
            piece = low(tap_of(fast_pad, 2 - down_by, 2 - right_by))
            term = nt(piece, blending[tap])
            acc = term if acc is None else acc + term
            part = nn(turned, low(tap_of(act_pad, down_by, right_by)))
            blend_grad[tap] = part if frame == 0 else blend_grad[tap] + part
        down = acc * held * silu_grad(level)
        e4[frame] = down
        pair = sums(down, scaled)
        fast_out = pair if fast_out is None else tuple(a + b for a, b in zip(fast_out, pair))
    put_narrow(out, block, slow_out, fast_out)


def mixing_grad_kernel(acts, uppers, out, pad):
    count = acts.shape[0]
    pad[...] = jnp.zeros_like(pad)
    for place in range(count):
        fill(pad.at[place], acts[place].astype(F32))
    for tap in range(9):
        total = None
        for place in range(count):
            piece = low(tap_of(pad.at[place], tap // 3, tap % 3))
            term = dot(piece, uppers[place], ((0,), (0,)))
            total = term if total is None else total + term
        out[tap] = low(total)


def first_back_kernel(
    e1, e4, h1, h4, total1, got, slow1, fast1, mask, u1, u4, total_out
):
    held = mask[...]
    frames = h4.shape[0]
    total = jnp.sum(got[...].astype(F32), axis=0)
    total_out[...] = total
    slow_count, fast_count = counts(total1[...], frames)
    slow_pair, fast_pair = get_narrow(total)
    slow, fast = get_narrow(total1[...])
    mean, inverse = moments(slow, slow_count)
    u1[...] = under(e1[...], h1[...], mean, inverse, slow1[0:1], slow_pair, slow_count, held)
    mean, inverse = moments(fast, fast_count)
    for frame in range(frames):
        u4[frame] = under(
            e4[frame], h4[frame], mean, inverse, fast1[0:1], fast_pair, fast_count, held
        )


def by_frame(place, target, parts):
    target[0] = jnp.zeros_like(target[0])
    target[len(parts) + 1] = jnp.zeros_like(target[0])
    for k, part in enumerate(parts):
        target[jnp.bitwise_xor(place, k) + 1] = part


def turn(parts):
    own, across, others = parts
    return [own[...], others[0], across[...], others[1]]


def stem_grad_kernel(
    place, slow_up, fast_up, video, small, out_0, out_1, out_2, out_3, total
):
    total[0:CS, :] = dot(slow_up[...], video[0], ((0,), (0,)))
    fast = None
    for frame in range(fast_up.shape[0]):
        term = dot(fast_up[frame], video[frame], ((0,), (0,)))
        fast = term if fast is None else fast + term
    total[CS:, :] = fast
    size = total.shape[0] // 8
    for k, out in enumerate((out_0, out_1, out_2, out_3)):
        target = jnp.bitwise_xor(place[0], k)
        for b in range(8):
            start = pl.multiple_of(b * size + target * (size // 4), 8)
            rows = total[pl.ds(start, size // 4), :]
            out[b] = low(jnp.concatenate([rows, small[target, b]]))


def early_kernel(*refs):
    uppers, acts, out = refs[0:4], refs[4:7], refs[7]
    total = None
    for upper, act in zip(uppers, turn(acts)):
        term = dot(upper[...], act, ((0,), (0,)))
        total = term if total is None else total + term
    size = total.shape[0] // out.shape[0]
    for b in range(out.shape[0]):
        out[b] = low(total[b * size : (b + 1) * size])


def mixing_kernel(*refs):
    acts, uppers, restore, out, pad = refs[0:4], refs[4:7], refs[7], refs[8], refs[9]
    pad[...] = jnp.zeros_like(pad)
    for k, act in enumerate(acts):
        fill(pad.at[k], act[...].astype(F32))
    parts = turn(uppers)
    for tap in range(9):
        total = None
        for k, upper in enumerate(parts):
            term = dot(low(tap_of(pad.at[k], tap // 3, tap % 3)), upper, ((0,), (0,)))
            total = term if total is None else total + term
        if tap < 8:
            out[tap, 0:128, :] = low(total)
        else:
            for b in range(8):
                out[b, 128:144, :] = low(total[b * 16 : (b + 1) * 16])
    for b in range(8):
        out[b, 144:208, :] = restore[b]


def late_kernel(*refs):
    place, cells, sides, uppers = refs[0], refs[1:5], refs[5:8], refs[8:11]
    out, frames, side_total, side_rows = refs[11:15]
    here = place[0]
    by_frame(here, frames, [cell[...] for cell in cells])
    parts = turn(uppers)
    for tap in range(3):
        total = None
        for k, upper in enumerate(parts):
            cell = frames[jnp.bitwise_xor(here, k) + tap]
            term = dot(cell, upper, ((0,), (0,)))
            total = term if total is None else total + term
        for b in range(4):
            if tap < 2:
                out[tap * 4 + b, 0:128, :] = low(total[b * 128 : (b + 1) * 128])
            else:
                out[2 * b, 128:192, :] = low(total[b * 128 : b * 128 + 64])
                out[2 * b + 1, 128:192, :] = low(total[b * 128 + 64 : (b + 1) * 128])
    core = here % 2
    own, across, others = sides
    for tap in range(5):
        total = None
        turned = (own[tap], others[0, tap], across[tap], others[1, tap])
        for side, upper in zip(turned, parts):
            term = dot(side, upper, ((0,), (0,)))
            total = term if total is None else total + term
        side_total[...] = total
        side_rows[tap * 64 : (tap + 1) * 64, :] = side_total[
            pl.ds(pl.multiple_of(core * 64, 64), 64), :
        ]
    blank = jnp.zeros((8, CSM), F32)
    for b in range(8):
        rows = jnp.concatenate([side_rows[b * 40 : (b + 1) * 40, :], blank])
        out[b, 192:240, :] = low(rows)


def stem_back_kernel(near, place, *refs):
    u1_held = refs[0:3] if near else refs[0]
    (
        u4, u4_before, u4_after, weights, squeeze, d3, d6, slow_pre, fast_pre,
        mask, slow_up, fast_up, first, frames_held, flags,
    ) = refs[-15:]
    spans = [(CONDENSE_AT + k * CS, 5 * CF + k * CS, CS) for k in range(3)]
    copies = fetch(weights, first, flags, spans + [(SIDE_AT, 0, 5 * CF)])
    held = mask[...]
    frames = fast_up.shape[0]
    total = d3[...]
    if near:
        by_frame(place[0], frames_held, turn(u1_held))
        source = frames_held
    else:
        source = u1_held
    u1_before, u1, u1_after = [source[place[0] + k] for k in range(3)]
    for tap, piece in enumerate((u1_after, u1, u1_before)):
        start = 5 * CF + tap * CS
        copies[tap].wait()
        total = total + nn(piece, first[:, start : start + CS])
    copies[3].wait()
    slow_up[...] = low(total * held * silu_grad(slow_pre[...]))
    for frame in range(frames):
        total = d6[frame]
        pairs = [(frame + 2, u1)] if frame < 3 else []
        pairs = pairs + ([(frame - 2, u1_after)] if frame >= 2 else [])
        for tap, piece in pairs:
            total = total + nn(piece, first[:, tap * CF : (tap + 1) * CF])
        for tap in range(3):
            place = frame + 1 - tap
            if place < 0:
                piece = u4_before[...]
            elif place >= frames:
                piece = u4_after[...]
            else:
                piece = u4[place]
            total = total + nn(piece, squeeze[:, tap * CF : (tap + 1) * CF])
        fast_up[frame] = low(total * held * silu_grad(fast_pre[frame]))


def product(left, right):
    left_high = low(left)
    right_high = low(right)
    if left.shape[0] >= CSM:
        return nn(left_high, right_high)
    left_rest = low(left - left_high.astype(F32))
    right_rest = low(right - right_high.astype(F32))
    return nn(left_high, right_high) + (nn(left_high, right_rest) + nn(left_rest, right_high))


def shape_kernel(*refs):
    half = len(refs) // 2
    grams = []
    eyes = []
    scales = []
    totals = []
    for source in refs[:half]:
        size = source.shape[0]
        gram = source[...]
        rows = lax.broadcasted_iota(jnp.int32, (size, size), 0)
        columns = lax.broadcasted_iota(jnp.int32, (size, size), 1)
        eye = (rows == columns).astype(F32)
        diagonal = jnp.sum(gram * eye, axis=1, keepdims=True)
        diagonal = jnp.sum(diagonal, axis=0, keepdims=True)
        scale = 1.0 / (jnp.sqrt(diagonal) + 1e-07)
        grams.append(gram * (scale * scale))
        eyes.append(eye)
        scales.append(scale)
    for step in range(NS_STEPS):
        extras = [NS_SECOND * gram + NS_THIRD * product(gram, gram) for gram in grams]
        if step == 0:
            totals = [NS_FIRST * eye + extra for eye, extra in zip(eyes, extras)]
        else:
            totals = [
                NS_FIRST * total + product(extra, total) for total, extra in zip(totals, extras)
            ]
        if step + 1 < NS_STEPS:
            middles = [NS_FIRST * g + product(extra, g) for g, extra in zip(grams, extras)]
            grams = [NS_FIRST * m + product(extra, m) for m, extra in zip(middles, extras)]
    for target, total, scale in zip(refs[half:], totals, scales):
        target[...] = (total * scale).astype(target.dtype)


def block_shape_kernel(whole, *refs):
    small, outs = refs[0:3], refs[3:8]
    gram, stem = refs[8:10]
    for b in range(8):
        gram[b * 64 : (b + 1) * 64, :] = whole[b, 0:64, :].astype(F32)
        rows = whole[b, 64:80, :].astype(F32)
        stem[b * 24 : b * 24 + 16, :] = rows[:, 0:192]
        stem[b * 24 + 16 : b * 24 + 24, :] = rows[0:8, 256:448]
    shape_kernel(gram, stem, *small, *outs)


def gram_kernel(
    place, factor, speed, restore_speed, own, got, stem_speed, stem_grad, one, two, stem_out,
    keep, give, stem_gram, wide, tall, held,
):
    x = place[0] // 2
    core = place[0] % 2
    scale = factor[...]
    for spot, part in ((x, own), (1 - x, got)):
        held[pl.ds(pl.multiple_of(spot * 128, 128), 128), :] = part[0:128, :].astype(F32)
        held[pl.ds(pl.multiple_of(spot * 64 + 256, 64), 64), :] = part[128:192, :].astype(F32)
        held[pl.ds(pl.multiple_of(spot * 64 + 384, 64), 64), :] = part[192:256, :].astype(F32)
    speeds = jnp.concatenate([speed[b, 0:64, :].astype(F32) for b in range(8)]).T
    grads = held[...]
    speed_two = jnp.where(x == 0, restore_speed[...].astype(F32), speeds[384:512])
    moved_one = low(MUON_KEEP * speeds[0:384] + grads[0:384] * scale)
    moved_two = low(MUON_KEEP * speed_two + grads[384:512] * scale)
    one[...] = moved_one
    two[...] = moved_two
    gram_one = low(dot(moved_one, moved_one, ((0,), (0,))))
    gram_two = low(dot(moved_two, moved_two, ((0,), (0,))))
    keep[...] = jnp.where(core == 0, gram_one, gram_two)
    give[...] = jnp.where(core == 0, gram_two, gram_one)
    moved = low(MUON_KEEP * stem_speed[...] + stem_grad[...].astype(F32) * scale)
    stem_out[...] = moved
    gram = dot(moved, moved, ((0,), (0,)))
    stem_gram[...] = jnp.zeros_like(stem_gram)
    blank = jnp.zeros((8, 192), F32)
    for b in range(8):
        stem_gram[b, :, 0:192] = low(gram[b * 24 : b * 24 + 16])
        rest = jnp.concatenate([gram[b * 24 + 16 : b * 24 + 24], blank])
        stem_gram[b, :, 256:448] = low(rest)
    turned = low(grads.T)
    for b in range(8):
        wide[b] = turned[b * 64 : (b + 1) * 64]
    put_tall(tall, low(grads[384:512]))


def put_tall(out, values):
    for k in range(4):
        for h in range(2):
            out[2 * k + h] = values[h * 64 : (h + 1) * 64, k * 128 : (k + 1) * 128]


def ortho_kernel(place, shaped, other, one, two, wide, tall):
    core = place[0] % 2
    shape_one = jnp.where(core == 0, shaped[...], other[...])
    shape_two = jnp.where(core == 0, other[...], shaped[...])
    first = low(nt(shape_one, one[...]))
    second = low(nt(shape_two, two[...]))
    for b in range(8):
        wide[b, :, 0:384] = first[b * 64 : (b + 1) * 64]
        wide[b, :, 384:512] = second[b * 64 : (b + 1) * 64]
    put_tall(tall, low(nn(two[...], shape_two)))


def shape_of(grams):
    return call(shape_kernel, [(item.shape, F32) for item in grams], grams, micros=13)


def carry(base, value, ratio, factor):
    return MUON_KEEP * base + value * factor


def renew(base, value, ratio, factor):
    return base - MUON_RATE * (value * ratio + WEIGHT_DECAY * base)


def selection(count, far, depth, size, x, width, target):
    column = lax.broadcasted_iota(jnp.int32, (count * far * depth, 1), 0)
    place = lax.rem(column, depth)
    block = lax.div(column, depth)
    goal = target(lax.div(block, far), place)
    goal = jnp.where((place < size) & (lax.rem(block, far) == x), goal, -1)
    columns = lax.broadcasted_iota(jnp.int32, (count * far * depth, width), 1)
    return low((goal == columns).astype(F32))


def place_kernel(
    rule, far, main_rows, depth, place, factor, own, across, others, lateral, condense, mixing,
    restore, lateral_out, condense_out, mixing_out, restore_out, frames,
):
    for k, part in enumerate((own[...], others[0], across[...], others[1])):
        frames[jnp.bitwise_xor(place[0], k)] = part
    half_one, half_two = [
        [frames.at[2 * target + c] for target in range(far)] for c in range(2)
    ]
    halves = (half_one, half_two)
    batch_count, out_rows, lanes_all = own.shape
    edge = far * main_rows
    stop = far * depth
    scale = factor[...]

    def put(out, base, spot, values):
        lanes = slice(spot, spot + values.shape[1])
        out[:, lanes] = rule(base[:, lanes], values.astype(F32), 1.0, scale)
        return spot + values.shape[1]

    devices = 2 * far
    rest_depth = depth - main_rows
    for target, out, base, main_taps in ((0, condense_out, condense, 2), (1, mixing_out, mixing, 8)):
        share = batch_count // main_taps
        spot = 0
        for tap in range(main_taps):
            for device in range(devices):
                lanes = slice(device // 2 * main_rows, (device // 2 + 1) * main_rows)
                for k in range(tap * share, (tap + 1) * share):
                    spot = put(out, base, spot, halves[device % 2][target][k, :, lanes])
        size = (out.shape[1] - spot) // (batch_count * devices)
        rests = [
            jnp.concatenate([half[target][k, :, edge:stop] for k in range(batch_count)], axis=1)
            for half in halves
        ]
        for x in range(far):
            chosen = selection(
                batch_count, far, rest_depth, size, x, batch_count * size,
                lambda k, r: k * size + r,
            )
            for rest in rests:
                spot = put(out, base, spot, nn(rest, chosen))
    side_depth = (lanes_all - stop) // far
    side_size = lateral.shape[1] // (batch_count * devices)
    channels = CF // devices
    sides = [
        jnp.concatenate([half[1][k, :, stop:] for k in range(batch_count)], axis=1)
        for half in halves
    ]
    for x in range(far):
        total = None
        for c, side in enumerate(sides):

            def goal(k, r):
                row = k * side_size + r
                return lax.div(row, channels) * 2 * channels + c * channels + lax.rem(row, channels)

            chosen = selection(
                batch_count, far, side_depth, side_size, x, 10 * channels, goal
            )
            term = nn(side, chosen)
            total = term if total is None else total + term
        for tap in range(5):
            put(
                lateral_out, lateral, tap * CF + 2 * x * channels,
                total[:, tap * 2 * channels : (tap + 1) * 2 * channels],
            )
    width = lanes_all - stop
    ratio = math.sqrt(max(1.0, restore.shape[0] * batch_count / restore.shape[1]))
    for c, half in enumerate(halves):
        for k in range(batch_count * out_rows // width):
            for h in range(far):
                start = (2 * h + c) * out_rows
                rows = slice(start, start + out_rows)
                lanes = slice(k * width, (k + 1) * width)
                values = half[0][k * width // out_rows + h, :, stop:].astype(F32)
                restore_out[rows, lanes] = rule(restore[rows, lanes], values, ratio, scale)


def adam(weight, moment, square, grad, rate, decay):
    moment = ADAM_ONE * moment + (1.0 - ADAM_ONE) * grad
    square = ADAM_TWO * square + (1.0 - ADAM_TWO) * grad * grad
    fixed_one = 1.0 - ADAM_ONE**STEP
    fixed_two = 1.0 - ADAM_TWO**STEP
    weight = weight - rate * (
        moment / fixed_one / (jnp.sqrt(square / fixed_two) + ADAM_EPS) + decay * weight
    )
    return (weight, moment, square)


def per_device(
    video,
    video_ids,
    crop_scales,
    labels,
    valid_clips,
    stem_weight,
    lateral_weight,
    condense,
    mixing,
    restore,
    squeeze,
    blending,
    recover,
    head_weight,
    stem_velocity,
    lateral_velocity,
    condense_velocity,
    mixing_velocity,
    restore_velocity,
    squeeze_velocity,
    blending_velocity,
    recover_velocity,
    head_moment,
    head_square,
    affine,
    affine_moment,
    affine_square,
):
    tm_count = lax.axis_size("tm")
    batch_count = lax.axis_size("batch")
    devices = tm_count * batch_count
    far = tm_count // 2
    tm_place = lax.axis_index("tm")
    batch_place = lax.axis_index("batch")
    core = tm_place % 2
    both = ("tm", "batch")

    clips, frames, height = video.shape[0:3]
    spots = height * height
    rows = spots * clips

    def quarter(block):
        part = block.shape[0] // tm_count
        return lax.dynamic_slice_in_dim(block, tm_place * part, part, axis=0)

    def gather(block):
        return lax.all_gather(quarter(block), ("batch", "tm"), axis=0, tiled=True)

    def by_place(items, place):
        whole = jnp.zeros((len(items),) + items[0].shape, items[0].dtype)
        for k, item in enumerate(items):
            whole = lax.dynamic_update_index_in_dim(whole, item, place ^ k, 0)
        return whole

    def over_tm(block):
        held = by_place(
            [block] + [swap(block, "tm", 2 * k) for k in range(1, far)], tm_place // 2
        )
        held = by_place([held, swap(held, "tm", 1)], core)
        return jnp.swapaxes(held, 0, 1).reshape((tm_count,) + block.shape)

    def gather_steps(block):
        held = spread_all(block, ("batch",))
        held = held.reshape(batch_count, -1, block.shape[1])
        held = jnp.swapaxes(over_tm(held), 0, 1)
        return held.reshape(-1, block.shape[1])

    out_rows = condense.shape[0]
    small_rows = squeeze.shape[0]
    weights_low = jnp.concatenate(
        [mixing, lateral_weight, condense]
        + [restore[k * out_rows : (k + 1) * out_rows] for k in range(4)],
        axis=1,
    )
    weights_low = quarter(weights_low).astype(BF16)
    stem_low = quarter(stem_weight).astype(BF16)
    weights_low, stem_low, video = lax.optimization_barrier((weights_low, stem_low, video))
    weights_full = lax.all_gather(weights_low, ("batch", "tm"), axis=0, tiled=True)
    stem_full = gather_steps(stem_low)
    small = jnp.concatenate(
        [squeeze, blending, recover.reshape(small_rows, -1)], axis=1
    ).astype(BF16)
    small_full = spread_all(small, ("batch",)).reshape(CFM, -1)
    squeeze_full = small_full[:, 0 : 3 * CF]
    blending_full = small_full[:, 3 * CF : 3 * CF + 9 * CFM]
    recover_full = small_full[:, 3 * CF + 9 * CFM :].reshape(CF, CFM)
    head_full = gather(head_weight.astype(BF16))

    own_video = jnp.transpose(video, (1, 2, 3, 0, 4)).reshape(frames, rows, -1)
    before = shift(
        jnp.concatenate([own_video[0:1], own_video[frames - 2 :]], axis=0), "tm", 1
    )
    after = shift(own_video[0:1], "tm", -1)
    slow_video = jnp.concatenate([before[0:1], own_video[0:1], after], axis=0)
    fast_video = jnp.concatenate([before[1:], own_video, after], axis=0)

    side = (height - crop_scales).astype(F32)
    places = jnp.arange(height).astype(F32)
    inside = (places[:, None] < side[None, :]).astype(F32)
    mask = (inside[:, None, :] * inside[None, :, :]).reshape(rows, 1)
    area = (side * side)[:, None]
    gains, shifts, class_bias = split_affine(affine)
    par = [jnp.stack([gain, shift]) for gain, shift in zip(gains, shifts)]
    valid = valid_clips.astype(F32)[:, None]
    blend_taps = jnp.transpose(blending_full.reshape(CFM, 9, CFM), (1, 2, 0))
    narrow = ((devices, 8, 256), F32)
    narrow_low = ((devices, 8, 256), BF16)
    total_narrow = ((8, 256), F32)
    wide = ((8, 640), F32)

    def exchange(copies):
        return lax.all_to_all(copies, both, 0, 0, tiled=True)

    def exchange_wide(block):
        return spread_all(block, both).reshape((devices,) + block.shape)

    slow_shape = (rows, CSM)
    fast_shape = (frames, rows, CFM)
    slow_wide = (rows, CS)
    fast_wide = (frames, rows, CF)
    first_shape = ((CSM, 5 * CF + 3 * CS), BF16)
    mixing_shape = ((CSM, 9 * CSM), BF16)
    restore_shape = ((CS, CSM), BF16)
    pad_shape = ((height + 2, height + 2, clips, CSM), F32)
    fast_pad = ((height + 2, height + 2, clips, CFM), F32)

    pieces = batch_count * far
    main_rows = 2048 // pieces
    mixing_rows = 9 * CSM // 2 // pieces
    condense_rows = 3 * CS // 2 // pieces
    far_place = tm_place // 2
    depth_one = condense_rows
    depth_two = CS // 2 // pieces

    def share_of(item, taps, place):
        width = item.shape[1] // taps
        size = width // tm_count
        return jnp.concatenate(
            [
                lax.dynamic_slice_in_dim(item, tap * width + place * size, size, axis=1)
                for tap in range(taps)
            ],
            axis=1,
        ).astype(BF16)

    def sent_columns(item, taps, parts):
        held = []
        start = 0
        shares = [share_of(item, taps, 2 * k + core) for k in range(far)]
        for size, depth in parts:
            for share in shares:
                block = share[:, start : start + size * batch_count]
                block = block.reshape(out_rows, batch_count, size)
                held.append(jnp.pad(block, ((0, 0), (0, 0), (0, depth - size))))
            start = start + size * batch_count
        return jnp.transpose(jnp.concatenate(held, axis=-1), (1, 0, 2))

    lateral_rows = 5 * CF // tm_count // batch_count
    rest_depth = depth_one - main_rows
    speed_send = jnp.concatenate(
        [
            jnp.where(
                far_place == 0,
                sent_columns(
                    condense_velocity, 3, ((main_rows, main_rows), (rest_depth, rest_depth))
                ),
                sent_columns(
                    mixing_velocity,
                    9,
                    ((main_rows, main_rows), (mixing_rows - main_rows, rest_depth)),
                ),
            ),
            sent_columns(lateral_velocity, 5, ((lateral_rows, depth_two),)),
        ],
        axis=-1,
    )
    small_speed = jnp.concatenate(
        [squeeze_velocity, blending_velocity, recover_velocity.reshape(small_rows, -1)], axis=1
    )
    small_speed = small_speed.astype(BF16).reshape(-1, speed_send.shape[-1])
    small_speed = jnp.broadcast_to(small_speed[None], (batch_count,) + small_speed.shape)
    speed_send = jnp.concatenate([speed_send, small_speed], axis=1)
    speed_send, small_full = lax.optimization_barrier((speed_send, small_full))
    speed = lax.all_to_all(speed_send, "batch", 0, 0, tiled=True)

    near = tm_count == 4 and batch_count == 8
    place_cell = tm_place.astype(jnp.int32).reshape(1)
    quarter_shape = (rows, CS // tm_count)
    slow_pre, fast_pre, slow_low, fast_low, *shares = call(
        functools.partial(stem_kernel, near),
        [
            (slow_wide, F32),
            (fast_wide, F32),
            ((3, rows, CS), BF16),
            ((frames + 3, rows, CF), BF16),
        ]
        + (
            [(quarter_shape, BF16)] * 4 + [((5, rows, 128), BF16)] * 2
            if near
            else [((tm_count,) + quarter_shape, BF16)]
        ),
        [place_cell, slow_video, fast_video, stem_full, mask],
        scalars=(0,),
    )
    def in_turn(items, margin=0):
        whole = jnp.zeros((len(items) + 2 * margin,) + items[0].shape, items[0].dtype)
        for k, item in enumerate(items):
            whole = lax.dynamic_update_index_in_dim(whole, item, (tm_place ^ k) + margin, 0)
        return whole

    def share_out(parts, margin=0):
        items = [pick(parts, 0, tm_place)]
        items += [swap(pick(parts, 0, tm_place ^ k), "tm", k) for k in range(1, tm_count)]
        return in_turn(items, margin)

    def every(block, margin=0):
        even = [block] + [swap(block, "tm", 2 * k) for k in range(1, far)]
        odd = swap(jnp.stack(even), "tm", 1)
        items = [item for k in range(far) for item in (even[k], odd[k])]
        return in_turn(items, margin)

    def by_share(block, outer):
        parts = block.reshape(block.shape[0], outer, tm_count, -1)
        return jnp.moveaxis(parts, 2, 0).reshape(tm_count, block.shape[0], -1)

    def swaps(parts):
        return [parts[0]] + [swap(parts[k], "tm", k) for k in range(1, tm_count)]

    def pairs_of(own, given):
        across = swap(given, "tm", 2)
        return [own, across, swap(jnp.stack([own, across]), "tm", 1)]

    if near:
        slow_shares = swaps(shares[0:4])
        side_shares = pairs_of(shares[4], shares[5])
    else:
        sides = jnp.transpose(fast_low[0:5], (1, 0, 2)).reshape(rows, 5 * CF)
        slow_shares = share_out(shares[0], 1)
        side_shares = share_out(by_share(sides, 5))
    slow_low, speed = lax.optimization_barrier((slow_low, speed))
    h1, h4, sent = call(
        first_kernel,
        [(slow_shape, F32), (fast_shape, F32), narrow],
        [slow_low, fast_low, weights_full, squeeze_full, mask, valid],
        [total_narrow, first_shape],
        far=(2,),
        copies=4,
    )
    act_width = CSM // tm_count
    act_shapes = [((rows, 128), BF16)] * 4 if near else [(slow_shape, BF16)]
    h2, h5, total1, sent, *acts = call(
        functools.partial(second_kernel, near),
        [(slow_shape, F32), (fast_shape, F32), total_narrow, narrow] + act_shapes,
        [place_cell, h1, h4, exchange(sent), par[0], par[3], mask, weights_full, blend_taps],
        [pad_shape, fast_pad, total_narrow, mixing_shape],
        far=(7,),
        copies=9,
        scalars=(0,),
    )
    acts = swaps(acts) if near else share_out(by_share(acts[0], 1))
    a2, a5, h3, h6, total2, sent = call(
        third_kernel,
        [
            (slow_shape, BF16),
            (fast_shape, BF16),
            (slow_wide, F32),
            (fast_wide, F32),
            total_narrow,
            wide,
        ],
        [h2, h5, total1, exchange(sent), par[1], par[4], mask, weights_full, recover_full],
        [restore_shape],
        far=(7,),
        copies=4 * batch_count,
    )
    a2_every = pairs_of(a2, a2) if near else every(a2)
    if near:
        h3, slow_shares[1], slow_shares[3] = lax.optimization_barrier(
            (h3, slow_shares[1], slow_shares[3])
        )
    else:
        h3, slow_shares, side_shares = lax.optimization_barrier((h3, slow_shares, side_shares))
    pool, total3 = call(
        pool_kernel,
        [((clips, CS + CF), F32), wide],
        [h3, h6, slow_pre, fast_pre, total1, exchange_wide(sent), par[2], par[5], mask],
    )
    if near:
        pools = jnp.stack([pool] + [swap(pool, "tm", k) for k in range(1, tm_count)])
    else:
        pools = spread_all(pool, ("tm",)).reshape(tm_count, clips, CS + CF)
    if near:
        pools, slow_shares[2] = lax.optimization_barrier((pools, slow_shares[2]))
    feature_low, logit_low, d3, d6, sent = call(
        head_kernel,
        [((clips, CS + CF), BF16), ((clips, CLS), BF16), (slow_wide, F32), (fast_wide, F32), wide],
        [
            pools,
            head_full,
            class_bias[None],
            video_ids[:, None],
            video_ids[None],
            labels[:, None],
            valid,
            area,
            h3,
            h6,
            slow_pre,
            fast_pre,
            total1,
            total3,
            par[2],
            par[5],
            mask,
        ],
    )
    d3, acts, a2_every, side_shares = lax.optimization_barrier((d3, acts, a2_every, side_shares))
    u6, e2, e5, back3, sent, *u3 = call(
        functools.partial(third_back_kernel, near),
        [
            (fast_wide, BF16),
            (slow_shape, F32),
            (fast_shape, F32),
            wide,
            narrow_low,
        ]
        + ([(quarter_shape, BF16)] * 4 if near else [(slow_wide, BF16)]),
        [
            place_cell,
            d3,
            d6,
            h3,
            h6,
            h2,
            h5,
            total1,
            total3,
            total2,
            exchange_wide(low(sent)),
            par[2],
            par[5],
            par[1],
            par[4],
            mask,
            weights_full,
            recover_full,
        ],
        [total_narrow, restore_shape],
        far=(16,),
        copies=4 * batch_count,
        scalars=(0,),
    )
    if near:
        (restore_grad,) = call(
            early_kernel,
            [((batch_count, CS // tm_count // batch_count, CSM), BF16)],
            [*swaps(u3), *a2_every],
        )
    else:
        u3_shares = share_out(by_share(u3[0], batch_count))
        restore_grad = low(dot(u3_shares, a2_every, ((0, 1), (0, 1))))
    recover_grad = over_rows(a5.reshape(frames * rows, CFM), u6.reshape(frames * rows, CF))

    u2, u5, e1, e4, blend_grad, back2, sent = call(
        second_back_kernel,
        [
            (slow_shape, BF16),
            (fast_shape, BF16),
            (slow_shape, F32),
            (fast_shape, F32),
            ((9, CFM, CFM), F32),
            total_narrow,
            narrow_low,
        ],
        [
            e2,
            e5,
            h2,
            h5,
            h1,
            h4,
            total2,
            total1,
            exchange(sent),
            par[1],
            par[4],
            par[0],
            par[3],
            mask,
            weights_full,
            blend_taps,
        ],
        [pad_shape, fast_pad, fast_pad, total_narrow, mixing_shape],
        far=(14,),
        copies=9,
    )
    blending_grad = jnp.transpose(blend_grad, (1, 0, 2)).reshape(CFM, 9 * CFM)

    def by_batch(parts):
        return jnp.concatenate(
            [part.reshape(batch_count, -1, part.shape[-1]) for part in parts], axis=1
        )

    def over_batch(view):
        got = lax.all_to_all(view, "batch", 0, 0, tiled=True)
        return jnp.sum(got.reshape(view.shape).astype(F32), axis=0)

    if near:
        (early,) = call(
            mixing_kernel,
            [((batch_count, 208, CSM), BF16)],
            [*acts, *pairs_of(u2, u2), restore_grad],
            [((tm_count, height + 2, height + 2, clips, act_width), F32)],
        )
    else:
        (mixing_grad,) = call(
            mixing_grad_kernel,
            [((9, act_width, CSM), BF16)],
            [acts, every(u2)],
            [((tm_count, height + 2, height + 2, clips, act_width), F32)],
        )
        mixing_grad = mixing_grad.reshape(9 * act_width, CSM)
        main_edge = 8 * act_width
        early = by_batch([mixing_grad[0:main_edge], mixing_grad[main_edge:], restore_grad])
    early, e1 = lax.optimization_barrier((early, e1))
    early = over_batch(early)

    u1, u4, back1 = call(
        first_back_kernel,
        [(slow_shape, BF16), (fast_shape, BF16), total_narrow],
        [e1, e4, h1, h4, total1, exchange(sent), par[0], par[3], mask],
    )
    if near:
        u1_parts = pairs_of(u1, u1)
        u1_held = u1_parts
    else:
        u1_held = every(u1, 1)
    squeeze_grad = jnp.concatenate(
        [dot(u4, fast_low[1 + k : 1 + k + frames], ((0, 1), (0, 1))) for k in range(3)], axis=1
    )
    slow_up, fast_up = call(
        functools.partial(stem_back_kernel, near),
        [(slow_wide, BF16), (fast_wide, BF16)],
        [
            place_cell,
            *(u1_held if near else [u1_held]),
            u4,
            shift(u4[frames - 1], "tm", 1),
            shift(u4[0], "tm", -1),
            weights_full,
            squeeze_full,
            d3,
            d6,
            slow_pre,
            fast_pre,
            mask,
        ],
        [first_shape, ((6,) + slow_shape, BF16)],
        far=(7 if near else 5,),
        copies=4,
        scalars=(0,),
    )
    slow_up, fast_up, u1_held = lax.optimization_barrier((slow_up, fast_up, u1_held))
    if near:
        (late,) = call(
            late_kernel,
            [((batch_count, 240, CSM), BF16)],
            [place_cell, *slow_shares, *side_shares, *u1_held],
            [((6,) + quarter_shape, BF16), ((128, CSM), F32), ((320, CSM), F32)],
            scalars=(0,),
        )
    else:
        u1_inner = u1_held[1 : tm_count + 1]
        cells = ((0, 1), (0, 1))
        condense_grad = [
            low(dot(slow_shares[k : k + tm_count], u1_inner, cells)) for k in range(3)
        ]
        lateral_grad = low(dot(side_shares, u1_inner, cells))
        late = by_batch(
            [jnp.concatenate(condense_grad[0:2]), condense_grad[2], lateral_grad]
        )
    late, early = lax.optimization_barrier((late, early))
    late = over_batch(late)
    clip_count = total1[7, 0] / tm_count
    loss_total = (back3[4, 512] + back3[5, 512] + back3[6, 512]) / tm_count
    slow_back3, fast_back3 = get_wide(back3)
    slow_back2, fast_back2 = get_narrow(back2)
    slow_back1, fast_back1 = get_narrow(back1)
    (b1, g1), (b2, g2), (b3, g3) = [
        [item[0] for item in pair] for pair in (slow_back1, slow_back2, slow_back3)
    ]
    (b4, g4), (b5, g5), (b6, g6) = [
        [item[0] for item in pair] for pair in (fast_back1, fast_back2, fast_back3)
    ]

    main_rows = 2048 // pieces
    mixing_rows = 9 * CSM // 2 // pieces
    condense_rows = 3 * CS // 2 // pieces
    tm_all = bits("tm", 0)
    columns_wide = stem_weight.shape[-1]

    def blocks(item):
        item = jnp.pad(item, ((0, 0), (0, -item.shape[1] % columns_wide)))
        item = item.reshape(batch_count, small_rows, -1, columns_wide)
        return jnp.swapaxes(item, 1, 2)

    small_view = [blocks(item) for item in (squeeze_grad, blending_grad, recover_grad)]
    small_view = jnp.concatenate(small_view, axis=1)
    small_blocks = small_view.shape[1]
    head_rows = head_weight.shape[0]
    feature_parts = jnp.transpose(feature_low.reshape(clips, batch_count, head_rows), (1, 0, 2))
    logit_parts = jnp.broadcast_to(logit_low.reshape(1, -1), (batch_count, clips * CLS))
    riders = jnp.concatenate([feature_parts.reshape(batch_count, -1), logit_parts], axis=1)
    riders = jnp.pad(riders, ((0, 0), (0, -riders.shape[1] % columns_wide)))
    riders = riders.reshape(batch_count, -1, columns_wide)
    if near:
        small_tm = small_view.reshape(batch_count, tm_count, -1, columns_wide)
        small_part = small_tm.shape[2]
        small_tm = jnp.pad(jnp.swapaxes(small_tm, 0, 1), ((0, 0), (0, 0), (0, 6), (0, 0)))
        share_shape = (batch_count, stem_weight.shape[0] // tm_count + 24, columns_wide)
        stem_shares = call(
            stem_grad_kernel,
            [(share_shape, BF16)] * 4,
            [place_cell, slow_up, fast_up, own_video, small_tm],
            [((CS + CF, columns_wide), F32)],
            scalars=(0,),
        )
        stem_shares = swaps(stem_shares)
        stem_shares = low(sum(share.astype(F32) for share in stem_shares))
        riders = jnp.concatenate([stem_shares, riders], axis=1)
        got = [pick(riders, 0, batch_place)] + [
            swap(pick(riders, 0, batch_place ^ k), "batch", k) for k in range(1, batch_count)
        ]
        shards_sum = sum(item[0 : share_shape[1]].astype(F32) for item in got)
        stem_part = share_shape[1] - 24
        stem_shard, small_shard = shards_sum[0:stem_part], shards_sum[stem_part:]
        riders = jnp.stack([item[share_shape[1] :] for item in got])
        riders = riders.reshape(batch_count, -1)
    else:
        stem_grad = jnp.concatenate(
            [over_rows(slow_up, own_video[0]), dot(fast_up, own_video, ((0, 1), (0, 1)))], axis=0
        )
        stem_view = stem_grad.reshape((batch_count,) + (2,) * len(tm_all) + (-1, stem_grad.shape[-1]))
        small_view = small_view.reshape(-1, columns_wide)
        live = list(tm_all)
        for axis, bit in tm_all[::-1]:
            dim = 1 + live.index((axis, bit))
            flag = (tm_place >> bit) & 1
            keep, give = pick(stem_view, dim, flag), pick(stem_view, dim, 1 - flag)
            flat_give = give.reshape(-1, columns_wide)
            count = flat_give.shape[0]
            sent = jnp.concatenate([flat_give, small_view]).astype(BF16)
            sent = lax.optimization_barrier(sent)
            got = swap(sent, axis, 1 << bit)
            stem_view = keep + got[0:count].astype(F32).reshape(keep.shape)
            small_view = sent[count:].astype(F32) + got[count:].astype(F32)
            live.remove((axis, bit))
        small_view = small_view.reshape(batch_count, -1, columns_wide)
        stem_part = stem_view.shape[1]
        late, riders = lax.optimization_barrier((late, riders))
        riders = jnp.concatenate([stem_view.astype(BF16), small_view.astype(BF16), riders], axis=1)
        got = lax.all_to_all(riders, "batch", 0, 0, tiled=True).reshape(batch_count, -1, columns_wide)
        both_parts = stem_part + small_view.shape[1]
        shards_sum = jnp.sum(got[:, 0:both_parts].astype(F32), axis=0)
        stem_shard, small_shard = shards_sum[0:stem_part], shards_sum[stem_part:]
        riders = got[:, both_parts:].reshape(batch_count, -1)
    feature_size = clips * head_rows
    feature_all = riders[:, 0:feature_size].reshape(batch_count * clips, head_rows)
    logit_all = riders[:, feature_size : feature_size + clips * CLS]
    logit_all = logit_all.reshape(batch_count * clips, CLS)
    mixing_shard, restore_shard = early[0:mixing_rows], early[mixing_rows:]
    condense_shard = late[0:condense_rows]
    lateral_shard = late[condense_rows : condense_rows + lateral_rows]
    head_grad = over_rows(feature_all, logit_all)
    class_grad = jnp.sum(logit_all.astype(F32), axis=0)
    affine_grad = jnp.concatenate([g1, g2, g3, g4, g5, g6, b1, b2, b3, b4, b5, b6, class_grad])

    small_speed = jnp.concatenate(
        [squeeze_velocity, blending_velocity, recover_velocity.reshape(small_rows, -1)], axis=1
    )
    small_speed = spread_all(small_speed.astype(BF16), ("batch",)).reshape(CFM, -1)

    leader = (tm_place == 0).astype(F32)
    squares = sum(jnp.sum(item * item) for item in (late, early, stem_shard))
    small_share = 1.0 if near else leader
    squares = squares + small_share * jnp.sum(small_shard * small_shard)
    squares = squares + leader * jnp.sum(head_grad * head_grad)
    first_device = leader * (batch_place == 0).astype(F32)
    squares = squares + first_device * jnp.sum(affine_grad * affine_grad)
    (total_squares,) = all_sum([squares], both)
    grad_norm = jnp.sqrt(total_squares) / clip_count
    factor = jnp.minimum(1.0, CLIP_AT / grad_norm) / clip_count

    small_speed = speed[:, out_rows:].reshape(CFM, -1)
    stem_rows = stem_weight.shape[0]
    if near:
        held = over_tm(low(shards_sum))
        stem_own = held[:, 0:stem_part].reshape(stem_rows, -1)
        small_shard = held[:, stem_part : stem_part + small_part].reshape(-1, columns_wide)
    else:
        stem_own = over_tm(low(stem_shard)).reshape(stem_rows, -1)

    def small_parts(small_whole):
        small_whole = small_whole.reshape(batch_count, small_blocks, small_rows, columns_wide)
        small_whole = jnp.swapaxes(small_whole, 1, 2).reshape(CFM, -1)
        small_grads = unpack(small_whole[:, 0 : 3 * CF + 9 * CFM + CF])
        speeds = unpack(small_speed)
        speeds = (speeds[0], speeds[1], speeds[2].reshape(CF, CFM).T)
        items = [
            low(MUON_KEEP * held.astype(F32) + grad.astype(F32) * factor)
            for held, grad in zip(speeds, small_grads)
        ]
        return small_grads, items

    def unpack(values):
        first = values[:, 0 : 3 * CF]
        second = values[:, 3 * CF : 3 * CF + 9 * CFM]
        return (first, second, values[:, 3 * CF + 9 * CFM :])

    def ratio_of(base):
        return math.sqrt(max(1.0, base.shape[0] * batch_count / base.shape[1]))

    def own(values, part):
        return lax.dynamic_slice_in_dim(values, batch_place * part, part, axis=0)

    def direct_orthos(stem_moved, shapes, items):
        tall_part = recover.shape[0]
        results = (
            rows_by_columns(stem_moved, shapes[0]),
            rows_by_columns(own(shapes[1], small_rows), items[0]),
            rows_by_columns(own(shapes[2], small_rows), items[1]),
            rows_by_columns(own(items[2].T, tall_part), shapes[3]),
        )
        return [low(result) for result in results]

    far_place = tm_place // 2
    factor_cell = factor.reshape(1, 1)
    bases = {
        carry: (lateral_velocity, condense_velocity, mixing_velocity, restore_velocity),
        renew: (lateral_weight, condense, mixing, restore),
    }

    def deep(item, depth):
        return jnp.pad(item, ((0, depth - item.shape[0]), (0, 0)))

    if near:
        pair_one = low(jnp.concatenate([condense_shard, restore_shard]))
        pair_two = low(
            jnp.concatenate([deep(mixing_shard, depth_one), deep(lateral_shard, depth_two)])
        )
        pair_own = jnp.where(far_place == 0, pair_one, pair_two)
        pair_got = swap(jnp.where(far_place == 0, pair_two, pair_one), "tm", 2)
        restore_speed = pick(restore_velocity.reshape(far, 2, depth_two, CSM), 1, core)
        restore_speed = low(restore_speed.reshape(far * depth_two, CSM))
        wide_shape = ((batch_count, out_rows, CSM), BF16)
        tall_shape = ((batch_count, out_rows, far * depth_two), BF16)
        gram_shape = ((CSM, CSM), BF16)
        moved_one, moved_two, stem_moved, keep, give, stem_gram, grad_wide, grad_tall = call(
            gram_kernel,
            [
                ((far * depth_one, CSM), BF16),
                ((far * depth_two, CSM), BF16),
                (stem_own.shape, BF16),
                gram_shape,
                gram_shape,
                ((batch_count, 16, CSM), BF16),
                wide_shape,
                tall_shape,
            ],
            [
                place_cell,
                factor_cell,
                speed,
                restore_speed,
                pair_own,
                pair_got,
                stem_velocity,
                stem_own,
            ],
            [((CSM, CSM), F32)],
            scalars=(0,),
        )
        gram = low(keep.astype(F32) + swap(give, "tm", 1).astype(F32))
        riders = low(small_shard)
        riders = jnp.concatenate(
            [
                jnp.pad(riders[0:40], ((0, 0), (0, 64))),
                jnp.pad(riders[40:], ((0, 8), (0, 64))),
            ],
            axis=1,
        )
        riders = jnp.broadcast_to(riders[None], (batch_count,) + riders.shape)
        got = lax.all_to_all(
            jnp.concatenate([gram.reshape(wide_shape[0]), stem_gram, riders], axis=1),
            "batch", 0, 0, tiled=True,
        )
        summed = low(jnp.sum(got[:, 0:80].astype(F32), axis=0))
        small_whole = jnp.concatenate([got[:, 80:120, 0:192], got[:, 80:112, 256:448]], axis=1)
        small_grads, items = small_parts(small_whole)
        whole = lax.all_to_all(
            jnp.concatenate(
                [jnp.broadcast_to(summed[None], (batch_count,) + summed.shape), grad_wide], axis=1
            ),
            "batch", 0, 0, tiled=True,
        )
        shaped, *shapes = call(
            block_shape_kernel,
            [gram_shape, ((192, 192), BF16)] + [((CFM, CFM), BF16)] * 3,
            [whole] + [rows_by_rows(item, item) for item in items],
            [((CSM, CSM), F32), ((192, 192), F32)],
            micros=10,
        )

        def put_rows(rule, held, tall):
            edge = far * depth_one
            second = jnp.where(far_place == 0, tall, held[..., edge:])
            held = jnp.concatenate([held[..., 0:edge], second], axis=-1)
            kernel = functools.partial(place_kernel, rule, far, main_rows, depth_one)
            return call(
                kernel,
                [(base.shape, F32) for base in bases[rule]],
                [place_cell, factor_cell, *pairs_of(held, held), *bases[rule]],
                [((tm_count,) + wide_shape[0], BF16)],
                scalars=(0,),
            )

        grads = put_rows(carry, whole[:, 80:144], grad_tall)
        ortho_wide, ortho_tall = call(
            ortho_kernel,
            [wide_shape, tall_shape],
            [place_cell, shaped, swap(shaped, "tm", 1), moved_one, moved_two],
            scalars=(0,),
        )
        ortho_wide = lax.all_to_all(ortho_wide, "batch", 0, 0, tiled=True)
        direct = direct_orthos(stem_moved, shapes, items)
        tied = lax.optimization_barrier((ortho_wide, *grads, *direct))
        ortho_wide, grads, direct = tied[0], tied[1:5], tied[5:]
        orthos = put_rows(renew, ortho_wide, ortho_tall)
    else:
        pair_one = jnp.concatenate([condense_shard, deep(restore_shard, depth_two)])
        pair_two = jnp.concatenate([deep(mixing_shard, depth_one), deep(lateral_shard, depth_two)])
        pairs = jnp.stack([pair_one, pair_two] + [jnp.zeros_like(pair_one)] * (far - 2)).astype(BF16)
        grads_held = by_place(
            [pick(pairs, 0, far_place)]
            + [swap(pick(pairs, 0, far_place ^ k), "tm", 2 * k) for k in range(1, far)],
            far_place,
        )

        def cut(held):
            one = jnp.concatenate(
                [
                    held[:, 0:main_rows].reshape(far * main_rows, CSM),
                    held[:, main_rows:depth_one].reshape(far * (depth_one - main_rows), CSM),
                ]
            )
            return one, held[:, depth_one:].reshape(far * depth_two, CSM)

        speed = speed[:, 0:out_rows].reshape(CSM, -1)
        speed_one = speed[:, 0 : far * depth_one].T
        restore_speed = pick(restore_velocity.reshape(far, 2, depth_two, CSM), 1, core)
        restore_speed = restore_speed.reshape(far * depth_two, CSM)
        speed_two = jnp.where(
            far_place == 0, restore_speed.astype(BF16), speed[:, far * depth_one :].T
        )
        grad_one, grad_two = cut(grads_held)
        used = far_place < 2

        def step_of(speed_part, grad_part):
            moved = MUON_KEEP * speed_part.astype(F32) + grad_part.astype(F32) * factor
            return jnp.where(used, moved, 0.0).astype(BF16)

        stem_moved = low(MUON_KEEP * stem_velocity + stem_own.astype(F32) * factor)

        moved_one = step_of(speed_one, grad_one)
        moved_two = step_of(speed_two, grad_two)
        gram_one = over_rows(moved_one, moved_one)
        gram_two = over_rows(moved_two, moved_two)
        gram = jnp.where(core == 0, gram_one, gram_two) + swap(
            jnp.where(core == 0, gram_two, gram_one), "tm", 1
        )
        stem_gram = over_rows(stem_moved, stem_moved)

        def flat_rows(item):
            return item.reshape(batch_count, -1).astype(GRAM)

        parts = [flat_rows(gram), flat_rows(stem_gram)]
        sizes = [part.shape[1] for part in parts]
        riders = jnp.broadcast_to(small_shard.reshape(1, -1).astype(GRAM), (batch_count, small_shard.size))

        def packed(items):
            whole = jnp.concatenate(items, axis=1)
            whole = jnp.pad(whole, ((0, 0), (0, -whole.shape[1] % 2048)))
            return whole.reshape(batch_count, -1, 256)

        def exchanged(items):
            whole = lax.all_to_all(packed(items), "batch", 0, 0, tiled=True)
            return whole.reshape(batch_count, -1)

        got = exchanged(parts + [riders])
        summed = jnp.sum(got[:, 0 : sum(sizes)].astype(F32), axis=0, keepdims=True).astype(GRAM)
        small_whole = got[:, sum(sizes) : sum(sizes) + small_shard.size]
        small_grads, items = small_parts(small_whole)
        grad_one, grad_two, summed = lax.optimization_barrier((grad_one, grad_two, summed))
        whole = exchanged([jnp.broadcast_to(summed, (batch_count, summed.shape[1]))]).astype(F32)
        gram = whole[:, 0 : sizes[0]].reshape(CSM, CSM)
        stem_gram = whole[:, sizes[0] : sum(sizes)].reshape(stem_gram.shape)

        shaped, *shapes = shape_of([gram, stem_gram] + [rows_by_rows(item, item) for item in items])
        shaped = low(shaped)
        shapes = [low(shape) for shape in shapes]
        shaped_other = swap(shaped, "tm", 1)
        shape_one = jnp.where(core == 0, shaped, shaped_other)
        shape_two = jnp.where(core == 0, shaped_other, shaped)

        def spread_rows(rule, bases, wide_one, wide_two, tall_two):
            lateral_base, condense_base, mixing_base, restore_base = bases
            wide_both = jnp.concatenate([wide_one, wide_two], axis=1)
            wide_both = wide_both.reshape(batch_count, out_rows, -1)
            held = lax.all_to_all(wide_both, "batch", 0, 0, tiled=True)
            width = far * depth_two
            tall = jnp.concatenate(
                [tall_two[:, k * width : (k + 1) * width] for k in range(CSM // width)], axis=0
            ).reshape(batch_count, out_rows, width)
            second = jnp.where(far_place == 0, tall, held[..., far * depth_one :])
            held = jnp.concatenate([held[..., 0 : far * depth_one], second], axis=-1)
            held = by_place(
                [held] + [swap(held, "tm", 2 * k) for k in range(1, far)], far_place
            )[0:2]
            other = swap(held, "tm", 1)
            held = (jnp.where(core == 0, held, other), jnp.where(core == 0, other, held))

            edge = far * main_rows
            stop = far * depth_one
            def taps_of(place, base, main_taps, size):
                block = jnp.stack([half[place] for half in held])
                main = block[..., 0:edge].reshape(
                    2, main_taps, batch_count // main_taps, out_rows, far, main_rows
                )
                main = jnp.transpose(main, (3, 1, 4, 0, 2, 5)).reshape(out_rows, -1)
                rest = block[..., edge:stop].reshape(
                    2, batch_count, out_rows, far, depth_one - main_rows
                )[..., 0:size]
                rest = jnp.transpose(rest, (2, 3, 0, 1, 4)).reshape(out_rows, -1)
                return jnp.concatenate([main, rest], axis=1)

            block = jnp.stack([half[1, :, :, stop:] for half in held])
            block = block.reshape(2, batch_count, out_rows, far, depth_two)[..., 0:lateral_rows]
            block = jnp.transpose(block, (2, 3, 0, 1, 4)).reshape(out_rows, tm_count, 5, -1)
            side_rows = jnp.swapaxes(block, 1, 2).reshape(out_rows, 5 * CF)
            tall_rows = []
            for half in held:
                block = half[0, :, :, stop:].reshape(CSM // width, width, width)
                block = jnp.concatenate([block[k] for k in range(CSM // width)], axis=1)
                tall_rows.append(block.reshape(far, depth_two, CSM))
            tall_rows = jnp.stack(tall_rows, axis=1).reshape(-1, CSM)
            results = (
                side_rows,
                taps_of(0, condense_base, 2, rest_depth),
                taps_of(1, mixing_base, 8, mixing_rows - main_rows),
                tall_rows,
            )
            return [rule(base, item.astype(F32), ratio_of(base), factor) for base, item in zip(bases, results)]

        grads = spread_rows(
            carry, bases[carry],
            grad_one.T, grad_two.T, grad_two,
        )
        orthos = spread_rows(
            renew, bases[renew],
            low(rows_by_rows(shape_one, moved_one)),
            low(rows_by_rows(shape_two, moved_two)),
            low(rows_by_columns(moved_two, shape_two)),
        )

    if not near:
        direct = direct_orthos(stem_moved, shapes, items)
    stem_ortho, *small_orthos = direct
    part = recover.shape[0]
    small_own = [
        own(small_grads[0], small_rows),
        own(small_grads[1], small_rows),
        own(small_grads[2].T, part),
    ]

    def both_of(weight, speed, grad, ortho):
        ortho = low(ortho).astype(F32)
        return (
            carry(speed, grad.astype(F32), 1.0, factor),
            renew(weight, ortho, ratio_of(weight), factor),
        )

    stem_pair = both_of(stem_weight, stem_velocity, stem_own, stem_ortho)
    small_pairs = [
        both_of(*items)
        for items in zip(
            (squeeze, blending, recover),
            (squeeze_velocity, blending_velocity, recover_velocity),
            small_own,
            small_orthos,
        )
    ]
    carried = [stem_pair[0], *grads] + [pair[0] for pair in small_pairs]
    updated = [stem_pair[1], *orthos] + [pair[1] for pair in small_pairs]
    head_new, head_first, head_second = adam(
        head_weight, head_moment, head_square, head_grad * factor, HEAD_RATE, WEIGHT_DECAY
    )
    affine_new, affine_first, affine_second = adam(
        affine, affine_moment, affine_square, affine_grad * factor, AFFINE_RATE, 0.0
    )
    return (
        *carried,
        *updated,
        head_new,
        head_first,
        head_second,
        affine_new,
        affine_first,
        affine_second,
        loss_total,
        clip_count,
        grad_norm,
    )


def solution(mesh):
    in_specs = (
        P("batch", "tm", None, None, None),
        P("batch"),
        P("batch"),
        P("batch"),
        P("batch"),
        P("batch", None),
        P("batch", None),
        P("batch", None),
        P("batch", None),
        P("batch", None),
        P("batch", None),
        P("batch", None),
        P("batch", None),
        P("batch", None),
        P("batch", None),
        P("batch", None),
        P("batch", None),
        P("batch", None),
        P("batch", None),
        P("batch", None),
        P("batch", None),
        P("batch", None),
        P("batch", None),
        P("batch", None),
        P(),
        P(),
        P(),
    )
    out_specs = (
        P("batch", None),
        P("batch", None),
        P("batch", None),
        P("batch", None),
        P("batch", None),
        P("batch", None),
        P("batch", None),
        P("batch", None),
        P("batch", None),
        P("batch", None),
        P("batch", None),
        P("batch", None),
        P("batch", None),
        P("batch", None),
        P("batch", None),
        P("batch", None),
        P("batch", None),
        P("batch", None),
        P("batch", None),
        P(),
        P(),
        P(),
        P(),
        P(),
        P(),
    )
    return jax.shard_map(
        per_device, mesh=mesh, in_specs=in_specs, out_specs=out_specs, check_vma=False
    )
```

time: 2650 us -> 635 us (0.24)
  waiting for transfers between devices: 1690 us -> 206 us
  blocking collectives: 541 us -> 29.9 us
  Pallas kernels: 0 us -> 144 us
  matrix products: 138 us -> 10.6 us
  starting transfers between devices: 27.4 us -> 105 us
  other arithmetic: 107 us -> 37.2 us
  loops' own time: 37.9 us -> 0 us
    reduce_scatter x12 -> x0, waiting for transfers between devices: 1050 us -> none  [the longest x1 211 us: per_device(): lax.psum_scatter(slow_grads[0], 'batch', scatter_dimension=0, tiled=True)]
    unnamed x33 -> x2, waiting for transfers between devices: 381 us -> 0.03 us
    psum x9 -> x0, blocking collectives: 281 us -> none  [the longest x3 120 us: norm_stats(): lax.psum((jnp.sum(mask * values, axis=(0, 1, 2, 3)), jnp.sum(mask * value...]
    all_gather x8 -> x0, blocking collectives: 260 us -> none  [the longest x1 37.6 us: per_device(): lax.all_gather(stem_weight.astype(jnp.bfloat16), 'batch', axis=0, tiled=T...]
    pallas_call x0 -> x19, Pallas kernels: none -> 144 us  [call(): pl.pallas_call(kernel, in_specs=specs, out_shape=[jax.ShapeDtypeStruct(sh...]
    dot_general x109 -> x12, matrix products: 138 us -> 10.6 us  [dot(): lax.dot_general(left, right, ((dims[0], dims[1]), ((), ())), preferred_el...]
    psum x2 -> x0, waiting for transfers between devices: 119 us -> none  [the longest x1 104 us: per_device(): lax.psum((summed[0], summed[1], summed[2], summed[3], summed[4], summed[5...]
    all_gather x9 -> x2, waiting for transfers between devices: 141 us -> 41.5 us  [the longest x1 41.5 us: per_device(): lax.all_gather(weights_low, ('batch', 'tm'), axis=0, tiled=True)]
  transfers between devices with their start and end apart: 38 -> 61, of which waited for: 22 -> 26; matrix products, arithmetic and copies ran while one was open for 8% -> 15% of each run, Pallas kernels for 0% -> 20%
where the time goes in v1:
time: 635 us; the launch traced here: 625 us
  waiting for transfers between devices  206 us (32%)
  Pallas kernels  144 us (23%)
  starting transfers between devices  105 us (17%)
  local copies, waits for them, and re-layouts  64.7 us (10%)
  other arithmetic  37.2 us (6%)
  blocking collectives  29.9 us (5%)
  between operations  27.8 us (4%)
  matrix products  10.6 us (2%)
    pallas_call x19, Pallas kernels, call(): pl.pallas_call(kernel, in_specs=specs, out_shape=[jax.ShapeDtypeStruct(sh...  144 us
    ppermute x41, waiting for transfers between devices, swap(): return lax.ppermute(values, axis, [(i, i ^ mask) for i in range(count)])  88.8 us
    all_gather x1, waiting for transfers between devices, per_device(): lax.all_gather(weights_low, ('batch', 'tm'), axis=0, tiled=True)  41.5 us
    ppermute x41, starting transfers between devices, swap(): return lax.ppermute(values, axis, [(i, i ^ mask) for i in range(count)])  34.9 us
    all_to_all x1, blocking collectives, per_device(): lax.all_to_all(jnp.concatenate([gram.reshape(wide_shape[0]), stem_gram, r...  29.9 us
    all_to_all x5, waiting for transfers between devices, spread_all(): return lax.all_to_all(copies, axes, 0, 0, tiled=True)  27.8 us
    all_to_all x5, starting transfers between devices, spread_all(): return lax.all_to_all(copies, axes, 0, 0, tiled=True)  24.3 us
    all_to_all x4, waiting for transfers between devices, exchange(): return lax.all_to_all(copies, both, 0, 0, tiled=True)  22.6 us
  transfers between devices with their start and end apart: 61, of which 26 were waited for; matrix products, arithmetic and copies ran while one was open for 15% of the time, Pallas kernels for 20%

profile of v1, /device:TPU:0, one launch (start us, length us, event | category | flops | bytes accessed | tf_op | source)
XLA Modules:
  0.0 624.5 jit_solution(6811584830833779852)
XLA Ops:
  15.3 3.8 collective-permute-start
  20.1 7.3 %all-to-all-start.1 = ((bf16[8,8,1600]{2,1,0:T(8,128)(2,1)}), bf16[8,8,1600]{2,1,0:T(8,128)(2,1)S(1)}, u32[]{:S(2)}, u32[]{:S(2)}) async-start(bf16[8,8,1600]{2,1,0:T(8,128)(2,1)} %broadcast_in_dim.127), calls=%async_computation.1 | async-start | bytes 425984 | tf_op jit(solution)/shard_map/all_to_all | solution.py:61
  38.2 2.8 all-to-all-done.1
  41.8 4.1 all-to-all-start
  51.1 11.4 %all-to-all-done = bf16[8,72,192]{2,1,0:T(8,128)(2,1)} async-done(((bf16[8,72,192]{2,1,0:T(8,128)(2,1)}), bf16[8,72,192]{2,1,0:T(8,128)(2,1)}, u32[]{:S(2)}, u32[]{:S(2)}) %all-to-all-start) | async-done | bytes 221216 | tf_op jit(solution)/shard_map/all_to_all | solution.py:61
  62.5 4.3 all-to-all-start.2
  69.6 6.1 collective-permute-done.2
  76.8 2.3 pad_maximum_fusion.fast_video
  84.4 12.0 %shard_map.450 = (f32[392,2048]{1,0:T(8,128)}, f32[4,392,256]{2,1,0:T(8,128)}, bf16[3,392,2048]{2,1,0:T(8,128)(2,1)}, bf16[7,392,256]{2,1,0:T(8,128)(2,1)}, bf16...) custom-call(s32[1]{0:T(128)} %bitcast.place.refs_0_, ...), custom_call_target="tpu_custom_call" | custom-call | flops 6899999744 | bytes 18000000 | tf_op jit(solution)/shard_map/pallas_call | solution.py:146
  96.4 41.5 %all-gather.3.cloned.1.call-done.weights.refs_7_.refs_6_ = bf16[512,14080]{1,0:T(8,128)(2,1)} async-done(((bf16[16,14080]{1,0:T(8,128)(2,1)}), bf16[512,14080]{1,0:T(8,128)(2,1)}) %all-gather.3.cloned.1.call-update) | async-done | bytes 14417936 | tf_op jit(solution)/shard_map/all_gather | solution.py:1119
  137.9 9.4 %shard_map.451 = (f32[392,512]{1,0:T(8,128)}, f32[4,392,64]{2,1,0:T(8,128)}, f32[32,8,256]{2,1,0:T(8,128)}) custom-call(bf16[3,392,2048]{2,1,0:T(8,128)(2,1)} %get-tuple-element.150.slow_low, bf16[7,392,256]{2,1,0:T(8,128)(2,1)} %get-tuple-element.151.fast_low, bf16[512,14080]{1,0:T(8,128)(2,1)} %all-gather.3.cloned.1.call-done.weights.refs_7_.refs_6_, ...), custom_call_target="tpu_custom_call" | custom-call | flops 6899999744 | bytes 18000000 | tf_op jit(solution)/shard_map/pallas_call | solution.py:146
  147.3 2.8 all-to-all-start.3
  152.2 9.6 %all-to-all-done.3.refs_3_ = f32[32,8,256]{2,1,0:T(8,128)S(1)} async-done(((f32[32,8,256]{2,1,0:T(8,128)}), f32[32,8,256]{2,1,0:T(8,128)S(1)}, u32[]{:S(2)}, u32[]{:S(2)}) %all-to-all-start.3) | async-done | bytes 262176 | tf_op jit(solution)/shard_map/all_to_all | solution.py:1153
  162.5 8.9 %shard_map.452 = (f32[392,512]{1,0:T(8,128)}, f32[4,392,64]{2,1,0:T(8,128)}, f32[8,256]{1,0:T(8,128)}, f32[32,8,256]{2,1,0:T(8,128)}, bf16[392,128]{1,0:T(8,128)...) custom-call(s32[1]{0:T(128)} %bitcast.place.refs_0_, ...), custom_call_target="tpu_custom_call" | custom-call | flops 6899999744 | bytes 18000000 | tf_op jit(solution)/shard_map/pallas_call | solution.py:146
  171.4 2.6 all-to-all-start.4
  176.0 8.7 %all-to-all-done.4.got = f32[32,8,256]{2,1,0:T(8,128)S(1)} async-done(((f32[32,8,256]{2,1,0:T(8,128)}), f32[32,8,256]{2,1,0:T(8,128)S(1)}, u32[]{:S(2)}, u32[]{:S(2)}) %all-to-all-start.4) | async-done | bytes 262176 | tf_op jit(solution)/shard_map/all_to_all | solution.py:1153
  185.4 7.3 %shard_map.453 = (bf16[392,512]{1,0:T(8,128)(2,1)}, bf16[4,392,64]{2,1,0:T(8,128)(2,1)}, f32[392,2048]{1,0:T(8,128)}, f32[4,392,256]{2,1,0:T(8,128)}, f32[8,256]{1,0:T(8,128)}, /*index=5*/f32[8,640]{1,0:T(8,128)}) custom-call(f32[392,512]{1,0:T(8,128)} %get-tuple-element.156.h2, f32[4,392,64]{2,1,0:T(8,128)} %get-tuple-element.157.h5, ...), custom_call_target="tpu_custom_call" | custom-call | flops 6899999744 | bytes 18000000 | tf_op jit(solution)/shard_map/pallas_call | solution.py:146
  194.5 3.2 all-to-all-start.5
  207.1 11.5 %collective-permute-done.15.refs_6_ = bf16[5,392,128]{2,1,0:T(8,128)(2,1)S(1)} collective-permute-done((bf16[5,392,128]{2,1,0:T(8,128)(2,1)S(1)}, bf16[5,392,128]{2,1,0:T(8,128)(2,1)S(1)}, u32[]{:S(2)}, u32[]{:S(2)}) %collective-permute-start.15) | collective-permute-done | bytes 501792 | tf_op jit(solution)/shard_map/ppermute | solution.py:49
  221.6 4.8 collective-permute-done.5.refs_4_
  227.3 8.8 %shard_map.454 = (f32[8,2304]{1,0:T(8,128)}, f32[8,640]{1,0:T(8,128)}) custom-call(f32[392,2048]{1,0:T(8,128)} %get-tuple-element.163.h3, f32[4,392,256]{2,1,0:T(8,128)} %get-tuple-element.164.h6, f32[392,2048]{1,0:T(8,128)} %get-tuple-element.165.slow_pre.refs_10_, f32[4,392,256]{2,1,0:T(8,128)} %get-tuple-element.166.fast_pre.refs_11_, ...), custom_call_target="tpu_custom_call" | custom-call | flops 6899999744 | bytes 18000000 | tf_op jit(solution)/shard_map/pallas_call | solution.py:146
  237.1 7.4 %collective-permute-done.13.refs_5_ = bf16[392,512]{1,0:T(8,128)(2,1)} collective-permute-done((bf16[392,512]{1,0:T(8,128)(2,1)S(1)}, bf16[392,512]{1,0:T(8,128)(2,1)}, u32[]{:S(2)}, u32[]{:S(2)}) %collective-permute-start.13) | collective-permute-done | bytes 401440 | tf_op jit(solution)/shard_map/ppermute | solution.py:49
  250.1 11.3 %shard_map.455 = (bf16[8,2304]{1,0:T(8,128)(2,1)}, bf16[8,400]{1,0:T(8,128)(2,1)}, f32[392,2048]{1,0:T(8,128)}, f32[4,392,256]{2,1,0:T(8,128)}, f32[8,640]{1,0:T(8,128)}) custom-call(f32[4,8,2304]{2,1,0:T(8,128)} %pad_maximum_fusion.15.pools, bf16[2304,400]{1,0:T(8,128)(2,1)} %all-gather.5.cloned.1.call-done.head, f32[1,400]{1,0:T(1,128)} %bitcast.272, ...), custom_call_target="tpu_custom_call" | custom-call | flops 6899999744 | bytes 18000000 | tf_op jit(solution)/shard_map/pallas_call | solution.py:146
  262.9 6.0 all-to-all-start.6
  271.9 9.1 %all-to-all-done.6.got = bf16[32,8,640]{2,1,0:T(8,128)(2,1)S(1)} async-done(((bf16[32,8,640]{2,1,0:T(8,128)(2,1)}), bf16[32,8,640]{2,1,0:T(8,128)(2,1)S(1)}, u32[]{:S(2)}, u32[]{:S(2)}) %all-to-all-start.6) | async-done | bytes 327712 | tf_op jit(solution)/shard_map/all_to_all | solution.py:61
  281.7 10.5 %shard_map.456 = (bf16[4,392,256]{2,1,0:T(8,128)(2,1)}, f32[392,512]{1,0:T(8,128)}, f32[4,392,64]{2,1,0:T(8,128)}, f32[8,640]{1,0:T(8,128)}, bf16[32,8,256]{2,1,...) custom-call(s32[1]{0:T(128)} %bitcast.place.refs_0_, ...), custom_call_target="tpu_custom_call" | custom-call | flops 6899999744 | bytes 18000000 | tf_op jit(solution)/shard_map/pallas_call | solution.py:146
  294.1 2.6 all-to-all-start.7
  300.1 4.3 all-to-all-done.7.got
  305.1 11.0 %shard_map.457 = (bf16[392,512]{1,0:T(8,128)(2,1)}, bf16[4,392,64]{2,1,0:T(8,128)(2,1)}, f32[392,512]{1,0:T(8,128)}, f32[4,392,64]{2,1,0:T(8,128)}, f32[9,64,64]...) custom-call(f32[392,512]{1,0:T(8,128)} %get-tuple-element.188.e2, f32[4,392,64]{2,1,0:T(8,128)} %get-tuple-element.189.e5, ...), custom_call_target="tpu_custom_call" | custom-call | flops 6899999744 | bytes 18000000 | tf_op jit(solution)/shard_map/pallas_call | solution.py:146
  319.3 2.9 all-to-all-start.8
  323.7 5.0 collective-permute-done.17.refs_5_
  329.7 3.9 shard_map.458.refs_7_
  333.6 5.6 shard_map.459
  339.8 4.9 all-to-all-start.9
  344.8 3.6 shard_map.460
  351.1 8.9 %collective-permute-done.22.refs_1_.refs_9_ = bf16[392,512]{1,0:T(8,128)(2,1)S(1)} collective-permute-done((bf16[392,512]{1,0:T(8,128)(2,1)}, bf16[392,512]{1,0:T(8,128)(2,1)S(1)}, u32[]{:S(2)}, u32[]{:S(2)}) %collective-permute-start.22) | collective-permute-done | bytes 401440 | tf_op jit(solution)/shard_map/ppermute | solution.py:49
  360.0 2.1 pad_maximum_fusion.8
  362.1 3.1 collective-permute-start.24
  368.5 12.5 %shard_map.461 = (bf16[392,2048]{1,0:T(8,128)(2,1)}, bf16[4,392,256]{2,1,0:T(8,128)(2,1)}) custom-call(s32[1]{0:T(128)} %bitcast.place.refs_0_, bf16[392,512]{1,0:T(8,128)(2,1)} %get-tuple-element.225.refs_0_.refs_8_, bf16[392,512]{1,0:T(8,128)(2,1)} %copy-done.6, bf16[2,392,512]{2,1,0:T(8,128)(2,1)} %collective-permute-done.23.refs_2_.refs_10_, ...), custom_call_target="tpu_custom_call" | custom-call | flops 6899999744 | bytes 18000000 | tf_op jit(solution)/shard_map/pallas_call | solution.py:146
  381.0 8.9 %shard_map.463 = bf16[8,240,512]{2,1,0:T(8,128)(2,1)} custom-call(s32[1]{0:T(128)} %bitcast.place.refs_0_, bf16[392,512]{1,0:T(8,128)(2,1)} %get-tuple-element.218.refs_1_, bf16[392,512]{1,0:T(8,128)(2,1)} %collective-permute-done.4.refs_2_, bf16[392,512]{1,0:T(8,128)(2,1)} %collective-permute-done.9.refs_3_, ...), custom_call_target="tpu_custom_call" | custom-call | flops 6899999744 | bytes 18000000 | tf_op jit(solution)/shard_map/pallas_call | solution.py:146
  390.1 6.3 %all-to-all-start.10 = ((bf16[8,240,512]{2,1,0:T(8,128)(2,1)}), bf16[8,240,512]{2,1,0:T(8,128)(2,1)S(1)}, u32[]{:S(2)}, u32[]{:S(2)}) async-start(bf16[8,240,512]{2,1,0:T(8,128)(2,1)} %shard_map.463), calls=%async_computation.10 | async-start | bytes 3932160 | tf_op jit(solution)/shard_map/all_to_all | solution.py:1446
  398.2 4.3 shard_map.462
  402.5 2.7 collective-permute-start.26
  407.6 9.7 %collective-permute-done.27 = bf16[8,96,192]{2,1,0:T(8,128)(2,1)S(1)} collective-permute-done((bf16[8,96,192]{2,1,0:T(8,128)(2,1)}, bf16[8,96,192]{2,1,0:T(8,128)(2,1)S(1)}, u32[]{:S(2)}, u32[]{:S(2)}) %collective-permute-start.27) | collective-permute-done | bytes 294944 | tf_op jit(solution)/shard_map/ppermute | solution.py:49
  417.4 6.5 %collective-permute-done.28 = bf16[8,96,192]{2,1,0:T(8,128)(2,1)S(1)} collective-permute-done((bf16[8,96,192]{2,1,0:T(8,128)(2,1)}, bf16[8,96,192]{2,1,0:T(8,128)(2,1)S(1)}, u32[]{:S(2)}, u32[]{:S(2)}) %collective-permute-start.28) | collective-permute-done | bytes 294944 | tf_op jit(solution)/shard_map/ppermute | solution.py:49
  428.8 2.6 collective-permute-start.32
  432.9 3.3 collective-permute-start.34
  437.6 11.3 %collective-permute-done.32 = bf16[125,192]{1,0:T(8,128)(2,1)S(1)} collective-permute-done((bf16[125,192]{1,0:T(8,128)(2,1)S(1)}, bf16[125,192]{1,0:T(8,128)(2,1)S(1)}, u32[]{:S(2)}, u32[]{:S(2)}) %collective-permute-start.32) | collective-permute-done | bytes 48032 | tf_op jit(solution)/shard_map/ppermute | solution.py:49
  449.0 2.4 collective-permute-done.33
  452.5 2.4 collective-permute-start.36
  465.8 3.8 all-to-all-start.11
  473.0 4.4 all-to-all-done.11
  480.7 3.5 shard_map.464
  487.6 29.9 %all_to_all.75 = bf16[8,120,512]{2,1,0:T(8,128)(2,1)S(1)} all-to-all(bf16[8,120,512]{2,1,0:T(8,128)(2,1)S(1)} %pad_maximum_fusion.5), channel_id=1, replica_groups=mesh['tm'=4,'batch'=8] {'batch'}, dimensions={0} | all-to-all | bytes 1966080 | tf_op jit(solution)/shard_map/all_to_all | solution.py:1734
  518.8 3.9 all-to-all-start.13
  528.3 2.9 multiply_subtract_fusion
  534.3 16.7 %all-to-all-done.13.whole = bf16[8,144,512]{2,1,0:T(8,128)(2,1)S(1)} async-done(((bf16[8,144,512]{2,1,0:T(8,128)(2,1)}), bf16[8,144,512]{2,1,0:T(8,128)(2,1)S(1)}, u32[]{:S(2)}, u32[]{:S(2)}) %all-to-all-start.13) | async-done | bytes 1179680 | tf_op jit(solution)/shard_map/all_to_all | solution.py:1741
  552.3 6.4 %shard_map.465 = (bf16[512,512]{1,0:T(8,128)(2,1)}, bf16[192,192]{1,0:T(8,128)(2,1)}, bf16[64,64]{1,0:T(8,128)(2,1)}, bf16[64,64]{1,0:T(8,128)(2,1)}, bf16[64,64]{1,0:T(8,128)(2,1)}) custom-call(bf16[8,144,512]{2,1,0:T(8,128)(2,1)} %copy-done.4, f32[64,64]{1,0:T(8,128)} %fusion.45.refs_0_, f32[64,64]{1,0:T(8,128)} %fusion.46.refs_1_, f32[64,64]{1,0:T(8,128)} %fusion.69.refs_2_), custom_call_target="tpu_custom_call" | custom-call | flops 11500000256 | bytes 30000000 | tf_op jit(solution)/shard_map/pallas_call | solution.py:146
  566.1 2.9 shard_map.466
  568.9 5.6 all-to-all-start.14
  575.6 6.5 %shard_map.467 = (f32[64,1280]{1,0:T(8,128)}, f32[64,6144]{1,0:T(8,128)}, f32[64,4608]{1,0:T(8,128)}, f32[256,512]{1,0:T(8,128)}) custom-call(s32[1]{0:T(128)} %bitcast.place.refs_0_, f32[1,1]{1,0:T(1,128)} %bitcast.101.factor, bf16[8,64,512]{2,1,0:T(8,128)(2,1)} %copy-done.16, bf16[8,64,512]{2,1,0:T(8,128)(2,1)} %copy-done.19, ...), custom_call_target="tpu_custom_call" | custom-call | flops 6899999744 | bytes 18000000 | tf_op jit(solution)/shard_map/pallas_call | solution.py:146
  582.2 7.4 %all-to-all-done.14 = bf16[8,64,512]{2,1,0:T(8,128)(2,1)S(1)} async-done(((bf16[8,64,512]{2,1,0:T(8,128)(2,1)}), bf16[8,64,512]{2,1,0:T(8,128)(2,1)S(1)}, u32[]{:S(2)}, u32[]{:S(2)}) %all-to-all-start.14) | async-done | bytes 524320 | tf_op jit(solution)/shard_map/all_to_all | solution.py:1775
  593.3 9.6 %collective-permute-done.43.across = bf16[8,64,512]{2,1,0:T(8,128)(2,1)S(1)} collective-permute-done((bf16[8,64,512]{2,1,0:T(8,128)(2,1)S(1)}, bf16[8,64,512]{2,1,0:T(8,128)(2,1)S(1)}, u32[]{:S(2)}, u32[]{:S(2)}) %collective-permute-start.43) | collective-permute-done | bytes 524320 | tf_op jit(solution)/shard_map/ppermute | solution.py:49
  607.4 6.7 %shard_map.468 = (f32[64,1280]{1,0:T(8,128)}, f32[64,6144]{1,0:T(8,128)}, f32[64,4608]{1,0:T(8,128)}, f32[256,512]{1,0:T(8,128)}) custom-call(s32[1]{0:T(128)} %bitcast.place.refs_0_, f32[1,1]{1,0:T(1,128)} %bitcast.101.factor, bf16[8,64,512]{2,1,0:T(8,128)(2,1)} %copy-done.17, bf16[8,64,512]{2,1,0:T(8,128)(2,1)} %copy-done.20, ...), custom_call_target="tpu_custom_call" | custom-call | flops 6899999744 | bytes 18000000 | tf_op jit(solution)/shard_map/pallas_call | solution.py:146
  (513 shorter events, 138.0 us)
Async XLA Ops:
  7.2 130.7 %all-gather.3.cloned.1.call-start = ((), (), s32[]{:S(2)}) async-start(), calls=%async_computation.15 | async-start | bytes 14868480 | tf_op jit(solution)/shard_map/all_gather | solution.py:1119
  12.3 64.5 %collective-permute-start.1 = (bf16[1,392,192]{2,1,0:T(8,128)(2,1)S(1)}, bf16[1,392,192]{2,1,0:T(8,128)(2,1)}, u32[]{:S(2)}, u32[]{:S(2)}) collective-permute-start(bf16[1,392,192]{2,1,0:T(8,128)(2,1)S(1)} %bitcast.216), channel_id=1, source_target_pairs={{8,0},{16,8},{24,16},{9,1},{17,9},{25,17},{10,2},{18,10},{26,18},{... | collective-permute-start | bytes 451592 | tf_op jit(solution)/shard_map/ppermute | solution.py:55
  15.3 53.0 %collective-permute-start = (bf16[3,392,192]{1,2,0:T(8,128)(2,1)}, bf16[3,392,192]{1,2,0:T(8,128)(2,1)}, u32[]{:S(2)}, u32[]{:S(2)}) collective-permute-start(bf16[3,392,192]{1,2,0:T(8,128)(2,1)} %copy.317), channel_id=1, source_target_pairs={{0,8},{8,16},{16,24},{1,9},{9,17},{17,25},{2,10},{10,18},{18,26},{... | collective-permute-start | bytes 1354760 | tf_op jit(solution)/shard_map/ppermute | solution.py:55
  20.1 21.0 %all-to-all-start.1 = ((bf16[8,8,1600]{2,1,0:T(8,128)(2,1)}), bf16[8,8,1600]{2,1,0:T(8,128)(2,1)S(1)}, u32[]{:S(2)}, u32[]{:S(2)}) async-start(bf16[8,8,1600]{2,1,0:T(8,128)(2,1)} %broadcast_in_dim.127), calls=%async_computation.1 | async-start | bytes 425984 | tf_op jit(solution)/shard_map/all_to_all | solution.py:61
  27.4 222.8 %all-gather.5.cloned.1.call-start = ((), (), s32[]{:S(2)}) async-start(), calls=%async_computation.16 | async-start | bytes 2433024 | tf_op jit(solution)/shard_map/all_gather | solution.py:1088
  41.8 20.7 %all-to-all-start = ((bf16[8,72,192]{2,1,0:T(8,128)(2,1)}), bf16[8,72,192]{2,1,0:T(8,128)(2,1)}, u32[]{:S(2)}, u32[]{:S(2)}) async-start(bf16[8,72,192]{2,1,0:T(8,128)(2,1)} %broadcast_in_dim.121), calls=%async_computation | async-start | bytes 589824 | tf_op jit(solution)/shard_map/all_to_all | solution.py:61
  46.1 30.7 %copy-start.3 = (bf16[4,7,7,8,192]{4,3,2,1,0:T(8,128)(2,1)}, bf16[4,7,7,8,192]{4,3,2,1,0:T(8,128)(2,1)S(1)}, u32[]{:S(2)}) copy-start(bf16[4,7,7,8,192]{4,3,2,1,0:T(8,128)(2,1)S(1)} %copy.320) | copy-start | bytes 1806340
  62.5 33.9 %all-to-all-start.2 = ((bf16[8,89,512]{2,1,0:T(8,128)(2,1)}), bf16[8,89,512]{2,1,0:T(8,128)(2,1)S(1)}, u32[]{:S(2)}, u32[]{:S(2)}) async-start(bf16[8,89,512]{2,1,0:T(8,128)(2,1)} %pad_maximum_fusion.9), calls=%async_computation.2 | async-start | bytes 1572864 | tf_op jit(solution)/shard_map/all_to_all | solution.py:1225
  66.9 8.8 %collective-permute-start.2 = (bf16[8,72,192]{2,1,0:T(8,128)(2,1)}, bf16[8,72,192]{2,1,0:T(8,128)(2,1)}, u32[]{:S(2)}, u32[]{:S(2)}) collective-permute-start(bf16[8,72,192]{2,1,0:T(8,128)(2,1)} %all-to-all-done), channel_id=1, source_target_pairs={{0,16},{8,24},{16,0},{24,8},{1,17},{9,25},{17,1},{25,9},{2,18},{10... | collective-permute-start | bytes 663560 | tf_op jit(solution)/shard_map/ppermute | solution.py:49
  76.7 5.6 collective-permute-start.3
  96.4 50.9 %copy-start.8 = (bf16[8,89,512]{2,1,0:T(8,128)(2,1)}, bf16[8,89,512]{2,1,0:T(8,128)(2,1)S(1)}, u32[]{:S(2)}) copy-start(bf16[8,89,512]{2,1,0:T(8,128)(2,1)S(1)} %all-to-all-done.2.speed) | copy-start | bytes 2187268
  147.3 14.5 %all-to-all-start.3 = ((f32[32,8,256]{2,1,0:T(8,128)}), f32[32,8,256]{2,1,0:T(8,128)S(1)}, u32[]{:S(2)}, u32[]{:S(2)}) async-start(f32[32,8,256]{2,1,0:T(8,128)} %get-tuple-element.155), calls=%async_computation.3 | async-start | bytes 524288 | tf_op jit(solution)/shard_map/all_to_all | solution.py:1153
  171.4 13.3 %all-to-all-start.4 = ((f32[32,8,256]{2,1,0:T(8,128)}), f32[32,8,256]{2,1,0:T(8,128)S(1)}, u32[]{:S(2)}, u32[]{:S(2)}) async-start(f32[32,8,256]{2,1,0:T(8,128)} %get-tuple-element.159), calls=%async_computation.4 | async-start | bytes 524288 | tf_op jit(solution)/shard_map/all_to_all | solution.py:1153
  194.5 32.0 %all-to-all-start.5 = ((f32[32,8,640]{2,1,0:T(8,128)}), f32[32,8,640]{2,1,0:T(8,128)S(1)}, u32[]{:S(2)}, u32[]{:S(2)}) async-start(f32[32,8,640]{2,1,0:T(8,128)} %broadcast_in_dim.129), calls=%async_computation.5 | async-start | bytes 1310720 | tf_op jit(solution)/shard_map/all_to_all | solution.py:61
  197.7 20.9 %collective-permute-start.15 = (bf16[5,392,128]{2,1,0:T(8,128)(2,1)S(1)}, bf16[5,392,128]{2,1,0:T(8,128)(2,1)S(1)}, u32[]{:S(2)}, u32[]{:S(2)}) collective-permute-start(bf16[5,392,128]{2,1,0:T(8,128)(2,1)S(1)} %copy-done.76), channel_id=1, source_target_pairs={{0,16},{8,24},{16,0},{24,8},{1,17},{9,25},{17,1},{25,9},{2,18},{10... | collective-permute-start | bytes 1505288 | tf_op jit(solution)/shard_map/ppermute | solution.py:49
  201.1 20.5 %collective-permute-start.4 = (bf16[392,512]{1,0:T(8,128)(2,1)}, bf16[392,512]{1,0:T(8,128)(2,1)}, u32[]{:S(2)}, u32[]{:S(2)}) collective-permute-start(bf16[392,512]{1,0:T(8,128)(2,1)} %get-tuple-element.161), channel_id=1, source_target_pairs={{0,8},{8,0},{16,24},{24,16},{1,9},{9,1},{17,25},{25,17},{2,10},{10... | collective-permute-start | bytes 1204232 | tf_op jit(solution)/shard_map/ppermute | solution.py:49
  201.1 25.4 %collective-permute-start.5 = (bf16[392,512]{1,0:T(8,128)(2,1)}, bf16[392,512]{1,0:T(8,128)(2,1)}, u32[]{:S(2)}, u32[]{:S(2)}) collective-permute-start(bf16[392,512]{1,0:T(8,128)(2,1)} %get-tuple-element.162), channel_id=1, source_target_pairs={{0,24},{8,16},{16,8},{24,0},{1,25},{9,17},{17,9},{25,1},{2,26},{10... | collective-permute-start | bytes 1204232 | tf_op jit(solution)/shard_map/ppermute | solution.py:49
  205.3 44.4 %collective-permute-start.9 = (bf16[392,512]{1,0:T(8,128)(2,1)}, bf16[392,512]{1,0:T(8,128)(2,1)}, u32[]{:S(2)}, u32[]{:S(2)}) collective-permute-start(bf16[392,512]{1,0:T(8,128)(2,1)} %get-tuple-element.169), channel_id=1, source_target_pairs={{0,16},{8,24},{16,0},{24,8},{1,17},{9,25},{17,1},{25,9},{2,18},{10... | collective-permute-start | bytes 1204232 | tf_op jit(solution)/shard_map/ppermute | solution.py:49
  218.7 52.0 %collective-permute-start.16 = (bf16[2,5,392,128]{3,2,1,0:T(8,128)(2,1)S(1)}, bf16[2,5,392,128]{3,2,1,0:T(8,128)(2,1)}, u32[]{:S(2)}, u32[]{:S(2)}) collective-permute-start(bf16[2,5,392,128]{3,2,1,0:T(8,128)(2,1)S(1)} %pad_maximum_fusion.4), channel_id=1, source_target_pairs={{0,8},{8,0},{16,24},{24,16},{1,9},{9,1},{17,25},{25,17},{2,10},{10... | collective-permute-start | bytes 3010568 | tf_op jit(solution)/shard_map/ppermute | solution.py:49
  221.3 23.2 %collective-permute-start.13 = (bf16[392,512]{1,0:T(8,128)(2,1)S(1)}, bf16[392,512]{1,0:T(8,128)(2,1)}, u32[]{:S(2)}, u32[]{:S(2)}) collective-permute-start(bf16[392,512]{1,0:T(8,128)(2,1)S(1)} %copy-done.25), channel_id=1, source_target_pairs={{0,16},{8,24},{16,0},{24,8},{1,17},{9,25},{17,1},{25,9},{2,18},{10... | collective-permute-start | bytes 1204232 | tf_op jit(solution)/shard_map/ppermute | solution.py:49
  236.1 9.5 %collective-permute-start.6 = (f32[8,2304]{1,0:T(8,128)}, f32[8,2304]{1,0:T(8,128)S(1)}, u32[]{:S(2)}, u32[]{:S(2)}) collective-permute-start(f32[8,2304]{1,0:T(8,128)} %get-tuple-element.168), channel_id=1, source_target_pairs={{0,8},{8,0},{16,24},{24,16},{1,9},{9,1},{17,25},{25,17},{2,10},{10... | collective-permute-start | bytes 221192 | tf_op jit(solution)/shard_map/ppermute | solution.py:49
  236.8 9.2 %collective-permute-start.7 = (f32[8,2304]{1,0:T(8,128)}, f32[8,2304]{1,0:T(8,128)S(1)}, u32[]{:S(2)}, u32[]{:S(2)}) collective-permute-start(f32[8,2304]{1,0:T(8,128)} %get-tuple-element.168), channel_id=1, source_target_pairs={{0,16},{8,24},{16,0},{24,8},{1,17},{9,25},{17,1},{25,9},{2,18},{10... | collective-permute-start | bytes 221192 | tf_op jit(solution)/shard_map/ppermute | solution.py:49
  244.5 4.2 collective-permute-start.8
  245.6 25.2 %collective-permute-start.10 = (bf16[392,128]{1,0:T(8,128)(2,1)}, bf16[392,128]{1,0:T(8,128)(2,1)}, u32[]{:S(2)}, u32[]{:S(2)}) collective-permute-start(bf16[392,128]{1,0:T(8,128)(2,1)} %get-tuple-element.174), channel_id=1, source_target_pairs={{0,8},{8,0},{16,24},{24,16},{1,9},{9,1},{17,25},{25,17},{2,10},{10... | collective-permute-start | bytes 301064 | tf_op jit(solution)/shard_map/ppermute | solution.py:49
  246.0 24.7 %collective-permute-start.11 = (bf16[392,128]{1,0:T(8,128)(2,1)}, bf16[392,128]{1,0:T(8,128)(2,1)}, u32[]{:S(2)}, u32[]{:S(2)}) collective-permute-start(bf16[392,128]{1,0:T(8,128)(2,1)} %get-tuple-element.175), channel_id=1, source_target_pairs={{0,16},{8,24},{16,0},{24,8},{1,17},{9,25},{17,1},{25,9},{2,18},{10... | collective-permute-start | bytes 301064 | tf_op jit(solution)/shard_map/ppermute | solution.py:49
  248.7 22.0 %collective-permute-start.12 = (bf16[392,128]{1,0:T(8,128)(2,1)}, bf16[392,128]{1,0:T(8,128)(2,1)}, u32[]{:S(2)}, u32[]{:S(2)}) collective-permute-start(bf16[392,128]{1,0:T(8,128)(2,1)} %get-tuple-element.176), channel_id=1, source_target_pairs={{0,24},{8,16},{16,8},{24,0},{1,25},{9,17},{17,9},{25,1},{2,26},{10... | collective-permute-start | bytes 301064 | tf_op jit(solution)/shard_map/ppermute | solution.py:49
  249.7 21.1 %collective-permute-start.14 = (bf16[2,392,512]{2,1,0:T(8,128)(2,1)S(1)}, bf16[2,392,512]{2,1,0:T(8,128)(2,1)S(1)}, u32[]{:S(2)}, u32[]{:S(2)}) collective-permute-start(bf16[2,392,512]{2,1,0:T(8,128)(2,1)S(1)} %pad_maximum_fusion.6), channel_id=1, source_target_pairs={{0,8},{8,0},{16,24},{24,16},{1,9},{9,1},{17,25},{25,17},{2,10},{10... | collective-permute-start | bytes 2408456 | tf_op jit(solution)/shard_map/ppermute | solution.py:49
  262.9 18.1 %all-to-all-start.6 = ((bf16[32,8,640]{2,1,0:T(8,128)(2,1)}), bf16[32,8,640]{2,1,0:T(8,128)(2,1)S(1)}, u32[]{:S(2)}, u32[]{:S(2)}) async-start(bf16[32,8,640]{2,1,0:T(8,128)(2,1)} %broadcast_in_dim.135), calls=%async_computation.6 | async-start | bytes 655360 | tf_op jit(solution)/shard_map/all_to_all | solution.py:61
  294.1 10.3 %all-to-all-start.7 = ((bf16[32,8,256]{2,1,0:T(8,128)(2,1)}), bf16[32,8,256]{2,1,0:T(8,128)(2,1)S(1)}, u32[]{:S(2)}, u32[]{:S(2)}) async-start(bf16[32,8,256]{2,1,0:T(8,128)(2,1)} %get-tuple-element.190), calls=%async_computation.7 | async-start | bytes 262144 | tf_op jit(solution)/shard_map/all_to_all | solution.py:1153
  296.7 32.2 %collective-permute-start.19 = (bf16[392,512]{1,0:T(8,128)(2,1)}, bf16[392,512]{1,0:T(8,128)(2,1)S(1)}, u32[]{:S(2)}, u32[]{:S(2)}) collective-permute-start(bf16[392,512]{1,0:T(8,128)(2,1)} %get-tuple-element.193), channel_id=1, source_target_pairs={{0,8},{8,0},{16,24},{24,16},{1,9},{9,1},{17,25},{25,17},{2,10},{10... | collective-permute-start | bytes 1204232 | tf_op jit(solution)/shard_map/ppermute | solution.py:49
  296.9 32.0 %collective-permute-start.20 = (bf16[392,512]{1,0:T(8,128)(2,1)}, bf16[392,512]{1,0:T(8,128)(2,1)}, u32[]{:S(2)}, u32[]{:S(2)}) collective-permute-start(bf16[392,512]{1,0:T(8,128)(2,1)} %get-tuple-element.194), channel_id=1, source_target_pairs={{0,16},{8,24},{16,0},{24,8},{1,17},{9,25},{17,1},{25,9},{2,18},{10... | collective-permute-start | bytes 1204232 | tf_op jit(solution)/shard_map/ppermute | solution.py:49
  298.6 30.3 %collective-permute-start.21 = (bf16[392,512]{1,0:T(8,128)(2,1)}, bf16[392,512]{1,0:T(8,128)(2,1)}, u32[]{:S(2)}, u32[]{:S(2)}) collective-permute-start(bf16[392,512]{1,0:T(8,128)(2,1)} %get-tuple-element.195), channel_id=1, source_target_pairs={{0,24},{8,16},{16,8},{24,0},{1,25},{9,17},{17,9},{25,1},{2,26},{10... | collective-permute-start | bytes 1204232 | tf_op jit(solution)/shard_map/ppermute | solution.py:49
  316.2 12.5 %collective-permute-start.17 = (bf16[392,512]{1,0:T(8,128)(2,1)}, bf16[392,512]{1,0:T(8,128)(2,1)S(1)}, u32[]{:S(2)}, u32[]{:S(2)}) collective-permute-start(bf16[392,512]{1,0:T(8,128)(2,1)} %get-tuple-element.191.refs_4_), channel_id=1, source_target_pairs={{0,16},{8,24},{16,0},{24,8},{1,17},{9,25},{17,1},{25,9},{2,18},{10... | collective-permute-start | bytes 1204232 | tf_op jit(solution)/shard_map/ppermute | solution.py:49
  319.3 19.9 %all-to-all-start.8 = ((bf16[32,8,256]{2,1,0:T(8,128)(2,1)}), bf16[32,8,256]{2,1,0:T(8,128)(2,1)S(1)}, u32[]{:S(2)}, u32[]{:S(2)}) async-start(bf16[32,8,256]{2,1,0:T(8,128)(2,1)} %get-tuple-element.202), calls=%async_computation.8 | async-start | bytes 262144 | tf_op jit(solution)/shard_map/all_to_all | solution.py:1153
  328.8 4.8 collective-permute-start.18
  339.8 50.0 %all-to-all-start.9 = ((bf16[8,208,512]{2,1,0:T(8,128)(2,1)}), bf16[8,208,512]{2,1,0:T(8,128)(2,1)S(1)}, u32[]{:S(2)}, u32[]{:S(2)}) async-start(bf16[8,208,512]{2,1,0:T(8,128)(2,1)} %shard_map.459), calls=%async_computation.9 | async-start | bytes 3407872 | tf_op jit(solution)/shard_map/all_to_all | solution.py:1446
  348.3 11.6 %collective-permute-start.22 = (bf16[392,512]{1,0:T(8,128)(2,1)}, bf16[392,512]{1,0:T(8,128)(2,1)S(1)}, u32[]{:S(2)}, u32[]{:S(2)}) collective-permute-start(bf16[392,512]{1,0:T(8,128)(2,1)} %get-tuple-element.225.refs_0_.refs_8_), channel_id=1, source_target_pairs={{0,16},{8,24},{16,0},{24,8},{1,17},{9,25},{17,1},{25,9},{2,18},{10... | collective-permute-start | bytes 1204232 | tf_op jit(solution)/shard_map/ppermute | solution.py:49
  362.1 6.4 %collective-permute-start.23 = (bf16[2,392,512]{2,1,0:T(8,128)(2,1)}, bf16[2,392,512]{2,1,0:T(8,128)(2,1)}, u32[]{:S(2)}, u32[]{:S(2)}) collective-permute-start(bf16[2,392,512]{2,1,0:T(8,128)(2,1)} %pad_maximum_fusion.8), channel_id=1, source_target_pairs={{0,8},{8,0},{16,24},{24,16},{1,9},{9,1},{17,25},{25,17},{2,10},{10... | collective-permute-start | bytes 2408456 | tf_op jit(solution)/shard_map/ppermute | solution.py:49
  362.1 5.7 collective-permute-start.24
  365.2 3.3 collective-permute-start.25
  390.1 71.4 %all-to-all-start.10 = ((bf16[8,240,512]{2,1,0:T(8,128)(2,1)}), bf16[8,240,512]{2,1,0:T(8,128)(2,1)S(1)}, u32[]{:S(2)}, u32[]{:S(2)}) async-start(bf16[8,240,512]{2,1,0:T(8,128)(2,1)} %shard_map.463), calls=%async_computation.10 | async-start | bytes 3932160 | tf_op jit(solution)/shard_map/all_to_all | solution.py:1446
  402.5 5.1 collective-permute-start.26
  405.2 12.2 %collective-permute-start.27 = (bf16[8,96,192]{2,1,0:T(8,128)(2,1)}, bf16[8,96,192]{2,1,0:T(8,128)(2,1)S(1)}, u32[]{:S(2)}, u32[]{:S(2)}) collective-permute-start(bf16[8,96,192]{2,1,0:T(8,128)(2,1)} %get-tuple-element.214), channel_id=1, source_target_pairs={{0,16},{8,24},{16,0},{24,8},{1,17},{9,25},{17,1},{25,9},{2,18},{10... | collective-permute-start | bytes 884744 | tf_op jit(solution)/shard_map/ppermute | solution.py:49
  405.2 18.7 %collective-permute-start.28 = (bf16[8,96,192]{2,1,0:T(8,128)(2,1)}, bf16[8,96,192]{2,1,0:T(8,128)(2,1)S(1)}, u32[]{:S(2)}, u32[]{:S(2)}) collective-permute-start(bf16[8,96,192]{2,1,0:T(8,128)(2,1)} %get-tuple-element.215), channel_id=1, source_target_pairs={{0,24},{8,16},{16,8},{24,0},{1,25},{9,17},{17,9},{25,1},{2,26},{10... | collective-permute-start | bytes 884744 | tf_op jit(solution)/shard_map/ppermute | solution.py:49
  425.2 7.7 %collective-permute-start.29 = (bf16[125,192]{1,0:T(8,128)(2,1)S(1)}, bf16[125,192]{1,0:T(8,128)(2,1)S(1)}, u32[]{:S(2)}, u32[]{:S(2)}) collective-permute-start(bf16[125,192]{1,0:T(8,128)(2,1)S(1)} %get-tuple-element.455), channel_id=1, source_target_pairs={{0,1},{1,0},{2,3},{3,2},{4,5},{5,4},{6,7},{7,6},{8,9},{9,8},{10,11... | collective-permute-start | bytes 144008 | tf_op jit(solution)/shard_map/ppermute | solution.py:49
  427.0 9.2 %collective-permute-start.30 = (bf16[125,192]{1,0:T(8,128)(2,1)S(1)}, bf16[125,192]{1,0:T(8,128)(2,1)S(1)}, u32[]{:S(2)}, u32[]{:S(2)}) collective-permute-start(bf16[125,192]{1,0:T(8,128)(2,1)S(1)} %get-tuple-element.456), channel_id=1, source_target_pairs={{0,2},{1,3},{2,0},{3,1},{4,6},{5,7},{6,4},{7,5},{8,10},{9,11},{10,... | collective-permute-start | bytes 144008 | tf_op jit(solution)/shard_map/ppermute | solution.py:49
  428.5 9.0 %collective-permute-start.31 = (bf16[125,192]{1,0:T(8,128)(2,1)S(1)}, bf16[125,192]{1,0:T(8,128)(2,1)S(1)}, u32[]{:S(2)}, u32[]{:S(2)}) collective-permute-start(bf16[125,192]{1,0:T(8,128)(2,1)S(1)} %get-tuple-element.457), channel_id=1, source_target_pairs={{0,3},{1,2},{2,1},{3,0},{4,7},{5,6},{6,5},{7,4},{8,11},{9,10},{10,... | collective-permute-start | bytes 144008 | tf_op jit(solution)/shard_map/ppermute | solution.py:49
  428.8 20.1 %collective-permute-start.32 = (bf16[125,192]{1,0:T(8,128)(2,1)S(1)}, bf16[125,192]{1,0:T(8,128)(2,1)S(1)}, u32[]{:S(2)}, u32[]{:S(2)}) collective-permute-start(bf16[125,192]{1,0:T(8,128)(2,1)S(1)} %get-tuple-element.458), channel_id=1, source_target_pairs={{0,4},{1,5},{2,6},{3,7},{4,0},{5,1},{6,2},{7,3},{8,12},{9,13},{10,... | collective-permute-start | bytes 144008 | tf_op jit(solution)/shard_map/ppermute | solution.py:49
  431.4 20.0 %collective-permute-start.33 = (bf16[125,192]{1,0:T(8,128)(2,1)S(1)}, bf16[125,192]{1,0:T(8,128)(2,1)S(1)}, u32[]{:S(2)}, u32[]{:S(2)}) collective-permute-start(bf16[125,192]{1,0:T(8,128)(2,1)S(1)} %get-tuple-element.459), channel_id=1, source_target_pairs={{0,5},{1,4},{2,7},{3,6},{4,1},{5,0},{6,3},{7,2},{8,13},{9,12},{10,... | collective-permute-start | bytes 144008 | tf_op jit(solution)/shard_map/ppermute | solution.py:49
  432.9 18.6 %collective-permute-start.34 = (bf16[125,192]{1,0:T(8,128)(2,1)S(1)}, bf16[125,192]{1,0:T(8,128)(2,1)S(1)}, u32[]{:S(2)}, u32[]{:S(2)}) collective-permute-start(bf16[125,192]{1,0:T(8,128)(2,1)S(1)} %get-tuple-element.460), channel_id=1, source_target_pairs={{0,6},{1,7},{2,4},{3,5},{4,2},{5,3},{6,0},{7,1},{8,14},{9,15},{10,... | collective-permute-start | bytes 144008 | tf_op jit(solution)/shard_map/ppermute | solution.py:49
  436.2 15.4 %collective-permute-start.35 = (bf16[125,192]{1,0:T(8,128)(2,1)S(1)}, bf16[125,192]{1,0:T(8,128)(2,1)S(1)}, u32[]{:S(2)}, u32[]{:S(2)}) collective-permute-start(bf16[125,192]{1,0:T(8,128)(2,1)S(1)} %get-tuple-element.461), channel_id=1, source_target_pairs={{0,7},{1,6},{2,5},{3,4},{4,3},{5,2},{6,1},{7,0},{8,15},{9,14},{10,... | collective-permute-start | bytes 144008 | tf_op jit(solution)/shard_map/ppermute | solution.py:49
  452.5 8.1 %collective-permute-start.36 = (bf16[96,192]{1,0:T(8,128)(2,1)S(1)}, bf16[96,192]{1,0:T(8,128)(2,1)S(1)}, u32[]{:S(2)}, u32[]{:S(2)}) collective-permute-start(bf16[96,192]{1,0:T(8,128)(2,1)S(1)} %get-tuple-element.424), channel_id=1, source_target_pairs={{0,16},{8,24},{16,0},{24,8},{1,17},{9,25},{17,1},{25,9},{2,18},{10... | collective-permute-start | bytes 110600 | tf_op jit(solution)/shard_map/ppermute | solution.py:49
  460.6 11.7 %collective-permute-start.37 = (bf16[2,96,192]{2,1,0:T(8,128)(2,1)S(1)}, bf16[2,96,192]{2,1,0:T(8,128)(2,1)S(1)}, u32[]{:S(2)}, u32[]{:S(2)}) collective-permute-start(bf16[2,96,192]{2,1,0:T(8,128)(2,1)S(1)} %bitcast_dynamic-update-slice_fusion.6), channel_id=1, source_target_pairs={{0,8},{8,0},{16,24},{24,16},{1,9},{9,1},{17,25},{25,17},{2,10},{10... | collective-permute-start | bytes 221192 | tf_op jit(solution)/shard_map/ppermute | solution.py:49
  465.8 11.6 %all-to-all-start.11 = ((f32[32,8,128]{2,1,0:T(8,128)}), f32[32,8,128]{2,1,0:T(8,128)S(1)}, u32[]{:S(2)}, u32[]{:S(2)}) async-start(f32[32,8,128]{2,1,0:T(8,128)} %broadcast_in_dim.143), calls=%async_computation.11 | async-start | bytes 262144 | tf_op jit(solution)/shard_map/all_to_all | solution.py:61
  470.5 9.5 %collective-permute-start.38 = (bf16[256,512]{1,0:T(8,128)(2,1)S(1)}, bf16[256,512]{1,0:T(8,128)(2,1)S(1)}, u32[]{:S(2)}, u32[]{:S(2)}) collective-permute-start(bf16[256,512]{1,0:T(8,128)(2,1)S(1)} %get-tuple-element.462), channel_id=1, source_target_pairs={{0,16},{8,24},{16,0},{24,8},{1,17},{9,25},{17,1},{25,9},{2,18},{10... | collective-permute-start | bytes 786440 | tf_op jit(solution)/shard_map/ppermute | solution.py:49
  484.2 2.1 collective-permute-start.39
  518.8 32.2 %all-to-all-start.13 = ((bf16[8,144,512]{2,1,0:T(8,128)(2,1)}), bf16[8,144,512]{2,1,0:T(8,128)(2,1)S(1)}, u32[]{:S(2)}, u32[]{:S(2)}) async-start(bf16[8,144,512]{2,1,0:T(8,128)(2,1)} %pad_maximum_fusion.1), calls=%async_computation.13 | async-start | bytes 2359296 | tf_op jit(solution)/shard_map/all_to_all | solution.py:1741
  531.8 60.1 %copy-start.11 = (bf16[64,1728]{1,0:T(8,128)(2,1)}, bf16[64,1728]{1,0:T(8,128)(2,1)S(1)}, u32[]{:S(2)}) copy-start(bf16[64,1728]{1,0:T(8,128)(2,1)S(1)} %reshape.364) | copy-start | bytes 663556
  551.2 12.1 %collective-permute-start.41 = (bf16[8,64,512]{2,1,0:T(8,128)(2,1)S(1)}, bf16[8,64,512]{2,1,0:T(8,128)(2,1)S(1)}, u32[]{:S(2)}, u32[]{:S(2)}) collective-permute-start(bf16[8,64,512]{2,1,0:T(8,128)(2,1)S(1)} %get-tuple-element.453.own), channel_id=1, source_target_pairs={{0,16},{8,24},{16,0},{24,8},{1,17},{9,25},{17,1},{25,9},{2,18},{10... | collective-permute-start | bytes 1572872 | tf_op jit(solution)/shard_map/ppermute | solution.py:49
  558.7 6.6 %collective-permute-start.40 = (bf16[512,512]{1,0:T(8,128)(2,1)}, bf16[512,512]{1,0:T(8,128)(2,1)S(1)}, u32[]{:S(2)}, u32[]{:S(2)}) collective-permute-start(bf16[512,512]{1,0:T(8,128)(2,1)} %get-tuple-element.239.shaped), channel_id=1, source_target_pairs={{0,8},{8,0},{16,24},{24,16},{1,9},{9,1},{17,25},{25,17},{2,10},{10... | collective-permute-start | bytes 1572872 | tf_op jit(solution)/shard_map/ppermute | solution.py:49
  565.2 10.5 %collective-permute-start.42 = (bf16[2,8,64,512]{3,2,1,0:T(8,128)(2,1)S(1)}, bf16[2,8,64,512]{3,2,1,0:T(8,128)(2,1)}, u32[]{:S(2)}, u32[]{:S(2)}) collective-permute-start(bf16[2,8,64,512]{3,2,1,0:T(8,128)(2,1)S(1)} %pad_maximum_fusion.2), channel_id=1, source_target_pairs={{0,8},{8,0},{16,24},{24,16},{1,9},{9,1},{17,25},{25,17},{2,10},{10... | collective-permute-start | bytes 3145736 | tf_op jit(solution)/shard_map/ppermute | solution.py:49
  568.9 20.7 %all-to-all-start.14 = ((bf16[8,64,512]{2,1,0:T(8,128)(2,1)}), bf16[8,64,512]{2,1,0:T(8,128)(2,1)S(1)}, u32[]{:S(2)}, u32[]{:S(2)}) async-start(bf16[8,64,512]{2,1,0:T(8,128)(2,1)} %get-tuple-element.242), calls=%async_computation.14 | async-start | bytes 1048576 | tf_op jit(solution)/shard_map/all_to_all | solution.py:1775
  590.0 13.0 %collective-permute-start.43 = (bf16[8,64,512]{2,1,0:T(8,128)(2,1)S(1)}, bf16[8,64,512]{2,1,0:T(8,128)(2,1)S(1)}, u32[]{:S(2)}, u32[]{:S(2)}) collective-permute-start(bf16[8,64,512]{2,1,0:T(8,128)(2,1)S(1)} %get-tuple-element.451.own), channel_id=1, source_target_pairs={{0,16},{8,24},{16,0},{24,8},{1,17},{9,25},{17,1},{25,9},{2,18},{10... | collective-permute-start | bytes 1572872 | tf_op jit(solution)/shard_map/ppermute | solution.py:49
  603.0 3.4 collective-permute-start.44
  (80 other events, 734.1 us)
Sparse Core Ops, SparseCore 0:
  12.1 125.7 all-gather.2
  141.4 55.9 all-gather.4
